TPU v7x, 512 devices: a whole 4x4x16 slice. The times are simulated.
512 devices in a mesh: shot: 32 (over x, z_lo, core), rcv: 16 (over y, z_hi).
Axes of the slice: x: 4, y: 4, z: 16 (z_hi: 4, z_lo: 4; z = z_hi * 4 + z_lo), core: 2. Of those that a mesh axis runs over, the one named last changes fastest.
Arguments:
- field: bfloat16 [2, 16384, 16384], P(None, 'shot', 'rcv'), may hold values from -1.09375 to 1.09375
Outputs:
- multiples: bfloat16 [2, 16384, 16384], P(None, 'shot', 'rcv')
All inputs are finite; a program needn't handle non-finite values.
Results may differ from a plain program's by a relative error of at most 0.001.
Values may be sent and summed in bfloat16 or wider, within the bound.
No kernel may reach another device: no remote copies, remote signals or barrier semaphores. Data moves between devices by JAX's collectives and lax.ppermute only.
A program may use at most 64 MiB of HBM per device.

v0:
```python
import jax
import jax.numpy as jnp
from jax import lax
from jax.sharding import PartitionSpec as P

PANEL = 256
STEPS = 2


def spread(value, axis, root):
    mine = lax.axis_index(axis) == root
    return lax.psum(jnp.where(mine, value, jnp.zeros_like(value)), axis)


def complex_product(left, right):
    real_part = jnp.dot(left[0], right[0], preferred_element_type=jnp.float32) - jnp.dot(
        left[1], right[1], preferred_element_type=jnp.float32
    )
    imag_part = jnp.dot(left[0], right[1], preferred_element_type=jnp.float32) + jnp.dot(
        left[1], right[0], preferred_element_type=jnp.float32
    )
    return jnp.stack([real_part, imag_part])


def per_device(field):
    rows_dev = field.shape[1]
    cols_dev = field.shape[2]
    total = jnp.zeros((2, rows_dev, cols_dev), jnp.float32)
    for step in range(STEPS):
        start = step * PANEL
        col_owner = start // cols_dev
        col_offset = start % cols_dev
        row_owner = start // rows_dev
        row_offset = start % rows_dev
        left = spread(field[:, :, col_offset : col_offset + PANEL], "rcv", col_owner)
        right = spread(field[:, row_offset : row_offset + PANEL, :], "shot", row_owner)
        total = total + complex_product(left, right)
    return (-total).astype(jnp.bfloat16)


def solution(mesh):
    return jax.shard_map(
        per_device,
        mesh=mesh,
        in_specs=(P(None, "shot", "rcv"),),
        out_specs=P(None, "shot", "rcv"),
        check_vma=False,
    )
```

profile of v0, /device:TPU:1, one launch (start us, length us, event | category | flops | bytes accessed | tf_op | source)
XLA Modules:
  0.0 537.2 jit_solution(3893516162021503626)
XLA Ops:
  6.5 0.0 all-reduce.7.cloned.1.call-start
  6.5 2.4 slice_select_fusion.2
  8.9 0.0 all-reduce.7.cloned.1.call-update
  9.0 0.0 all-reduce.5.cloned.1.call-start
  9.0 0.0 copy-done
  9.0 1.5 slice_select_fusion
  10.5 0.0 all-reduce.5.cloned.1.call-update
  10.5 211.5 %all-reduce.7.cloned.1.call-done = (bf16[2,512,256]{2,1,0:T(8,128)(2,1)}, bf16[2,512,256]{2,1,0:T(8,128)(2,1)}) async-done(((bf16[2,512,256]{2,1,0:T(8,128)(2,1)}, bf16[2,512,256]{2,1,0:T(8,128)(2,1)}), (bf16[2,512,256]{2,1,0:T(8,128)(2,1)}, bf16[2,512,256]{2,1,0:T(8,128)(2,1)})) %all-reduce.7.cloned.1.call-update) | async-done | bytes 1048592 | tf_op jit(solution)/shard_map/psum | solution.py:12
  222.0 300.2 %all-reduce.5.cloned.1.call-done = (bf16[2,256,1024]{2,1,0:T(8,128)(2,1)}, bf16[2,256,1024]{2,1,0:T(8,128)(2,1)}) async-done(((bf16[2,256,1024]{2,1,0:T(8,128)(2,1)}, bf16[2,256,1024]{2,1,0:T(8,128)(2,1)}), (bf16[2,256,1024]{2,1,0:T(8,128)(2,1)}, bf16[2,256,1024]{2,1,0:T(8,128)(2,1)})) %all-reduce.5.cloned.1.call-update) | async-done | bytes 2097168 | tf_op jit(solution)/shard_map/psum | solution.py:12
  522.2 1.6 fusion.3
  523.9 0.0 copy-done.4
  523.9 0.0 copy-done.2
  523.9 0.0 copy-start.1
  523.9 0.0 copy-start.3
  523.9 0.4 fusion.2
  524.4 0.8 copy-done.1
  525.1 0.1 copy-done.3
  525.3 0.4 fusion.5
  525.7 0.4 fusion.4
  526.1 0.4 add_bitcast_fusion.1
  526.6 0.4 subtract_bitcast_fusion.1
  527.0 0.4 add_bitcast_fusion
  527.5 0.4 subtract_bitcast_fusion
  527.9 2.5 fusion.1
  (3 shorter events, 0.0 us)
Async XLA Ops:
  6.5 2.5 copy-start
  6.5 215.5 %all-reduce.7.cloned.1.call-start = ((), (), s32[]{:S(2)}) async-start(), calls=%async_computation.1 | async-start | bytes 2097152 | tf_op jit(solution)/shard_map/psum | solution.py:12
  9.0 513.3 %all-reduce.5.cloned.1.call-start = ((), (), s32[]{:S(2)}) async-start(), calls=%async_computation | async-start | bytes 4194304 | tf_op jit(solution)/shard_map/psum | solution.py:12
  222.0 301.9 %copy-start.4 = (bf16[2,512,256]{2,1,0:T(8,128)(2,1)S(1)}, bf16[2,512,256]{2,1,0:T(8,128)(2,1)}, u32[]{:S(2)}) copy-start(bf16[2,512,256]{2,1,0:T(8,128)(2,1)} %get-tuple-element.7) | copy-start | bytes 1572868
  522.2 1.7 copy-start.2
  523.9 1.2 copy-start.1
  523.9 1.3 copy-start.3
Sparse Core Ops, SparseCore 0:
  10.3 211.6 all-reduce.6
  225.2 296.9 all-reduce.4
where the time goes:
time: 537 us
  waiting for transfers between devices  512 us (95%)
  between operations  13.5 us (3%)
  other arithmetic  6.33 us (1%)
    psum x2, waiting for transfers between devices, spread(): return lax.psum(jnp.where(mine, value, jnp.zeros_like(value)), axis)  512 us
  transfers between devices with their start and end apart: 2, of which 2 were waited for; matrix products, arithmetic and copies ran while one was open for 0% of the time, Pallas kernels for 0%

commit v1 on v0

v1 whole, which is shorter than its diff:
```python
import jax
import jax.numpy as jnp
from jax import lax
from jax.sharding import PartitionSpec as P

WIDTH = 512
AXES = ("shot", "rcv")
NX, NL, NC, NY, NH = 4, 4, 2, 4, 4


def moves(rule):
    pairs = []
    for x in range(NX):
        for l in range(NL):
            for c in range(NC):
                for y in range(NY):
                    for h in range(NH):
                        to = rule(x, l, c, y, h)
                        if to is None:
                            continue
                        X, L, C, Y, H = to
                        src = ((x * NL + l) * NC + c) * NY * NH + y * NH + h
                        dst = (((X % NX) * NL + L) * NC + C) * NY * NH + (Y % NY) * NH + H % NH
                        pairs.append((src, dst))
    return pairs


def send(value, rule):
    return lax.ppermute(value, AXES, moves(rule))


def place(whole, piece, index):
    return lax.dynamic_update_slice_in_dim(whole, piece, index * piece.shape[1], 1)


def left_panel(field, x, l, c, y, h):
    mine = field[:, :, :WIDTH]
    rows = mine.shape[1]
    part = rows // NY
    got = [
        send(mine[:, part * d : part * (d + 1)], lambda x, l, c, y, h, d=d: (x, l, c, d, h) if y == 0 and h == 0 else None)
        for d in (1, 3, 2)
    ]
    quarter = jnp.where(y == 0, mine[:, :part], got[0] + got[1] + got[2])
    bit = part // NH
    got = [
        send(quarter[:, bit * d : bit * (d + 1)], lambda x, l, c, y, h, d=d: (x, l, c, y, d) if h == 0 else None)
        for d in (1, 3, 2)
    ]
    own = jnp.where(h == 0, quarter[:, :bit], got[0] + got[1] + got[2])
    gathered = place(quarter, own, h)
    for d in (1, 3, 2):
        came = send(own, lambda x, l, c, y, h, d=d: (x, l, c, y, h + d) if (h + d) % NH != 0 else None)
        gathered = place(gathered, came, (h - d) % NH)
    quarter = jnp.where(h == 0, quarter, gathered)
    panel = place(mine, quarter, y)
    for d in (1, 3, 2):
        came = send(quarter, lambda x, l, c, y, h, d=d: (x, l, c, y + d, h))
        panel = place(panel, came, (y - d) % NY)
    return panel


def right_panel(field, x, l, c, y, h):
    mine = field[:, :WIDTH, :]
    part = WIDTH // NX
    got = [
        send(mine[:, part * d : part * (d + 1)], lambda x, l, c, y, h, d=d: (d, l, c, y, h) if x == 0 and l == 0 and c == 0 else None)
        for d in (1, 3, 2)
    ]
    quarter = jnp.where(x == 0, mine[:, :part], got[0] + got[1] + got[2])
    came = send(quarter, lambda x, l, c, y, h: (x, 2, c, y, h) if l == 0 and c == 0 else None)
    quarter = jnp.where(l == 2, came, quarter)
    came = send(quarter, lambda x, l, c, y, h: (x, l + 1, c, y, h) if l % 2 == 0 and c == 0 else None)
    quarter = jnp.where(l % 2 == 1, came, quarter)
    panel = place(mine, quarter, x)
    for d in (1, 3, 2):
        came = send(quarter, lambda x, l, c, y, h, d=d: (x + d, l, c, y, h) if c == 0 else None)
        panel = place(panel, came, (x - d) % NX)
    came = send(panel, lambda x, l, c, y, h: (x, l, 1, y, h) if c == 0 else None)
    return jnp.where(c == 0, panel, came)


def per_device(field):
    s, r = lax.axis_index("shot"), lax.axis_index("rcv")
    place_of = (s // (NL * NC), s // NC % NL, s % NC, r // NH, r % NH)
    left = left_panel(field, *place_of)
    right = right_panel(field, *place_of)
    dot = lambda a, b: jnp.dot(a, b, preferred_element_type=jnp.float32)
    real = dot(left[0], right[0]) - dot(left[1], right[1])
    imag = dot(left[0], right[1]) + dot(left[1], right[0])
    return jnp.stack([-real, -imag]).astype(jnp.bfloat16)


def solution(mesh):
    return jax.shard_map(
        per_device,
        mesh=mesh,
        in_specs=(P(None, "shot", "rcv"),),
        out_specs=P(None, "shot", "rcv"),
        check_vma=False,
    )
```

time: 537 us -> 133 us (0.25)
  the two profiles are of different devices: /device:TPU:1 before, /device:TPU:98 now
where the time goes in v1:
time: 133 us; the launch traced here: 132 us
  starting transfers between devices  75.5 us (57%)
  waiting for transfers between devices  34.7 us (26%)
  local copies, waits for them, and re-layouts  9.72 us (7%)
  other arithmetic  8.76 us (7%)
  matrix products  2.88 us (2%)
    ppermute x21, starting transfers between devices, send(): return lax.ppermute(value, AXES, moves(rule))  75.5 us
    ppermute x21, waiting for transfers between devices, send(): return lax.ppermute(value, AXES, moves(rule))  34.7 us
    dynamic_update_slice x10, local copies, waits for them, and re-layouts, place(): lax.dynamic_update_slice_in_dim(whole, piece, index * piece.shape[1], 1)  5.24 us
    dot_general x4, matrix products, per_device(): dot = lambda a, b: jnp.dot(a, b, preferred_element_type=jnp.float32)  2.88 us
    dynamic_update_slice x2, other arithmetic, place(): lax.dynamic_update_slice_in_dim(whole, piece, index * piece.shape[1], 1)  2.86 us
  transfers between devices with their start and end apart: 21, of which 10 were waited for; matrix products, arithmetic and copies ran while one was open for 7% of the time, Pallas kernels for 0%

profile of v1, /device:TPU:98, one launch (start us, length us, event | category | flops | bytes accessed | tf_op | source)
XLA Modules:
  0.0 132.1 jit_solution(10582115738038897646)
XLA Ops:
  11.5 4.9 %collective-permute-start.1 = (bf16[2,128,512]{2,1,0:T(8,128)(2,1)}, bf16[2,128,512]{2,1,0:T(8,128)(2,1)S(1)}, u32[]{:S(2)}, u32[]{:S(2)}) collective-permute-start(bf16[2,128,512]{2,1,0:T(8,128)(2,1)} %get-tuple-element.9), channel_id=1, source_target_pairs={{0,12},{16,28},{32,44},{48,60},{64,76},{80,92},{96,108},{112,124},... | collective-permute-start | bytes 786440 | tf_op jit(solution)/shard_map/ppermute | solution.py:29
  16.5 2.0 %collective-permute-start.2 = (bf16[2,128,512]{2,1,0:T(8,128)(2,1)}, bf16[2,128,512]{2,1,0:T(8,128)(2,1)}, u32[]{:S(2)}, u32[]{:S(2)}) collective-permute-start(bf16[2,128,512]{2,1,0:T(8,128)(2,1)} %get-tuple-element.10), channel_id=1, source_target_pairs={{0,8},{16,24},{32,40},{48,56},{64,72},{80,88},{96,104},{112,120},{... | collective-permute-start | bytes 786440 | tf_op jit(solution)/shard_map/ppermute | solution.py:29
  18.5 2.0 %collective-permute-start = (bf16[2,128,512]{2,1,0:T(8,128)(2,1)}, bf16[2,128,512]{2,1,0:T(8,128)(2,1)}, u32[]{:S(2)}, u32[]{:S(2)}) collective-permute-start(bf16[2,128,512]{2,1,0:T(8,128)(2,1)} %get-tuple-element.11), channel_id=1, source_target_pairs={{0,4},{16,20},{32,36},{48,52},{64,68},{80,84},{96,100},{112,116},{... | collective-permute-start | bytes 786440 | tf_op jit(solution)/shard_map/ppermute | solution.py:29
  20.6 1.9 %collective-permute-done.1 = bf16[2,128,512]{2,1,0:T(8,128)(2,1)S(1)} collective-permute-done((bf16[2,128,512]{2,1,0:T(8,128)(2,1)}, bf16[2,128,512]{2,1,0:T(8,128)(2,1)S(1)}, u32[]{:S(2)}, u32[]{:S(2)}) %collective-permute-start.1) | collective-permute-done | bytes 262176 | tf_op jit(solution)/shard_map/ppermute | solution.py:29
  22.5 2.3 %collective-permute-done.2 = bf16[2,128,512]{2,1,0:T(8,128)(2,1)} collective-permute-done((bf16[2,128,512]{2,1,0:T(8,128)(2,1)}, bf16[2,128,512]{2,1,0:T(8,128)(2,1)}, u32[]{:S(2)}, u32[]{:S(2)}) %collective-permute-start.2) | collective-permute-done | bytes 262176 | tf_op jit(solution)/shard_map/ppermute | solution.py:29
  24.8 4.7 %collective-permute-done = bf16[2,128,512]{2,1,0:T(8,128)(2,1)} collective-permute-done((bf16[2,128,512]{2,1,0:T(8,128)(2,1)}, bf16[2,128,512]{2,1,0:T(8,128)(2,1)}, u32[]{:S(2)}, u32[]{:S(2)}) %collective-permute-start) | collective-permute-done | bytes 262176 | tf_op jit(solution)/shard_map/ppermute | solution.py:29
  30.6 7.3 %collective-permute-done.16 = bf16[2,128,1024]{2,1,0:T(8,128)(2,1)} collective-permute-done((bf16[2,128,1024]{2,1,0:T(8,128)(2,1)}, bf16[2,128,1024]{2,1,0:T(8,128)(2,1)}, u32[]{:S(2)}, u32[]{:S(2)}) %collective-permute-start.16) | collective-permute-done | bytes 524320 | tf_op jit(solution)/shard_map/ppermute | solution.py:29
  37.8 2.1 %constant_dynamic-update-slice_fusion.3 = (bf16[2,512,1024]{2,1,0:T(8,128)(2,1)S(1)}, bf16[2,128,1024]{2,1,0:T(8,128)(2,1)}) fusion(bf16[2,512,1024]{2,1,0:T(8,128)(2,1)S(1)} %copy.15, s32[]{:T(128)S(6)} %select_n.185, bf16[2,128,1024]{2,1,0:T(8,128)(2,1)} %collective-permute-done.16, bf16[2,128,1024]{2,1,0:T(8,128)(2,1)} %broadcast_select_fusion.1, pred[]{:T(512)S(6)} %eq.36), kind=kLoop, calls=%fused_computation.21 | loop fusion | flops 262144 | bytes 2097157 | tf_op jit(solution)/shard_map/dynamic_update_slice | solution.py:33
  39.9 9.0 %collective-permute-start.17 = (bf16[2,128,1024]{2,1,0:T(8,128)(2,1)}, bf16[2,128,1024]{2,1,0:T(8,128)(2,1)}, u32[]{:S(2)}, u32[]{:S(2)}) collective-permute-start(bf16[2,128,1024]{2,1,0:T(8,128)(2,1)} %get-tuple-element.8), channel_id=1, source_target_pairs={{0,128},{1,129},{2,130},{3,131},{4,132},{5,133},{6,134},{7,135},{8... | collective-permute-start | bytes 1572872 | tf_op jit(solution)/shard_map/ppermute | solution.py:29
  48.9 1.9 %collective-permute-start.18 = (bf16[2,128,1024]{2,1,0:T(8,128)(2,1)}, bf16[2,128,1024]{2,1,0:T(8,128)(2,1)}, u32[]{:S(2)}, u32[]{:S(2)}) collective-permute-start(bf16[2,128,1024]{2,1,0:T(8,128)(2,1)} %get-tuple-element.8), channel_id=1, source_target_pairs={{0,384},{1,385},{2,386},{3,387},{4,388},{5,389},{6,390},{7,391},{8... | collective-permute-start | bytes 1572872 | tf_op jit(solution)/shard_map/ppermute | solution.py:29
  50.8 3.4 %collective-permute-start.19 = (bf16[2,128,1024]{2,1,0:T(8,128)(2,1)}, bf16[2,128,1024]{2,1,0:T(8,128)(2,1)}, u32[]{:S(2)}, u32[]{:S(2)}) collective-permute-start(bf16[2,128,1024]{2,1,0:T(8,128)(2,1)} %get-tuple-element.8), channel_id=1, source_target_pairs={{0,256},{1,257},{2,258},{3,259},{4,260},{5,261},{6,262},{7,263},{8... | collective-permute-start | bytes 1572872 | tf_op jit(solution)/shard_map/ppermute | solution.py:29
  57.0 8.9 %collective-permute-done.18 = bf16[2,128,1024]{2,1,0:T(8,128)(2,1)} collective-permute-done((bf16[2,128,1024]{2,1,0:T(8,128)(2,1)}, bf16[2,128,1024]{2,1,0:T(8,128)(2,1)}, u32[]{:S(2)}, u32[]{:S(2)}) %collective-permute-start.18) | collective-permute-done | bytes 524320 | tf_op jit(solution)/shard_map/ppermute | solution.py:29
  68.1 2.6 %collective-permute-start.20 = (bf16[2,512,1024]{2,1,0:T(8,128)(2,1)S(1)}, bf16[2,512,1024]{2,1,0:T(8,128)(2,1)}, u32[]{:S(2)}, u32[]{:S(2)}) collective-permute-start(bf16[2,512,1024]{2,1,0:T(8,128)(2,1)S(1)} %constant_dynamic-update-slice_fusion), channel_id=1, source_target_pairs={{0,16},{1,17},{2,18},{3,19},{4,20},{5,21},{6,22},{7,23},{8,24},{9,... | collective-permute-start | bytes 6291464 | tf_op jit(solution)/shard_map/ppermute | solution.py:29
  71.4 10.7 %collective-permute-start.4 = (bf16[2,32,512]{2,1,0:T(8,128)(2,1)}, bf16[2,32,512]{2,1,0:T(8,128)(2,1)S(1)}, u32[]{:S(2)}, u32[]{:S(2)}) collective-permute-start(bf16[2,32,512]{2,1,0:T(8,128)(2,1)} %get-tuple-element.15), channel_id=1, source_target_pairs={{0,3},{4,7},{8,11},{12,15},{16,19},{20,23},{24,27},{28,31},{32,35}... | collective-permute-start | bytes 196616 | tf_op jit(solution)/shard_map/ppermute | solution.py:29
  82.1 3.7 %collective-permute-start.5 = (bf16[2,32,512]{2,1,0:T(8,128)(2,1)}, bf16[2,32,512]{2,1,0:T(8,128)(2,1)S(1)}, u32[]{:S(2)}, u32[]{:S(2)}) collective-permute-start(bf16[2,32,512]{2,1,0:T(8,128)(2,1)} %get-tuple-element.16), channel_id=1, source_target_pairs={{0,2},{4,6},{8,10},{12,14},{16,18},{20,22},{24,26},{28,30},{32,34}... | collective-permute-start | bytes 196616 | tf_op jit(solution)/shard_map/ppermute | solution.py:29
  85.8 1.9 %collective-permute-start.3 = (bf16[2,32,512]{2,1,0:T(8,128)(2,1)}, bf16[2,32,512]{2,1,0:T(8,128)(2,1)}, u32[]{:S(2)}, u32[]{:S(2)}) collective-permute-start(bf16[2,32,512]{2,1,0:T(8,128)(2,1)} %get-tuple-element.17), channel_id=1, source_target_pairs={{0,1},{4,5},{8,9},{12,13},{16,17},{20,21},{24,25},{28,29},{32,33},... | collective-permute-start | bytes 196616 | tf_op jit(solution)/shard_map/ppermute | solution.py:29
  88.0 1.9 %collective-permute-done.3 = bf16[2,32,512]{2,1,0:T(8,128)(2,1)} collective-permute-done((bf16[2,32,512]{2,1,0:T(8,128)(2,1)}, bf16[2,32,512]{2,1,0:T(8,128)(2,1)}, u32[]{:S(2)}, u32[]{:S(2)}) %collective-permute-start.3) | collective-permute-done | bytes 65568 | tf_op jit(solution)/shard_map/ppermute | solution.py:29
  90.8 11.0 %collective-permute-start.8 = (bf16[2,32,512]{2,1,0:T(8,128)(2,1)S(1)}, bf16[2,32,512]{2,1,0:T(8,128)(2,1)S(1)}, u32[]{:S(2)}, u32[]{:S(2)}) collective-permute-start(bf16[2,32,512]{2,1,0:T(8,128)(2,1)S(1)} %slice_select_fusion), channel_id=1, source_target_pairs={{0,2},{1,3},{3,1},{4,6},{5,7},{7,5},{8,10},{9,11},{11,9},{12,14},{... | collective-permute-start | bytes 196616 | tf_op jit(solution)/shard_map/ppermute | solution.py:29
  101.7 4.6 %collective-permute-start.7 = (bf16[2,32,512]{2,1,0:T(8,128)(2,1)S(1)}, bf16[2,32,512]{2,1,0:T(8,128)(2,1)S(1)}, u32[]{:S(2)}, u32[]{:S(2)}) collective-permute-start(bf16[2,32,512]{2,1,0:T(8,128)(2,1)S(1)} %slice_select_fusion), channel_id=1, source_target_pairs={{0,3},{2,1},{3,2},{4,7},{6,5},{7,6},{8,11},{10,9},{11,10},{12,15},... | collective-permute-start | bytes 196616 | tf_op jit(solution)/shard_map/ppermute | solution.py:29
  107.6 1.9 %collective-permute-done.6 = bf16[2,32,512]{2,1,0:T(8,128)(2,1)S(1)} collective-permute-done((bf16[2,32,512]{2,1,0:T(8,128)(2,1)S(1)}, bf16[2,32,512]{2,1,0:T(8,128)(2,1)S(1)}, u32[]{:S(2)}, u32[]{:S(2)}) %collective-permute-start.6) | collective-permute-done | bytes 65568 | tf_op jit(solution)/shard_map/ppermute | solution.py:29
  110.3 3.5 %collective-permute-start.9 = (bf16[2,128,512]{2,1,0:T(8,128)(2,1)}, bf16[2,128,512]{2,1,0:T(8,128)(2,1)}, u32[]{:S(2)}, u32[]{:S(2)}) collective-permute-start(bf16[2,128,512]{2,1,0:T(8,128)(2,1)} %get-tuple-element.6), channel_id=1, source_target_pairs={{0,4},{1,5},{2,6},{3,7},{4,8},{5,9},{6,10},{7,11},{8,12},{9,13},{1... | collective-permute-start | bytes 786440 | tf_op jit(solution)/shard_map/ppermute | solution.py:29
  113.8 3.6 %collective-permute-start.10 = (bf16[2,128,512]{2,1,0:T(8,128)(2,1)}, bf16[2,128,512]{2,1,0:T(8,128)(2,1)}, u32[]{:S(2)}, u32[]{:S(2)}) collective-permute-start(bf16[2,128,512]{2,1,0:T(8,128)(2,1)} %get-tuple-element.6), channel_id=1, source_target_pairs={{0,12},{1,13},{2,14},{3,15},{4,0},{5,1},{6,2},{7,3},{8,4},{9,5},{1... | collective-permute-start | bytes 786440 | tf_op jit(solution)/shard_map/ppermute | solution.py:29
  117.4 3.9 %collective-permute-start.11 = (bf16[2,128,512]{2,1,0:T(8,128)(2,1)}, bf16[2,128,512]{2,1,0:T(8,128)(2,1)S(1)}, u32[]{:S(2)}, u32[]{:S(2)}) collective-permute-start(bf16[2,128,512]{2,1,0:T(8,128)(2,1)} %get-tuple-element.6), channel_id=1, source_target_pairs={{0,8},{1,9},{2,10},{3,11},{4,12},{5,13},{6,14},{7,15},{8,0},{9,1},... | collective-permute-start | bytes 786440 | tf_op jit(solution)/shard_map/ppermute | solution.py:29
  123.4 4.0 %collective-permute-done.11 = bf16[2,128,512]{2,1,0:T(8,128)(2,1)S(1)} collective-permute-done((bf16[2,128,512]{2,1,0:T(8,128)(2,1)}, bf16[2,128,512]{2,1,0:T(8,128)(2,1)S(1)}, u32[]{:S(2)}, u32[]{:S(2)}) %collective-permute-start.11) | collective-permute-done | bytes 262176 | tf_op jit(solution)/shard_map/ppermute | solution.py:29
  (48 shorter events, 28.1 us)
Async XLA Ops:
  2.8 3.6 %collective-permute-start.13 = (bf16[2,128,1024]{2,1,0:T(8,128)(2,1)}, bf16[2,128,1024]{2,1,0:T(8,128)(2,1)S(1)}, u32[]{:S(2)}, u32[]{:S(2)}) collective-permute-start(bf16[2,128,1024]{2,1,0:T(8,128)(2,1)} %get-tuple-element.12), channel_id=1, source_target_pairs={{0,384},{1,385},{2,386},{3,387},{4,388},{5,389},{6,390},{7,391},{8... | collective-permute-start | bytes 1572872 | tf_op jit(solution)/shard_map/ppermute | solution.py:29
  3.5 3.0 %collective-permute-start.12 = (bf16[2,128,1024]{2,1,0:T(8,128)(2,1)}, bf16[2,128,1024]{2,1,0:T(8,128)(2,1)}, u32[]{:S(2)}, u32[]{:S(2)}) collective-permute-start(bf16[2,128,1024]{2,1,0:T(8,128)(2,1)} %get-tuple-element.13), channel_id=1, source_target_pairs={{0,128},{1,129},{2,130},{3,131},{4,132},{5,133},{6,134},{7,135},{8... | collective-permute-start | bytes 1572872 | tf_op jit(solution)/shard_map/ppermute | solution.py:29
  5.0 1.5 %collective-permute-start.14 = (bf16[2,128,1024]{2,1,0:T(8,128)(2,1)S(1)}, bf16[2,128,1024]{2,1,0:T(8,128)(2,1)}, u32[]{:S(2)}, u32[]{:S(2)}) collective-permute-start(bf16[2,128,1024]{2,1,0:T(8,128)(2,1)S(1)} %get-tuple-element.14), channel_id=1, source_target_pairs={{0,256},{1,257},{2,258},{3,259},{4,260},{5,261},{6,262},{7,263},{8... | collective-permute-start | bytes 1572872 | tf_op jit(solution)/shard_map/ppermute | solution.py:29
  7.7 0.7 collective-permute-start.15
  9.3 28.5 %collective-permute-start.16 = (bf16[2,128,1024]{2,1,0:T(8,128)(2,1)}, bf16[2,128,1024]{2,1,0:T(8,128)(2,1)}, u32[]{:S(2)}, u32[]{:S(2)}) collective-permute-start(bf16[2,128,1024]{2,1,0:T(8,128)(2,1)} %broadcast_select_fusion.1), channel_id=1, source_target_pairs={{0,32},{1,33},{2,34},{3,35},{4,36},{5,37},{6,38},{7,39},{8,40},{9,... | collective-permute-start | bytes 1572872 | tf_op jit(solution)/shard_map/ppermute | solution.py:29
  11.5 10.9 %collective-permute-start.1 = (bf16[2,128,512]{2,1,0:T(8,128)(2,1)}, bf16[2,128,512]{2,1,0:T(8,128)(2,1)S(1)}, u32[]{:S(2)}, u32[]{:S(2)}) collective-permute-start(bf16[2,128,512]{2,1,0:T(8,128)(2,1)} %get-tuple-element.9), channel_id=1, source_target_pairs={{0,12},{16,28},{32,44},{48,60},{64,76},{80,92},{96,108},{112,124},... | collective-permute-start | bytes 786440 | tf_op jit(solution)/shard_map/ppermute | solution.py:29
  16.5 8.3 %collective-permute-start.2 = (bf16[2,128,512]{2,1,0:T(8,128)(2,1)}, bf16[2,128,512]{2,1,0:T(8,128)(2,1)}, u32[]{:S(2)}, u32[]{:S(2)}) collective-permute-start(bf16[2,128,512]{2,1,0:T(8,128)(2,1)} %get-tuple-element.10), channel_id=1, source_target_pairs={{0,8},{16,24},{32,40},{48,56},{64,72},{80,88},{96,104},{112,120},{... | collective-permute-start | bytes 786440 | tf_op jit(solution)/shard_map/ppermute | solution.py:29
  18.5 10.9 %collective-permute-start = (bf16[2,128,512]{2,1,0:T(8,128)(2,1)}, bf16[2,128,512]{2,1,0:T(8,128)(2,1)}, u32[]{:S(2)}, u32[]{:S(2)}) collective-permute-start(bf16[2,128,512]{2,1,0:T(8,128)(2,1)} %get-tuple-element.11), channel_id=1, source_target_pairs={{0,4},{16,20},{32,36},{48,52},{64,68},{80,84},{96,100},{112,116},{... | collective-permute-start | bytes 786440 | tf_op jit(solution)/shard_map/ppermute | solution.py:29
  22.5 2.3 %copy-start = (bf16[2,128,512]{2,1,0:T(8,128)(2,1)}, bf16[2,128,512]{2,1,0:T(8,128)(2,1)S(1)}, u32[]{:S(2)}) copy-start(bf16[2,128,512]{2,1,0:T(8,128)(2,1)S(1)} %collective-permute-done.1) | copy-start | bytes 786436
  39.9 16.0 %collective-permute-start.17 = (bf16[2,128,1024]{2,1,0:T(8,128)(2,1)}, bf16[2,128,1024]{2,1,0:T(8,128)(2,1)}, u32[]{:S(2)}, u32[]{:S(2)}) collective-permute-start(bf16[2,128,1024]{2,1,0:T(8,128)(2,1)} %get-tuple-element.8), channel_id=1, source_target_pairs={{0,128},{1,129},{2,130},{3,131},{4,132},{5,133},{6,134},{7,135},{8... | collective-permute-start | bytes 1572872 | tf_op jit(solution)/shard_map/ppermute | solution.py:29
  48.9 17.0 %collective-permute-start.18 = (bf16[2,128,1024]{2,1,0:T(8,128)(2,1)}, bf16[2,128,1024]{2,1,0:T(8,128)(2,1)}, u32[]{:S(2)}, u32[]{:S(2)}) collective-permute-start(bf16[2,128,1024]{2,1,0:T(8,128)(2,1)} %get-tuple-element.8), channel_id=1, source_target_pairs={{0,384},{1,385},{2,386},{3,387},{4,388},{5,389},{6,390},{7,391},{8... | collective-permute-start | bytes 1572872 | tf_op jit(solution)/shard_map/ppermute | solution.py:29
  50.8 16.2 %collective-permute-start.19 = (bf16[2,128,1024]{2,1,0:T(8,128)(2,1)}, bf16[2,128,1024]{2,1,0:T(8,128)(2,1)}, u32[]{:S(2)}, u32[]{:S(2)}) collective-permute-start(bf16[2,128,1024]{2,1,0:T(8,128)(2,1)} %get-tuple-element.8), channel_id=1, source_target_pairs={{0,256},{1,257},{2,258},{3,259},{4,260},{5,261},{6,262},{7,263},{8... | collective-permute-start | bytes 1572872 | tf_op jit(solution)/shard_map/ppermute | solution.py:29
  68.1 59.3 %collective-permute-start.20 = (bf16[2,512,1024]{2,1,0:T(8,128)(2,1)S(1)}, bf16[2,512,1024]{2,1,0:T(8,128)(2,1)}, u32[]{:S(2)}, u32[]{:S(2)}) collective-permute-start(bf16[2,512,1024]{2,1,0:T(8,128)(2,1)S(1)} %constant_dynamic-update-slice_fusion), channel_id=1, source_target_pairs={{0,16},{1,17},{2,18},{3,19},{4,20},{5,21},{6,22},{7,23},{8,24},{9,... | collective-permute-start | bytes 6291464 | tf_op jit(solution)/shard_map/ppermute | solution.py:29
  71.4 16.3 %collective-permute-start.4 = (bf16[2,32,512]{2,1,0:T(8,128)(2,1)}, bf16[2,32,512]{2,1,0:T(8,128)(2,1)S(1)}, u32[]{:S(2)}, u32[]{:S(2)}) collective-permute-start(bf16[2,32,512]{2,1,0:T(8,128)(2,1)} %get-tuple-element.15), channel_id=1, source_target_pairs={{0,3},{4,7},{8,11},{12,15},{16,19},{20,23},{24,27},{28,31},{32,35}... | collective-permute-start | bytes 196616 | tf_op jit(solution)/shard_map/ppermute | solution.py:29
  82.1 5.9 %collective-permute-start.5 = (bf16[2,32,512]{2,1,0:T(8,128)(2,1)}, bf16[2,32,512]{2,1,0:T(8,128)(2,1)S(1)}, u32[]{:S(2)}, u32[]{:S(2)}) collective-permute-start(bf16[2,32,512]{2,1,0:T(8,128)(2,1)} %get-tuple-element.16), channel_id=1, source_target_pairs={{0,2},{4,6},{8,10},{12,14},{16,18},{20,22},{24,26},{28,30},{32,34}... | collective-permute-start | bytes 196616 | tf_op jit(solution)/shard_map/ppermute | solution.py:29
  85.8 4.1 %collective-permute-start.3 = (bf16[2,32,512]{2,1,0:T(8,128)(2,1)}, bf16[2,32,512]{2,1,0:T(8,128)(2,1)}, u32[]{:S(2)}, u32[]{:S(2)}) collective-permute-start(bf16[2,32,512]{2,1,0:T(8,128)(2,1)} %get-tuple-element.17), channel_id=1, source_target_pairs={{0,1},{4,5},{8,9},{12,13},{16,17},{20,21},{24,25},{28,29},{32,33},... | collective-permute-start | bytes 196616 | tf_op jit(solution)/shard_map/ppermute | solution.py:29
  90.8 18.8 %collective-permute-start.8 = (bf16[2,32,512]{2,1,0:T(8,128)(2,1)S(1)}, bf16[2,32,512]{2,1,0:T(8,128)(2,1)S(1)}, u32[]{:S(2)}, u32[]{:S(2)}) collective-permute-start(bf16[2,32,512]{2,1,0:T(8,128)(2,1)S(1)} %slice_select_fusion), channel_id=1, source_target_pairs={{0,2},{1,3},{3,1},{4,6},{5,7},{7,5},{8,10},{9,11},{11,9},{12,14},{... | collective-permute-start | bytes 196616 | tf_op jit(solution)/shard_map/ppermute | solution.py:29
  101.7 7.8 %collective-permute-start.7 = (bf16[2,32,512]{2,1,0:T(8,128)(2,1)S(1)}, bf16[2,32,512]{2,1,0:T(8,128)(2,1)S(1)}, u32[]{:S(2)}, u32[]{:S(2)}) collective-permute-start(bf16[2,32,512]{2,1,0:T(8,128)(2,1)S(1)} %slice_select_fusion), channel_id=1, source_target_pairs={{0,3},{2,1},{3,2},{4,7},{6,5},{7,6},{8,11},{10,9},{11,10},{12,15},... | collective-permute-start | bytes 196616 | tf_op jit(solution)/shard_map/ppermute | solution.py:29
  106.3 3.2 %collective-permute-start.6 = (bf16[2,32,512]{2,1,0:T(8,128)(2,1)S(1)}, bf16[2,32,512]{2,1,0:T(8,128)(2,1)S(1)}, u32[]{:S(2)}, u32[]{:S(2)}) collective-permute-start(bf16[2,32,512]{2,1,0:T(8,128)(2,1)S(1)} %slice_select_fusion), channel_id=1, source_target_pairs={{0,1},{1,2},{2,3},{4,5},{5,6},{6,7},{8,9},{9,10},{10,11},{12,13},{... | collective-permute-start | bytes 196616 | tf_op jit(solution)/shard_map/ppermute | solution.py:29
  110.3 11.0 %collective-permute-start.9 = (bf16[2,128,512]{2,1,0:T(8,128)(2,1)}, bf16[2,128,512]{2,1,0:T(8,128)(2,1)}, u32[]{:S(2)}, u32[]{:S(2)}) collective-permute-start(bf16[2,128,512]{2,1,0:T(8,128)(2,1)} %get-tuple-element.6), channel_id=1, source_target_pairs={{0,4},{1,5},{2,6},{3,7},{4,8},{5,9},{6,10},{7,11},{8,12},{9,13},{1... | collective-permute-start | bytes 786440 | tf_op jit(solution)/shard_map/ppermute | solution.py:29
  113.8 8.6 %collective-permute-start.10 = (bf16[2,128,512]{2,1,0:T(8,128)(2,1)}, bf16[2,128,512]{2,1,0:T(8,128)(2,1)}, u32[]{:S(2)}, u32[]{:S(2)}) collective-permute-start(bf16[2,128,512]{2,1,0:T(8,128)(2,1)} %get-tuple-element.6), channel_id=1, source_target_pairs={{0,12},{1,13},{2,14},{3,15},{4,0},{5,1},{6,2},{7,3},{8,4},{9,5},{1... | collective-permute-start | bytes 786440 | tf_op jit(solution)/shard_map/ppermute | solution.py:29
  117.4 10.0 %collective-permute-start.11 = (bf16[2,128,512]{2,1,0:T(8,128)(2,1)}, bf16[2,128,512]{2,1,0:T(8,128)(2,1)S(1)}, u32[]{:S(2)}, u32[]{:S(2)}) collective-permute-start(bf16[2,128,512]{2,1,0:T(8,128)(2,1)} %get-tuple-element.6), channel_id=1, source_target_pairs={{0,8},{1,9},{2,10},{3,11},{4,12},{5,13},{6,14},{7,15},{8,0},{9,1},... | collective-permute-start | bytes 786440 | tf_op jit(solution)/shard_map/ppermute | solution.py:29

commit v2 on v1

v2 whole, which is shorter than its diff:
```python
import jax
import jax.numpy as jnp
from jax import lax
from jax.sharding import PartitionSpec as P

WIDTH = 512
AXES = ("shot", "rcv")
NX, NL, NC, NY, NH = 4, 4, 2, 4, 4
HOPS = (2, 1, 3)


def moves(rule):
    pairs = []
    for x in range(NX):
        for l in range(NL):
            for c in range(NC):
                for y in range(NY):
                    for h in range(NH):
                        to = rule(x, l, c, y, h)
                        if to is None:
                            continue
                        X, L, C, Y, H = to
                        src = ((x * NL + l) * NC + c) * NY * NH + y * NH + h
                        dst = (((X % NX) * NL + L) * NC + C) * NY * NH + (Y % NY) * NH + H % NH
                        pairs.append((src, dst))
    return pairs


def send(value, rule):
    return lax.ppermute(value, AXES, moves(rule))


def place(whole, piece, index):
    return lax.dynamic_update_slice_in_dim(whole, piece, index * piece.shape[1], 1)


def after(value, *others):
    return lax.optimization_barrier((value, *others))[0]


def per_device(field):
    s, r = lax.axis_index("shot"), lax.axis_index("rcv")
    x, l, c, y, h = s // (NL * NC), s // NC % NL, s % NC, r // NH, r % NH

    lmine = field[:, :, :WIDTH]
    rmine = field[:, :WIDTH]
    half = rmine.shape[2] // NC
    lpart = lmine.shape[1] // NY
    rpart = WIDTH // NX

    rhalf1 = send(rmine[:, :, half:], lambda x, l, c, y, h: (x, l, 1, y, h) if x == 0 and l == 0 and c == 0 else None)

    lgot = {
        d: send(lmine[:, lpart * d : lpart * (d + 1)], lambda x, l, c, y, h, d=d: (x, l, c, d, h) if y == 0 and h == 0 else None)
        for d in HOPS
    }
    rhalf = jnp.where(c == 0, rmine[:, :, :half], rhalf1)
    rgot = {
        d: send(rhalf[:, rpart * d : rpart * (d + 1)], lambda x, l, c, y, h, d=d: (d, l, c, y, h) if x == 0 and l == 0 else None)
        for d in HOPS
    }
    lq = jnp.where(y == 0, lmine[:, :lpart], lgot[1] + lgot[2] + lgot[3])

    bit = lpart // 8
    a, b, e = slice(0, 3 * bit), slice(3 * bit, 5 * bit), slice(5 * bit, 8 * bit)
    z1 = {
        d: send(lq[:, w], lambda x, l, c, y, h, d=d: (x, l, c, y, d) if h == 0 else None)
        for d, w in ((1, a), (3, e), (2, b))
    }
    rq = jnp.where(x == 0, rhalf[:, :rpart], rgot[1] + rgot[2] + rgot[3])
    rq = after(rq, lq)
    came = send(rq, lambda x, l, c, y, h: (x, 2, c, y, h) if l == 0 else None)

    wide = jnp.concatenate([z1[2], jnp.zeros_like(z1[2][:, : 3 * bit - 2 * bit])], 1)
    up = jnp.where(h == 0, lq[:, e], jnp.where(h == 1, z1[1], wide))
    down = jnp.where(h == 0, lq[:, a], jnp.where(h == 3, z1[3], wide))
    gup = send(up, lambda x, l, c, y, h: (x, l, c, y, h + 1) if h < 3 else None)
    gdown = send(down, lambda x, l, c, y, h: (x, l, c, y, h - 1) if h != 1 else None)
    rq = jnp.where(l == 2, came, rq)
    rq = after(rq, up, down)
    came = send(rq, lambda x, l, c, y, h: (x, l + 1, c, y, h) if l % 2 == 0 else None)
    rq = jnp.where(l % 2 == 1, came, rq)

    right = jnp.zeros((2, WIDTH, half), jnp.bfloat16)
    right = place(right, rq, x)
    for d in HOPS:
        came = send(rq, lambda x, l, c, y, h, d=d: (x + d, l, c, y, h))
        right = place(right, came, (x - d) % NX)
    other = send(right, lambda x, l, c, y, h: (x, l, 1 - c, y, h))

    pa = jnp.where(h == 1, z1[1], jnp.where(h == 2, gup, gdown))
    pb = jnp.where(h == 2, z1[2], jnp.where(h == 1, gdown, gup)[:, : 2 * bit])
    pe = jnp.where(h == 3, z1[3], jnp.where(h == 1, gup, gdown))
    lq = jnp.where(h == 0, lq, jnp.concatenate([pa, pb, pe], 1))
    left = jnp.zeros_like(lmine)
    left = place(left, lq, y)
    for d in HOPS:
        came = send(lq, lambda x, l, c, y, h, d=d: (x, l, c, y + d, h))
        left = place(left, came, (y - d) % NY)

    right = jnp.where(c == 0, jnp.concatenate([right, other], 2), jnp.concatenate([other, right], 2))
    dot = lambda a, b: jnp.dot(a, b, preferred_element_type=jnp.float32)
    real = dot(left[0], right[0]) - dot(left[1], right[1])
    imag = dot(left[0], right[1]) + dot(left[1], right[0])
    return jnp.stack([-real, -imag]).astype(jnp.bfloat16)


def solution(mesh):
    return jax.shard_map(
        per_device,
        mesh=mesh,
        in_specs=(P(None, "shot", "rcv"),),
        out_specs=P(None, "shot", "rcv"),
        check_vma=False,
    )
```

time: 133 us -> 97.6 us (0.73)
  the two profiles are of different devices: /device:TPU:98 before, /device:TPU:1 now
where the time goes in v2:
time: 97.6 us; the launch traced here: 96.2 us
  starting transfers between devices  67.2 us (69%)
  waiting for transfers between devices  15.4 us (16%)
  local copies, waits for them, and re-layouts  5.57 us (6%)
  other arithmetic  4.35 us (4%)
  matrix products  2.98 us (3%)
    ppermute x21, starting transfers between devices, send(): return lax.ppermute(value, AXES, moves(rule))  67.2 us
    ppermute x21, waiting for transfers between devices, send(): return lax.ppermute(value, AXES, moves(rule))  15.4 us
    dot_general x4, matrix products, per_device(): dot = lambda a, b: jnp.dot(a, b, preferred_element_type=jnp.float32)  2.98 us
    slice x1, local copies, waits for them, and re-layouts, per_device(): rmine[:, :, half:]  2.41 us
    dynamic_update_slice x6, local copies, waits for them, and re-layouts, place(): lax.dynamic_update_slice_in_dim(whole, piece, index * piece.shape[1], 1)  2.03 us
  transfers between devices with their start and end apart: 21, of which 6 were waited for; matrix products, arithmetic and copies ran while one was open for 6% of the time, Pallas kernels for 0%

profile of v2, /device:TPU:1, one launch (start us, length us, event | category | flops | bytes accessed | tf_op | source)
XLA Modules:
  0.0 96.2 jit_solution(16270355855121713282)
XLA Ops:
  0.0 2.4 %slice.75 = bf16[2,512,512]{2,1,0:T(8,128)(2,1)} slice(bf16[2,512,1024]{2,1,0:T(8,128)(2,1)} %param.1), slice={[0:2], [0:512], [512:1024]} | slice | bytes 2097152 | tf_op jit(solution)/shard_map/slice | solution.py:51
  4.6 5.7 %collective-permute-start.1 = (bf16[2,128,512]{2,1,0:T(8,128)(2,1)}, bf16[2,128,512]{2,1,0:T(8,128)(2,1)S(1)}, u32[]{:S(2)}, u32[]{:S(2)}) collective-permute-start(bf16[2,128,512]{2,1,0:T(8,128)(2,1)} %get-tuple-element.13), channel_id=1, source_target_pairs={{0,8},{16,24},{32,40},{48,56},{64,72},{80,88},{96,104},{112,120},{... | collective-permute-start | bytes 786440 | tf_op jit(solution)/shard_map/ppermute | solution.py:30
  10.3 2.0 %collective-permute-start.2 = (bf16[2,128,512]{2,1,0:T(8,128)(2,1)}, bf16[2,128,512]{2,1,0:T(8,128)(2,1)}, u32[]{:S(2)}, u32[]{:S(2)}) collective-permute-start(bf16[2,128,512]{2,1,0:T(8,128)(2,1)} %get-tuple-element.14), channel_id=1, source_target_pairs={{0,12},{16,28},{32,44},{48,60},{64,76},{80,92},{96,108},{112,124},... | collective-permute-start | bytes 786440 | tf_op jit(solution)/shard_map/ppermute | solution.py:30
  12.3 2.0 %collective-permute-start = (bf16[2,128,512]{2,1,0:T(8,128)(2,1)}, bf16[2,128,512]{2,1,0:T(8,128)(2,1)}, u32[]{:S(2)}, u32[]{:S(2)}) collective-permute-start(bf16[2,128,512]{2,1,0:T(8,128)(2,1)} %get-tuple-element.15), channel_id=1, source_target_pairs={{0,4},{16,20},{32,36},{48,52},{64,68},{80,84},{96,100},{112,116},{... | collective-permute-start | bytes 786440 | tf_op jit(solution)/shard_map/ppermute | solution.py:30
  14.5 4.1 %collective-permute-start.13 = (bf16[2,128,512]{2,1,0:T(8,128)(2,1)S(1)}, bf16[2,128,512]{2,1,0:T(8,128)(2,1)S(1)}, u32[]{:S(2)}, u32[]{:S(2)}) collective-permute-start(bf16[2,128,512]{2,1,0:T(8,128)(2,1)S(1)} %get-tuple-element.16), channel_id=1, source_target_pairs={{0,256},{1,257},{2,258},{3,259},{4,260},{5,261},{6,262},{7,263},{8... | collective-permute-start | bytes 786440 | tf_op jit(solution)/shard_map/ppermute | solution.py:30
  18.6 1.3 %collective-permute-start.14 = (bf16[2,128,512]{2,1,0:T(8,128)(2,1)S(1)}, bf16[2,128,512]{2,1,0:T(8,128)(2,1)S(1)}, u32[]{:S(2)}, u32[]{:S(2)}) collective-permute-start(bf16[2,128,512]{2,1,0:T(8,128)(2,1)S(1)} %get-tuple-element.17), channel_id=1, source_target_pairs={{0,384},{1,385},{2,386},{3,387},{4,388},{5,389},{6,390},{7,391},{8... | collective-permute-start | bytes 786440 | tf_op jit(solution)/shard_map/ppermute | solution.py:30
  19.9 1.3 %collective-permute-start.12 = (bf16[2,128,512]{2,1,0:T(8,128)(2,1)S(1)}, bf16[2,128,512]{2,1,0:T(8,128)(2,1)S(1)}, u32[]{:S(2)}, u32[]{:S(2)}) collective-permute-start(bf16[2,128,512]{2,1,0:T(8,128)(2,1)S(1)} %get-tuple-element.18), channel_id=1, source_target_pairs={{0,128},{1,129},{2,130},{3,131},{4,132},{5,133},{6,134},{7,135},{8... | collective-permute-start | bytes 786440 | tf_op jit(solution)/shard_map/ppermute | solution.py:30
  22.3 10.0 %collective-permute-start.4 = (bf16[2,32,512]{2,1,0:T(8,128)(2,1)S(1)}, bf16[2,32,512]{2,1,0:T(8,128)(2,1)S(1)}, u32[]{:S(2)}, u32[]{:S(2)}) collective-permute-start(bf16[2,32,512]{2,1,0:T(8,128)(2,1)S(1)} %slice.85), channel_id=1, source_target_pairs={{0,2},{4,6},{8,10},{12,14},{16,18},{20,22},{24,26},{28,30},{32,34}... | collective-permute-start | bytes 196616 | tf_op jit(solution)/shard_map/ppermute | solution.py:30
  35.1 1.3 %collective-permute-start.15 = (bf16[2,128,512]{2,1,0:T(8,128)(2,1)S(1)}, bf16[2,128,512]{2,1,0:T(8,128)(2,1)S(1)}, u32[]{:S(2)}, u32[]{:S(2)}) collective-permute-start(bf16[2,128,512]{2,1,0:T(8,128)(2,1)S(1)} %slice_select_fusion.1), channel_id=1, source_target_pairs={{0,64},{1,65},{2,66},{3,67},{4,68},{5,69},{6,70},{7,71},{8,72},{9,... | collective-permute-start | bytes 786440 | tf_op jit(solution)/shard_map/ppermute | solution.py:30
  36.5 2.9 %collective-permute-done.6 = bf16[2,48,512]{2,1,0:T(8,128)(2,1)S(1)} collective-permute-done((bf16[2,48,512]{2,1,0:T(8,128)(2,1)S(1)}, bf16[2,48,512]{2,1,0:T(8,128)(2,1)S(1)}, u32[]{:S(2)}, u32[]{:S(2)}) %collective-permute-start.6) | collective-permute-done | bytes 98336 | tf_op jit(solution)/shard_map/ppermute | solution.py:30
  39.5 3.0 %collective-permute-done.15 = bf16[2,128,512]{2,1,0:T(8,128)(2,1)S(1)} collective-permute-done((bf16[2,128,512]{2,1,0:T(8,128)(2,1)S(1)}, bf16[2,128,512]{2,1,0:T(8,128)(2,1)S(1)}, u32[]{:S(2)}, u32[]{:S(2)}) %collective-permute-start.15) | collective-permute-done | bytes 262176 | tf_op jit(solution)/shard_map/ppermute | solution.py:30
  42.5 1.3 %collective-permute-start.16 = (bf16[2,128,512]{2,1,0:T(8,128)(2,1)S(1)}, bf16[2,128,512]{2,1,0:T(8,128)(2,1)S(1)}, u32[]{:S(2)}, u32[]{:S(2)}) collective-permute-start(bf16[2,128,512]{2,1,0:T(8,128)(2,1)S(1)} %broadcast_select_fusion), channel_id=1, source_target_pairs={{0,32},{1,33},{2,34},{3,35},{4,36},{5,37},{6,38},{7,39},{8,40},{9,... | collective-permute-start | bytes 786440 | tf_op jit(solution)/shard_map/ppermute | solution.py:30
  43.9 5.0 %collective-permute-start.7 = (bf16[2,48,512]{2,1,0:T(8,128)(2,1)S(1)}, bf16[2,48,512]{2,1,0:T(8,128)(2,1)S(1)}, u32[]{:S(2)}, u32[]{:S(2)}) collective-permute-start(bf16[2,48,512]{2,1,0:T(8,128)(2,1)S(1)} %get-tuple-element.19), channel_id=1, source_target_pairs={{0,3},{2,1},{3,2},{4,7},{6,5},{7,6},{8,11},{10,9},{11,10},{12,15},... | collective-permute-start | bytes 294920 | tf_op jit(solution)/shard_map/ppermute | solution.py:30
  48.9 1.4 %collective-permute-start.5 = (bf16[2,48,512]{2,1,0:T(8,128)(2,1)S(1)}, bf16[2,48,512]{2,1,0:T(8,128)(2,1)S(1)}, u32[]{:S(2)}, u32[]{:S(2)}) collective-permute-start(bf16[2,48,512]{2,1,0:T(8,128)(2,1)S(1)} %get-tuple-element.20), channel_id=1, source_target_pairs={{0,1},{1,2},{2,3},{4,5},{5,6},{6,7},{8,9},{9,10},{10,11},{12,13},{... | collective-permute-start | bytes 294920 | tf_op jit(solution)/shard_map/ppermute | solution.py:30
  50.5 4.6 %collective-permute-start.17 = (bf16[2,128,512]{2,1,0:T(8,128)(2,1)S(1)}, bf16[2,128,512]{2,1,0:T(8,128)(2,1)S(1)}, u32[]{:S(2)}, u32[]{:S(2)}) collective-permute-start(bf16[2,128,512]{2,1,0:T(8,128)(2,1)S(1)} %get-tuple-element.12), channel_id=1, source_target_pairs={{0,256},{1,257},{2,258},{3,259},{4,260},{5,261},{6,262},{7,263},{8... | collective-permute-start | bytes 786440 | tf_op jit(solution)/shard_map/ppermute | solution.py:30
  55.1 2.2 %collective-permute-start.18 = (bf16[2,128,512]{2,1,0:T(8,128)(2,1)S(1)}, bf16[2,128,512]{2,1,0:T(8,128)(2,1)S(1)}, u32[]{:S(2)}, u32[]{:S(2)}) collective-permute-start(bf16[2,128,512]{2,1,0:T(8,128)(2,1)S(1)} %get-tuple-element.12), channel_id=1, source_target_pairs={{0,128},{1,129},{2,130},{3,131},{4,132},{5,133},{6,134},{7,135},{8... | collective-permute-start | bytes 786440 | tf_op jit(solution)/shard_map/ppermute | solution.py:30
  57.3 4.3 %collective-permute-start.19 = (bf16[2,128,512]{2,1,0:T(8,128)(2,1)S(1)}, bf16[2,128,512]{2,1,0:T(8,128)(2,1)S(1)}, u32[]{:S(2)}, u32[]{:S(2)}) collective-permute-start(bf16[2,128,512]{2,1,0:T(8,128)(2,1)S(1)} %get-tuple-element.12), channel_id=1, source_target_pairs={{0,384},{1,385},{2,386},{3,387},{4,388},{5,389},{6,390},{7,391},{8... | collective-permute-start | bytes 786440 | tf_op jit(solution)/shard_map/ppermute | solution.py:30
  61.7 4.0 %collective-permute-done.18 = bf16[2,128,512]{2,1,0:T(8,128)(2,1)S(1)} collective-permute-done((bf16[2,128,512]{2,1,0:T(8,128)(2,1)S(1)}, bf16[2,128,512]{2,1,0:T(8,128)(2,1)S(1)}, u32[]{:S(2)}, u32[]{:S(2)}) %collective-permute-start.18) | collective-permute-done | bytes 262176 | tf_op jit(solution)/shard_map/ppermute | solution.py:30
  66.0 5.6 %collective-permute-start.20 = (bf16[2,512,512]{2,1,0:T(8,128)(2,1)S(1)}, bf16[2,512,512]{2,1,0:T(8,128)(2,1)S(1)}, u32[]{:S(2)}, u32[]{:S(2)}) collective-permute-start(bf16[2,512,512]{2,1,0:T(8,128)(2,1)S(1)} %constant_dynamic-update-slice_fusion), channel_id=1, source_target_pairs={{0,16},{1,17},{2,18},{3,19},{4,20},{5,21},{6,22},{7,23},{8,24},{9,... | collective-permute-start | bytes 3145736 | tf_op jit(solution)/shard_map/ppermute | solution.py:30
  72.5 4.8 %collective-permute-start.8 = (bf16[2,128,512]{2,1,0:T(8,128)(2,1)}, bf16[2,128,512]{2,1,0:T(8,128)(2,1)}, u32[]{:S(2)}, u32[]{:S(2)}) collective-permute-start(bf16[2,128,512]{2,1,0:T(8,128)(2,1)} %get-tuple-element.10), channel_id=1, source_target_pairs={{0,8},{1,9},{2,10},{3,11},{4,12},{5,13},{6,14},{7,15},{8,0},{9,1},... | collective-permute-start | bytes 786440 | tf_op jit(solution)/shard_map/ppermute | solution.py:30
  77.3 2.3 %collective-permute-start.9 = (bf16[2,128,512]{2,1,0:T(8,128)(2,1)}, bf16[2,128,512]{2,1,0:T(8,128)(2,1)}, u32[]{:S(2)}, u32[]{:S(2)}) collective-permute-start(bf16[2,128,512]{2,1,0:T(8,128)(2,1)} %get-tuple-element.10), channel_id=1, source_target_pairs={{0,4},{1,5},{2,6},{3,7},{4,8},{5,9},{6,10},{7,11},{8,12},{9,13},{1... | collective-permute-start | bytes 786440 | tf_op jit(solution)/shard_map/ppermute | solution.py:30
  79.6 4.2 %collective-permute-start.10 = (bf16[2,128,512]{2,1,0:T(8,128)(2,1)}, bf16[2,128,512]{2,1,0:T(8,128)(2,1)S(1)}, u32[]{:S(2)}, u32[]{:S(2)}) collective-permute-start(bf16[2,128,512]{2,1,0:T(8,128)(2,1)} %get-tuple-element.10), channel_id=1, source_target_pairs={{0,12},{1,13},{2,14},{3,15},{4,0},{5,1},{6,2},{7,3},{8,4},{9,5},{1... | collective-permute-start | bytes 786440 | tf_op jit(solution)/shard_map/ppermute | solution.py:30
  85.1 5.0 %collective-permute-done.9 = bf16[2,128,512]{2,1,0:T(8,128)(2,1)} collective-permute-done((bf16[2,128,512]{2,1,0:T(8,128)(2,1)}, bf16[2,128,512]{2,1,0:T(8,128)(2,1)}, u32[]{:S(2)}, u32[]{:S(2)}) %collective-permute-start.9) | collective-permute-done | bytes 262176 | tf_op jit(solution)/shard_map/ppermute | solution.py:30
  94.7 1.5 %pad_maximum_fusion = bf16[2,512,1024]{2,1,0:T(8,128)(2,1)} fusion(bf16[1,512,1024]{2,1,0:T(8,128)(2,1)S(1)} %fusion.1, bf16[1,512,1024]{2,1,0:T(8,128)(2,1)S(1)} %fusion), kind=kLoop, calls=%fused_computation.1 | loop fusion | flops 1048576 | bytes 4194304 | tf_op jit(solution)/shard_map/stack | solution.py:105
  (48 shorter events, 13.3 us)
Async XLA Ops:
  0.0 3.7 %copy-start = (bf16[2,512,1024]{2,1,0:T(8,128)(2,1)S(1)}, bf16[2,512,1024]{2,1,0:T(8,128)(2,1)}, u32[]{:S(2)}) copy-start(bf16[2,512,1024]{2,1,0:T(8,128)(2,1)} %param.1) | copy-start | bytes 6291460
  2.4 11.9 %collective-permute-start.11 = (bf16[2,512,512]{2,1,0:T(8,128)(2,1)}, bf16[2,512,512]{2,1,0:T(8,128)(2,1)S(1)}, u32[]{:S(2)}, u32[]{:S(2)}) collective-permute-start(bf16[2,512,512]{2,1,0:T(8,128)(2,1)} %slice.75), channel_id=1, source_target_pairs={{0,16},{1,17},{2,18},{3,19},{4,20},{5,21},{6,22},{7,23},{8,24},{9,... | collective-permute-start | bytes 3145736 | tf_op jit(solution)/shard_map/ppermute | solution.py:30
  4.6 15.3 %collective-permute-start.1 = (bf16[2,128,512]{2,1,0:T(8,128)(2,1)}, bf16[2,128,512]{2,1,0:T(8,128)(2,1)S(1)}, u32[]{:S(2)}, u32[]{:S(2)}) collective-permute-start(bf16[2,128,512]{2,1,0:T(8,128)(2,1)} %get-tuple-element.13), channel_id=1, source_target_pairs={{0,8},{16,24},{32,40},{48,56},{64,72},{80,88},{96,104},{112,120},{... | collective-permute-start | bytes 786440 | tf_op jit(solution)/shard_map/ppermute | solution.py:30
  10.3 10.9 %collective-permute-start.2 = (bf16[2,128,512]{2,1,0:T(8,128)(2,1)}, bf16[2,128,512]{2,1,0:T(8,128)(2,1)}, u32[]{:S(2)}, u32[]{:S(2)}) collective-permute-start(bf16[2,128,512]{2,1,0:T(8,128)(2,1)} %get-tuple-element.14), channel_id=1, source_target_pairs={{0,12},{16,28},{32,44},{48,60},{64,76},{80,92},{96,108},{112,124},... | collective-permute-start | bytes 786440 | tf_op jit(solution)/shard_map/ppermute | solution.py:30
  12.3 8.9 %collective-permute-start = (bf16[2,128,512]{2,1,0:T(8,128)(2,1)}, bf16[2,128,512]{2,1,0:T(8,128)(2,1)}, u32[]{:S(2)}, u32[]{:S(2)}) collective-permute-start(bf16[2,128,512]{2,1,0:T(8,128)(2,1)} %get-tuple-element.15), channel_id=1, source_target_pairs={{0,4},{16,20},{32,36},{48,52},{64,68},{80,84},{96,100},{112,116},{... | collective-permute-start | bytes 786440 | tf_op jit(solution)/shard_map/ppermute | solution.py:30
  14.5 19.2 %collective-permute-start.13 = (bf16[2,128,512]{2,1,0:T(8,128)(2,1)S(1)}, bf16[2,128,512]{2,1,0:T(8,128)(2,1)S(1)}, u32[]{:S(2)}, u32[]{:S(2)}) collective-permute-start(bf16[2,128,512]{2,1,0:T(8,128)(2,1)S(1)} %get-tuple-element.16), channel_id=1, source_target_pairs={{0,256},{1,257},{2,258},{3,259},{4,260},{5,261},{6,262},{7,263},{8... | collective-permute-start | bytes 786440 | tf_op jit(solution)/shard_map/ppermute | solution.py:30
  18.6 16.4 %collective-permute-start.14 = (bf16[2,128,512]{2,1,0:T(8,128)(2,1)S(1)}, bf16[2,128,512]{2,1,0:T(8,128)(2,1)S(1)}, u32[]{:S(2)}, u32[]{:S(2)}) collective-permute-start(bf16[2,128,512]{2,1,0:T(8,128)(2,1)S(1)} %get-tuple-element.17), channel_id=1, source_target_pairs={{0,384},{1,385},{2,386},{3,387},{4,388},{5,389},{6,390},{7,391},{8... | collective-permute-start | bytes 786440 | tf_op jit(solution)/shard_map/ppermute | solution.py:30
  19.9 15.1 %collective-permute-start.12 = (bf16[2,128,512]{2,1,0:T(8,128)(2,1)S(1)}, bf16[2,128,512]{2,1,0:T(8,128)(2,1)S(1)}, u32[]{:S(2)}, u32[]{:S(2)}) collective-permute-start(bf16[2,128,512]{2,1,0:T(8,128)(2,1)S(1)} %get-tuple-element.18), channel_id=1, source_target_pairs={{0,128},{1,129},{2,130},{3,131},{4,132},{5,133},{6,134},{7,135},{8... | collective-permute-start | bytes 786440 | tf_op jit(solution)/shard_map/ppermute | solution.py:30
  22.3 14.1 %collective-permute-start.4 = (bf16[2,32,512]{2,1,0:T(8,128)(2,1)S(1)}, bf16[2,32,512]{2,1,0:T(8,128)(2,1)S(1)}, u32[]{:S(2)}, u32[]{:S(2)}) collective-permute-start(bf16[2,32,512]{2,1,0:T(8,128)(2,1)S(1)} %slice.85), channel_id=1, source_target_pairs={{0,2},{4,6},{8,10},{12,14},{16,18},{20,22},{24,26},{28,30},{32,34}... | collective-permute-start | bytes 196616 | tf_op jit(solution)/shard_map/ppermute | solution.py:30
  32.4 7.0 %collective-permute-start.6 = (bf16[2,48,512]{2,1,0:T(8,128)(2,1)S(1)}, bf16[2,48,512]{2,1,0:T(8,128)(2,1)S(1)}, u32[]{:S(2)}, u32[]{:S(2)}) collective-permute-start(bf16[2,48,512]{2,1,0:T(8,128)(2,1)S(1)} %get-tuple-element.21), channel_id=1, source_target_pairs={{0,3},{4,7},{8,11},{12,15},{16,19},{20,23},{24,27},{28,31},{32,35}... | collective-permute-start | bytes 294920 | tf_op jit(solution)/shard_map/ppermute | solution.py:30
  33.7 5.7 %collective-permute-start.3 = (bf16[2,48,512]{2,1,0:T(8,128)(2,1)S(1)}, bf16[2,48,512]{2,1,0:T(8,128)(2,1)S(1)}, u32[]{:S(2)}, u32[]{:S(2)}) collective-permute-start(bf16[2,48,512]{2,1,0:T(8,128)(2,1)S(1)} %get-tuple-element.22), channel_id=1, source_target_pairs={{0,1},{4,5},{8,9},{12,13},{16,17},{20,21},{24,25},{28,29},{32,33},... | collective-permute-start | bytes 294920 | tf_op jit(solution)/shard_map/ppermute | solution.py:30
  35.1 7.4 %collective-permute-start.15 = (bf16[2,128,512]{2,1,0:T(8,128)(2,1)S(1)}, bf16[2,128,512]{2,1,0:T(8,128)(2,1)S(1)}, u32[]{:S(2)}, u32[]{:S(2)}) collective-permute-start(bf16[2,128,512]{2,1,0:T(8,128)(2,1)S(1)} %slice_select_fusion.1), channel_id=1, source_target_pairs={{0,64},{1,65},{2,66},{3,67},{4,68},{5,69},{6,70},{7,71},{8,72},{9,... | collective-permute-start | bytes 786440 | tf_op jit(solution)/shard_map/ppermute | solution.py:30
  42.5 7.8 %collective-permute-start.16 = (bf16[2,128,512]{2,1,0:T(8,128)(2,1)S(1)}, bf16[2,128,512]{2,1,0:T(8,128)(2,1)S(1)}, u32[]{:S(2)}, u32[]{:S(2)}) collective-permute-start(bf16[2,128,512]{2,1,0:T(8,128)(2,1)S(1)} %broadcast_select_fusion), channel_id=1, source_target_pairs={{0,32},{1,33},{2,34},{3,35},{4,36},{5,37},{6,38},{7,39},{8,40},{9,... | collective-permute-start | bytes 786440 | tf_op jit(solution)/shard_map/ppermute | solution.py:30
  43.9 17.8 %collective-permute-start.7 = (bf16[2,48,512]{2,1,0:T(8,128)(2,1)S(1)}, bf16[2,48,512]{2,1,0:T(8,128)(2,1)S(1)}, u32[]{:S(2)}, u32[]{:S(2)}) collective-permute-start(bf16[2,48,512]{2,1,0:T(8,128)(2,1)S(1)} %get-tuple-element.19), channel_id=1, source_target_pairs={{0,3},{2,1},{3,2},{4,7},{6,5},{7,6},{8,11},{10,9},{11,10},{12,15},... | collective-permute-start | bytes 294920 | tf_op jit(solution)/shard_map/ppermute | solution.py:30
  48.9 12.7 %collective-permute-start.5 = (bf16[2,48,512]{2,1,0:T(8,128)(2,1)S(1)}, bf16[2,48,512]{2,1,0:T(8,128)(2,1)S(1)}, u32[]{:S(2)}, u32[]{:S(2)}) collective-permute-start(bf16[2,48,512]{2,1,0:T(8,128)(2,1)S(1)} %get-tuple-element.20), channel_id=1, source_target_pairs={{0,1},{1,2},{2,3},{4,5},{5,6},{6,7},{8,9},{9,10},{10,11},{12,13},{... | collective-permute-start | bytes 294920 | tf_op jit(solution)/shard_map/ppermute | solution.py:30
  50.5 11.2 %collective-permute-start.17 = (bf16[2,128,512]{2,1,0:T(8,128)(2,1)S(1)}, bf16[2,128,512]{2,1,0:T(8,128)(2,1)S(1)}, u32[]{:S(2)}, u32[]{:S(2)}) collective-permute-start(bf16[2,128,512]{2,1,0:T(8,128)(2,1)S(1)} %get-tuple-element.12), channel_id=1, source_target_pairs={{0,256},{1,257},{2,258},{3,259},{4,260},{5,261},{6,262},{7,263},{8... | collective-permute-start | bytes 786440 | tf_op jit(solution)/shard_map/ppermute | solution.py:30
  55.1 10.6 %collective-permute-start.18 = (bf16[2,128,512]{2,1,0:T(8,128)(2,1)S(1)}, bf16[2,128,512]{2,1,0:T(8,128)(2,1)S(1)}, u32[]{:S(2)}, u32[]{:S(2)}) collective-permute-start(bf16[2,128,512]{2,1,0:T(8,128)(2,1)S(1)} %get-tuple-element.12), channel_id=1, source_target_pairs={{0,128},{1,129},{2,130},{3,131},{4,132},{5,133},{6,134},{7,135},{8... | collective-permute-start | bytes 786440 | tf_op jit(solution)/shard_map/ppermute | solution.py:30
  57.3 8.6 %collective-permute-start.19 = (bf16[2,128,512]{2,1,0:T(8,128)(2,1)S(1)}, bf16[2,128,512]{2,1,0:T(8,128)(2,1)S(1)}, u32[]{:S(2)}, u32[]{:S(2)}) collective-permute-start(bf16[2,128,512]{2,1,0:T(8,128)(2,1)S(1)} %get-tuple-element.12), channel_id=1, source_target_pairs={{0,384},{1,385},{2,386},{3,387},{4,388},{5,389},{6,390},{7,391},{8... | collective-permute-start | bytes 786440 | tf_op jit(solution)/shard_map/ppermute | solution.py:30
  66.0 25.1 %collective-permute-start.20 = (bf16[2,512,512]{2,1,0:T(8,128)(2,1)S(1)}, bf16[2,512,512]{2,1,0:T(8,128)(2,1)S(1)}, u32[]{:S(2)}, u32[]{:S(2)}) collective-permute-start(bf16[2,512,512]{2,1,0:T(8,128)(2,1)S(1)} %constant_dynamic-update-slice_fusion), channel_id=1, source_target_pairs={{0,16},{1,17},{2,18},{3,19},{4,20},{5,21},{6,22},{7,23},{8,24},{9,... | collective-permute-start | bytes 3145736 | tf_op jit(solution)/shard_map/ppermute | solution.py:30
  72.5 11.6 %collective-permute-start.8 = (bf16[2,128,512]{2,1,0:T(8,128)(2,1)}, bf16[2,128,512]{2,1,0:T(8,128)(2,1)}, u32[]{:S(2)}, u32[]{:S(2)}) collective-permute-start(bf16[2,128,512]{2,1,0:T(8,128)(2,1)} %get-tuple-element.10), channel_id=1, source_target_pairs={{0,8},{1,9},{2,10},{3,11},{4,12},{5,13},{6,14},{7,15},{8,0},{9,1},... | collective-permute-start | bytes 786440 | tf_op jit(solution)/shard_map/ppermute | solution.py:30
  77.3 12.8 %collective-permute-start.9 = (bf16[2,128,512]{2,1,0:T(8,128)(2,1)}, bf16[2,128,512]{2,1,0:T(8,128)(2,1)}, u32[]{:S(2)}, u32[]{:S(2)}) collective-permute-start(bf16[2,128,512]{2,1,0:T(8,128)(2,1)} %get-tuple-element.10), channel_id=1, source_target_pairs={{0,4},{1,5},{2,6},{3,7},{4,8},{5,9},{6,10},{7,11},{8,12},{9,13},{1... | collective-permute-start | bytes 786440 | tf_op jit(solution)/shard_map/ppermute | solution.py:30
  79.6 11.4 %collective-permute-start.10 = (bf16[2,128,512]{2,1,0:T(8,128)(2,1)}, bf16[2,128,512]{2,1,0:T(8,128)(2,1)S(1)}, u32[]{:S(2)}, u32[]{:S(2)}) collective-permute-start(bf16[2,128,512]{2,1,0:T(8,128)(2,1)} %get-tuple-element.10), channel_id=1, source_target_pairs={{0,12},{1,13},{2,14},{3,15},{4,0},{5,1},{6,2},{7,3},{8,4},{9,5},{1... | collective-permute-start | bytes 786440 | tf_op jit(solution)/shard_map/ppermute | solution.py:30

commit v3 on v0

v3 whole, which is shorter than its diff:
```python
import jax
import jax.numpy as jnp
from jax import lax
from jax.experimental import pallas as pl
from jax.experimental.pallas import tpu as pltpu
from jax.sharding import PartitionSpec as P

WIDTH = 512
AXES = ("shot", "rcv")
NX, NL, NC, NY, NH = 4, 4, 2, 4, 4
VMEM = pl.BlockSpec(memory_space=pltpu.VMEM)
SMEM = pl.BlockSpec(memory_space=pltpu.SMEM)
HBM = pl.BlockSpec(memory_space=pl.ANY)


def moves(rule):
    pairs = []
    for x in range(NX):
        for l in range(NL):
            for c in range(NC):
                for y in range(NY):
                    for h in range(NH):
                        to = rule(x, l, c, y, h)
                        if to is None:
                            continue
                        X, L, C, Y, H = to
                        src = ((x * NL + l) * NC + c) * NY * NH + y * NH + h
                        dst = (((X % NX) * NL + L) * NC + C) * NY * NH + (Y % NY) * NH + H % NH
                        pairs.append((src, dst))
    return pairs


def send(value, rule):
    return lax.ppermute(value, AXES, moves(rule))


def pick(index, choices):
    out = choices[-1]
    for i, choice in enumerate(choices[:-1]):
        out = jnp.where(index == i, choice, out)
    return out


def cut_kernel(role, field, came, *refs):
    units, sem = refs[:-1], refs[-1]
    rows = units[0].shape[1]
    cols = units[0].shape[2]

    def run(copies):
        for copy in copies:
            copy.start()
        for copy in copies:
            copy.wait()

    @pl.when(role[0] == 1)
    def _():
        run([
            pltpu.make_async_copy(
                field.at[:, pl.ds(rows * d, rows), pl.ds(cols * t, cols)], unit.at[pl.ds(2 * t, 2)], sem.at[2 * d + t]
            )
            for d, unit in enumerate(units)
            for t in range(2)
        ])

    @pl.when(role[0] == 2)
    def _():
        run([
            pltpu.make_async_copy(
                came.at[:, pl.ds(rows * d, rows)] if t == 0 else field.at[:, pl.ds(rows * d, rows), pl.ds(0, cols)],
                unit.at[pl.ds(2 * t, 2)],
                sem.at[2 * d + t],
            )
            for d, unit in enumerate(units)
            for t in range(2)
        ])


def cut(role, field, came, unit_shape):
    return pl.pallas_call(
        cut_kernel,
        out_shape=[jax.ShapeDtypeStruct(unit_shape, jnp.bfloat16)] * 4,
        in_specs=[SMEM, HBM, HBM],
        out_specs=[VMEM] * 4,
        scratch_shapes=[pltpu.SemaphoreType.DMA((8,))],
        compiler_params=pltpu.CompilerParams(vmem_limit_bytes=16 * 1024 * 1024),
    )(role, field, came)


def product_kernel(at, *refs):
    mine, theirs = refs[0:4], refs[4:8]
    out, lre, lim, buf, sem = refs[8:]
    rows = mine[0].shape[1]
    dot = lambda a, b: jnp.dot(a, b, preferred_element_type=jnp.float32)

    def work(lefts, rights, first):
        for i, left in enumerate(lefts):
            for j in range(4):
                k = pl.ds(pl.multiple_of(at[5 + j], rows), rows)
                re, im = left[first, :, k], left[first + 1, :, k]
                here = pl.ds(rows * i, rows)
                lre[j, here, :rows] = -re
                lre[j, here, rows:] = im
                lim[j, here, :rows] = -im
                lim[j, here, rows:] = -re
        copies = []
        for i in range(4):
            here = pl.ds(rows * i, rows)
            for t in range(2):
                cols = pl.ds(WIDTH * t, WIDTH)
                for q, lhs in ((0, lre), (1, lim)):
                    acc = None
                    for j, right in enumerate(rights):
                        both = right[2 * t : 2 * t + 2].reshape(2 * rows, WIDTH)
                        term = dot(lhs[j, here], both)
                        acc = term if acc is None else acc + term
                    buf[i, q, :, cols] = acc.astype(buf.dtype)
            place = pl.ds(pl.multiple_of(at[1 + i], rows), rows)
            copies.append(pltpu.make_async_copy(buf.at[i], out.at[:, place], sem.at[i]))
            copies[-1].start()
        for copy in copies:
            copy.wait()

    @pl.when(at[0] == 0)
    def _():
        work(theirs, mine, 0)

    @pl.when(at[0] == 1)
    def _():
        work(mine, theirs, 2)


def product(at, mine, theirs, shape):
    rows = mine[0].shape[1]
    return pl.pallas_call(
        product_kernel,
        out_shape=jax.ShapeDtypeStruct(shape, jnp.bfloat16),
        in_specs=[SMEM] + [VMEM] * 8,
        out_specs=HBM,
        scratch_shapes=[
            pltpu.VMEM((4, 4 * rows, 2 * rows), jnp.bfloat16),
            pltpu.VMEM((4, 4 * rows, 2 * rows), jnp.bfloat16),
            pltpu.VMEM((4, 2, rows, shape[2]), jnp.bfloat16),
            pltpu.SemaphoreType.DMA((4,)),
        ],
        compiler_params=pltpu.CompilerParams(vmem_limit_bytes=40 * 1024 * 1024),
        cost_estimate=pl.CostEstimate(flops=8 * shape[1] * shape[2] * WIDTH, bytes_accessed=1 << 22, transcendentals=0),
    )(at, *mine, *theirs)


def per_device(field):
    s, r = lax.axis_index("shot"), lax.axis_index("rcv")
    x, l, c, y, h = s // (NL * NC), s // NC % NL, s % NC, r // NH, r % NH
    part = WIDTH // 4
    unit_shape = (4, part, WIDTH)

    came = send(field[:, :, :WIDTH], lambda x, l, c, y, h: (x, l, 1, y, h) if c == 0 and y == 0 and h == 0 else None)
    right_root = (c == 0) & (x == 0) & (l == 0)
    left_root = (c == 1) & (y == 0) & (h == 0)
    role = jnp.where(right_root, 1, jnp.where(left_root, 2, 0)).astype(jnp.int32).reshape(1)
    units = cut(role, field, came, unit_shape)

    def scatter(d):
        def rule(x, l, c, y, h):
            if c == 0:
                return (d, l, c, y, h) if x == 0 and l == 0 else None
            return (x, l, c, d, h) if y == 0 and h == 0 else None
        return rule

    got = {d: send(units[d], scatter(d)) for d in (2, 1, 3)}
    unit = jnp.where(jnp.where(c == 0, x, y) == 0, units[0], got[1] + got[2] + got[3])

    a, e = unit[:, : part // 2], unit[:, part // 2 :]

    def hop(to):
        def rule(x, l, c, y, h):
            if c == 0:
                return (x, 2, c, y, h) if l == 0 else None
            return (x, l, c, y, to) if h == 0 else None
        return rule

    za, ze = lax.optimization_barrier((send(a, hop(1)), send(e, hop(3))))

    def onwards(step, sources):
        def rule(x, l, c, y, h):
            if c == 0:
                return (x, l + 1, c, y, h) if l in (0, 2) else None
            return (x, l, c, y, h + step) if h in sources else None
        return rule

    start = jnp.where(c == 0, l, h) == 0
    up = jnp.where(start, jnp.where(c == 0, a, e), za)
    down = jnp.where(start, jnp.where(c == 0, e, a), ze)
    up, down = lax.optimization_barrier((up, down))
    gup, gdown = send(up, onwards(1, (0, 1))), send(down, onwards(-1, (0, 3)))
    a_from = jnp.where(c == 0, pick(l, (0, 2, 1, 2)), pick(h, (0, 1, 2, 3)))
    e_from = jnp.where(c == 0, pick(l, (0, 3, 1, 3)), pick(h, (0, 2, 3, 1)))
    unit = jnp.concatenate([pick(a_from, (a, za, gup, gdown)), pick(e_from, (e, ze, gup, gdown))], 1)

    def gather(d):
        return lambda x, l, c, y, h: (x + d, l, c, y, h) if c == 0 else (x, l, c, y + d, h)

    order = (0, 2, 1, 3)
    mine = [unit] + [send(unit, gather(d)) for d in order[1:]]
    theirs = [send(value, lambda x, l, c, y, h: (x, l, 1 - c, y, h)) for value in mine]
    at = jnp.stack([c] + [(y - d) % NY * part for d in order] + [(x - d) % NX * part for d in order]).astype(jnp.int32)
    return product(at, mine, theirs, field.shape)


def solution(mesh):
    return jax.shard_map(
        per_device,
        mesh=mesh,
        in_specs=(P(None, "shot", "rcv"),),
        out_specs=P(None, "shot", "rcv"),
        check_vma=False,
    )
```

time: 537 us -> 88.7 us (0.17)
  the two profiles are of different devices: /device:TPU:1 before, /device:TPU:249 now
where the time goes in v3:
time: 88.7 us; the launch traced here: 88.2 us
  starting transfers between devices  41.3 us (47%)
  waiting for transfers between devices  37 us (42%)
  Pallas kernels  5.68 us (6%)
  local copies, waits for them, and re-layouts  3.34 us (4%)
    ppermute x15, starting transfers between devices, send(): return lax.ppermute(value, AXES, moves(rule))  41.3 us
    ppermute x15, waiting for transfers between devices, send(): return lax.ppermute(value, AXES, moves(rule))  37 us
    pallas_call x1, Pallas kernels, product(): pl.pallas_call(product_kernel, out_shape=jax.ShapeDtypeStruct(shape, jnp....  4.45 us
    slice x1, local copies, waits for them, and re-layouts, per_device(): field[:, :, :WIDTH]  2.41 us
  transfers between devices with their start and end apart: 15, of which 3 were waited for; matrix products, arithmetic and copies ran while one was open for 0% of the time, Pallas kernels for 0%

profile of v3, /device:TPU:249, one launch (start us, length us, event | category | flops | bytes accessed | tf_op | source)
XLA Modules:
  0.0 88.2 jit_solution(10040799051271970024)
XLA Ops:
  0.0 2.4 %slice.9 = bf16[2,512,512]{2,1,0:T(8,128)(2,1)} slice(bf16[2,512,1024]{2,1,0:T(8,128)(2,1)} %field.1), slice={[0:2], [0:512], [0:512]} | slice | bytes 2097152 | tf_op jit(solution)/shard_map/slice | solution.py:156
  2.4 0.7 collective-permute-start
  3.2 1.2 %shard_map.17 = (bf16[4,128,512]{2,1,0:T(8,128)(2,1)S(1)}, bf16[4,128,512]{2,1,0:T(8,128)(2,1)}, bf16[4,128,512]{2,1,0:T(8,128)(2,1)}, bf16[4,128,512]{2,1,0:T(8,128)(2,1)}) custom-call(s32[1]{0:T(128)} %bitcast.9.role, bf16[2,512,1024]{2,1,0:T(8,128)(2,1)S(1)} %copy-done, bf16[2,512,512]{2,1,0:T(8,128)(2,1)S(1)} %collective-permute-done.came), custom_call_target="tpu_custom_call" | custom-call | tf_op jit(solution)/shard_map/pallas_call | solution.py:79
  4.5 0.8 copy-done.1
  5.3 0.7 collective-permute-start.1
  6.0 0.7 collective-permute-start.2
  6.7 0.7 collective-permute-start.3
  7.4 0.1 add_select_fusion
  7.6 0.7 collective-permute-start.5
  8.3 1.3 %collective-permute-start.4 = (bf16[4,64,512]{2,1,0:T(8,128)(2,1)S(1)}, bf16[4,64,512]{2,1,0:T(8,128)(2,1)S(1)}, u32[]{:S(2)}, u32[]{:S(2)}) collective-permute-start(bf16[4,64,512]{2,1,0:T(8,128)(2,1)S(1)} %get-tuple-element.26), channel_id=1, source_target_pairs={{0,64},{1,65},{2,66},{3,67},{4,68},{5,69},{6,70},{7,71},{8,72},{9,... | collective-permute-start | bytes 786440 | tf_op jit(solution)/shard_map/ppermute | solution.py:34
  9.6 21.4 %collective-permute-done.4 = bf16[4,64,512]{2,1,0:T(8,128)(2,1)S(1)} collective-permute-done((bf16[4,64,512]{2,1,0:T(8,128)(2,1)S(1)}, bf16[4,64,512]{2,1,0:T(8,128)(2,1)S(1)}, u32[]{:S(2)}, u32[]{:S(2)}) %collective-permute-start.4) | collective-permute-done | bytes 262176 | tf_op jit(solution)/shard_map/ppermute | solution.py:34
  31.0 1.9 %collective-permute-start.6 = (bf16[4,64,512]{2,1,0:T(8,128)(2,1)S(1)}, bf16[4,64,512]{2,1,0:T(8,128)(2,1)S(1)}, u32[]{:S(2)}, u32[]{:S(2)}) collective-permute-start(bf16[4,64,512]{2,1,0:T(8,128)(2,1)S(1)} %get-tuple-element.19), channel_id=1, source_target_pairs={{0,32},{1,33},{2,34},{3,35},{4,36},{5,37},{6,38},{7,39},{8,40},{9,... | collective-permute-start | bytes 786440 | tf_op jit(solution)/shard_map/ppermute | solution.py:34
  33.0 0.7 collective-permute-start.7
  33.7 14.2 %collective-permute-done.6 = bf16[4,64,512]{2,1,0:T(8,128)(2,1)S(1)} collective-permute-done((bf16[4,64,512]{2,1,0:T(8,128)(2,1)S(1)}, bf16[4,64,512]{2,1,0:T(8,128)(2,1)S(1)}, u32[]{:S(2)}, u32[]{:S(2)}) %collective-permute-start.6) | collective-permute-done | bytes 262176 | tf_op jit(solution)/shard_map/ppermute | solution.py:34
  48.1 4.4 %collective-permute-start.10 = (bf16[4,128,512]{2,1,0:T(8,128)(2,1)S(1)}, bf16[4,128,512]{2,1,0:T(8,128)(2,1)S(1)}, u32[]{:S(2)}, u32[]{:S(2)}) collective-permute-start(bf16[4,128,512]{2,1,0:T(8,128)(2,1)S(1)} %pad_maximum_fusion.refs_0_), channel_id=1, source_target_pairs={{0,384},{1,385},{2,386},{3,387},{4,388},{5,389},{6,390},{7,391},{8... | collective-permute-start | bytes 1572872 | tf_op jit(solution)/shard_map/ppermute | solution.py:34
  52.4 2.1 %collective-permute-start.9 = (bf16[4,128,512]{2,1,0:T(8,128)(2,1)S(1)}, bf16[4,128,512]{2,1,0:T(8,128)(2,1)S(1)}, u32[]{:S(2)}, u32[]{:S(2)}) collective-permute-start(bf16[4,128,512]{2,1,0:T(8,128)(2,1)S(1)} %pad_maximum_fusion.refs_0_), channel_id=1, source_target_pairs={{0,128},{1,129},{2,130},{3,131},{4,132},{5,133},{6,134},{7,135},{8... | collective-permute-start | bytes 1572872 | tf_op jit(solution)/shard_map/ppermute | solution.py:34
  54.6 3.5 %collective-permute-start.8 = (bf16[4,128,512]{2,1,0:T(8,128)(2,1)S(1)}, bf16[4,128,512]{2,1,0:T(8,128)(2,1)S(1)}, u32[]{:S(2)}, u32[]{:S(2)}) collective-permute-start(bf16[4,128,512]{2,1,0:T(8,128)(2,1)S(1)} %pad_maximum_fusion.refs_0_), channel_id=1, source_target_pairs={{0,256},{1,257},{2,258},{3,259},{4,260},{5,261},{6,262},{7,263},{8... | collective-permute-start | bytes 1572872 | tf_op jit(solution)/shard_map/ppermute | solution.py:34
  58.1 13.2 %collective-permute-start.11 = (bf16[4,128,512]{2,1,0:T(8,128)(2,1)S(1)}, bf16[4,128,512]{2,1,0:T(8,128)(2,1)S(1)}, u32[]{:S(2)}, u32[]{:S(2)}) collective-permute-start(bf16[4,128,512]{2,1,0:T(8,128)(2,1)S(1)} %pad_maximum_fusion.refs_0_), channel_id=1, source_target_pairs={{0,16},{1,17},{2,18},{3,19},{4,20},{5,21},{6,22},{7,23},{8,24},{9,... | collective-permute-start | bytes 1572872 | tf_op jit(solution)/shard_map/ppermute | solution.py:34
  71.3 1.9 %collective-permute-start.14 = (bf16[4,128,512]{2,1,0:T(8,128)(2,1)S(1)}, bf16[4,128,512]{2,1,0:T(8,128)(2,1)S(1)}, u32[]{:S(2)}, u32[]{:S(2)}) collective-permute-start(bf16[4,128,512]{2,1,0:T(8,128)(2,1)S(1)} %collective-permute-done.10.refs_3_), channel_id=1, source_target_pairs={{0,16},{1,17},{2,18},{3,19},{4,20},{5,21},{6,22},{7,23},{8,24},{9,... | collective-permute-start | bytes 1572872 | tf_op jit(solution)/shard_map/ppermute | solution.py:34
  73.2 2.4 %collective-permute-start.13 = (bf16[4,128,512]{2,1,0:T(8,128)(2,1)S(1)}, bf16[4,128,512]{2,1,0:T(8,128)(2,1)}, u32[]{:S(2)}, u32[]{:S(2)}) collective-permute-start(bf16[4,128,512]{2,1,0:T(8,128)(2,1)S(1)} %collective-permute-done.9.refs_2_), channel_id=1, source_target_pairs={{0,16},{1,17},{2,18},{3,19},{4,20},{5,21},{6,22},{7,23},{8,24},{9,... | collective-permute-start | bytes 1572872 | tf_op jit(solution)/shard_map/ppermute | solution.py:34
  75.6 6.4 %collective-permute-start.12 = (bf16[4,128,512]{2,1,0:T(8,128)(2,1)S(1)}, bf16[4,128,512]{2,1,0:T(8,128)(2,1)}, u32[]{:S(2)}, u32[]{:S(2)}) collective-permute-start(bf16[4,128,512]{2,1,0:T(8,128)(2,1)S(1)} %collective-permute-done.8.refs_1_), channel_id=1, source_target_pairs={{0,16},{1,17},{2,18},{3,19},{4,20},{5,21},{6,22},{7,23},{8,24},{9,... | collective-permute-start | bytes 1572872 | tf_op jit(solution)/shard_map/ppermute | solution.py:34
  82.2 0.1 stack.39.at
  82.3 1.4 %collective-permute-done.12.refs_5_ = bf16[4,128,512]{2,1,0:T(8,128)(2,1)} collective-permute-done((bf16[4,128,512]{2,1,0:T(8,128)(2,1)S(1)}, bf16[4,128,512]{2,1,0:T(8,128)(2,1)}, u32[]{:S(2)}, u32[]{:S(2)}) %collective-permute-start.12) | collective-permute-done | bytes 524320 | tf_op jit(solution)/shard_map/ppermute | solution.py:34
  83.7 4.4 %shard_map.18 = bf16[2,512,1024]{2,1,0:T(8,128)(2,1)} custom-call(s32[9]{0:T(128)S(1)} %stack.39.at, bf16[4,128,512]{2,1,0:T(8,128)(2,1)S(1)} %pad_maximum_fusion.refs_0_, bf16[4,128,512]{2,1,0:T(8,128)(2,1)S(1)} %collective-permute-done.8.refs_1_, bf16[4,128,512]{2,1,0:T(8,128)(2,1)S(1)} %collective-permute-done.9.refs_2_, ...), custom_call_target="tpu_custom_call" | custom-call | flops 2147483648 | bytes 4194304 | tf_op jit(solution)/shard_map/pallas_call | solution.py:134
  (19 shorter events, 0.2 us)
Async XLA Ops:
  0.0 3.2 %copy-start = (bf16[2,512,1024]{2,1,0:T(8,128)(2,1)S(1)}, bf16[2,512,1024]{2,1,0:T(8,128)(2,1)}, u32[]{:S(2)}) copy-start(bf16[2,512,1024]{2,1,0:T(8,128)(2,1)} %field.1) | copy-start | bytes 6291460
  2.4 0.8 collective-permute-start
  4.5 0.8 copy-start.1
  5.3 2.1 %collective-permute-start.1 = (bf16[4,128,512]{2,1,0:T(8,128)(2,1)}, bf16[4,128,512]{2,1,0:T(8,128)(2,1)S(1)}, u32[]{:S(2)}, u32[]{:S(2)}) collective-permute-start(bf16[4,128,512]{2,1,0:T(8,128)(2,1)} %get-tuple-element.14), channel_id=1, source_target_pairs={{0,128},{1,129},{2,130},{3,131},{4,132},{5,133},{6,134},{7,135},{8... | collective-permute-start | bytes 1572872 | tf_op jit(solution)/shard_map/ppermute | solution.py:34
  6.0 1.4 %collective-permute-start.2 = (bf16[4,128,512]{2,1,0:T(8,128)(2,1)}, bf16[4,128,512]{2,1,0:T(8,128)(2,1)S(1)}, u32[]{:S(2)}, u32[]{:S(2)}) collective-permute-start(bf16[4,128,512]{2,1,0:T(8,128)(2,1)} %get-tuple-element.15), channel_id=1, source_target_pairs={{0,256},{1,257},{2,258},{3,259},{4,260},{5,261},{6,262},{7,263},{8... | collective-permute-start | bytes 1572872 | tf_op jit(solution)/shard_map/ppermute | solution.py:34
  6.7 0.7 collective-permute-start.3
  7.6 2.0 %collective-permute-start.5 = (bf16[4,64,512]{2,1,0:T(8,128)(2,1)S(1)}, bf16[4,64,512]{2,1,0:T(8,128)(2,1)S(1)}, u32[]{:S(2)}, u32[]{:S(2)}) collective-permute-start(bf16[4,64,512]{2,1,0:T(8,128)(2,1)S(1)} %get-tuple-element.25), channel_id=1, source_target_pairs={{0,64},{1,65},{2,66},{3,67},{4,68},{5,69},{6,70},{7,71},{8,72},{9,... | collective-permute-start | bytes 786440 | tf_op jit(solution)/shard_map/ppermute | solution.py:34
  8.3 22.7 %collective-permute-start.4 = (bf16[4,64,512]{2,1,0:T(8,128)(2,1)S(1)}, bf16[4,64,512]{2,1,0:T(8,128)(2,1)S(1)}, u32[]{:S(2)}, u32[]{:S(2)}) collective-permute-start(bf16[4,64,512]{2,1,0:T(8,128)(2,1)S(1)} %get-tuple-element.26), channel_id=1, source_target_pairs={{0,64},{1,65},{2,66},{3,67},{4,68},{5,69},{6,70},{7,71},{8,72},{9,... | collective-permute-start | bytes 786440 | tf_op jit(solution)/shard_map/ppermute | solution.py:34
  31.0 16.9 %collective-permute-start.6 = (bf16[4,64,512]{2,1,0:T(8,128)(2,1)S(1)}, bf16[4,64,512]{2,1,0:T(8,128)(2,1)S(1)}, u32[]{:S(2)}, u32[]{:S(2)}) collective-permute-start(bf16[4,64,512]{2,1,0:T(8,128)(2,1)S(1)} %get-tuple-element.19), channel_id=1, source_target_pairs={{0,32},{1,33},{2,34},{3,35},{4,36},{5,37},{6,38},{7,39},{8,40},{9,... | collective-permute-start | bytes 786440 | tf_op jit(solution)/shard_map/ppermute | solution.py:34
  33.0 15.0 %collective-permute-start.7 = (bf16[4,64,512]{2,1,0:T(8,128)(2,1)S(1)}, bf16[4,64,512]{2,1,0:T(8,128)(2,1)S(1)}, u32[]{:S(2)}, u32[]{:S(2)}) collective-permute-start(bf16[4,64,512]{2,1,0:T(8,128)(2,1)S(1)} %get-tuple-element.20), channel_id=1, source_target_pairs={{0,32},{1,33},{2,34},{3,35},{4,36},{5,37},{6,38},{7,39},{8,40},{9,... | collective-permute-start | bytes 786440 | tf_op jit(solution)/shard_map/ppermute | solution.py:34
  48.1 23.2 %collective-permute-start.10 = (bf16[4,128,512]{2,1,0:T(8,128)(2,1)S(1)}, bf16[4,128,512]{2,1,0:T(8,128)(2,1)S(1)}, u32[]{:S(2)}, u32[]{:S(2)}) collective-permute-start(bf16[4,128,512]{2,1,0:T(8,128)(2,1)S(1)} %pad_maximum_fusion.refs_0_), channel_id=1, source_target_pairs={{0,384},{1,385},{2,386},{3,387},{4,388},{5,389},{6,390},{7,391},{8... | collective-permute-start | bytes 1572872 | tf_op jit(solution)/shard_map/ppermute | solution.py:34
  52.4 20.8 %collective-permute-start.9 = (bf16[4,128,512]{2,1,0:T(8,128)(2,1)S(1)}, bf16[4,128,512]{2,1,0:T(8,128)(2,1)S(1)}, u32[]{:S(2)}, u32[]{:S(2)}) collective-permute-start(bf16[4,128,512]{2,1,0:T(8,128)(2,1)S(1)} %pad_maximum_fusion.refs_0_), channel_id=1, source_target_pairs={{0,128},{1,129},{2,130},{3,131},{4,132},{5,133},{6,134},{7,135},{8... | collective-permute-start | bytes 1572872 | tf_op jit(solution)/shard_map/ppermute | solution.py:34
  54.6 21.1 %collective-permute-start.8 = (bf16[4,128,512]{2,1,0:T(8,128)(2,1)S(1)}, bf16[4,128,512]{2,1,0:T(8,128)(2,1)S(1)}, u32[]{:S(2)}, u32[]{:S(2)}) collective-permute-start(bf16[4,128,512]{2,1,0:T(8,128)(2,1)S(1)} %pad_maximum_fusion.refs_0_), channel_id=1, source_target_pairs={{0,256},{1,257},{2,258},{3,259},{4,260},{5,261},{6,262},{7,263},{8... | collective-permute-start | bytes 1572872 | tf_op jit(solution)/shard_map/ppermute | solution.py:34
  58.1 24.2 %collective-permute-start.11 = (bf16[4,128,512]{2,1,0:T(8,128)(2,1)S(1)}, bf16[4,128,512]{2,1,0:T(8,128)(2,1)S(1)}, u32[]{:S(2)}, u32[]{:S(2)}) collective-permute-start(bf16[4,128,512]{2,1,0:T(8,128)(2,1)S(1)} %pad_maximum_fusion.refs_0_), channel_id=1, source_target_pairs={{0,16},{1,17},{2,18},{3,19},{4,20},{5,21},{6,22},{7,23},{8,24},{9,... | collective-permute-start | bytes 1572872 | tf_op jit(solution)/shard_map/ppermute | solution.py:34
  71.3 11.0 %collective-permute-start.14 = (bf16[4,128,512]{2,1,0:T(8,128)(2,1)S(1)}, bf16[4,128,512]{2,1,0:T(8,128)(2,1)S(1)}, u32[]{:S(2)}, u32[]{:S(2)}) collective-permute-start(bf16[4,128,512]{2,1,0:T(8,128)(2,1)S(1)} %collective-permute-done.10.refs_3_), channel_id=1, source_target_pairs={{0,16},{1,17},{2,18},{3,19},{4,20},{5,21},{6,22},{7,23},{8,24},{9,... | collective-permute-start | bytes 1572872 | tf_op jit(solution)/shard_map/ppermute | solution.py:34
  73.2 9.1 %collective-permute-start.13 = (bf16[4,128,512]{2,1,0:T(8,128)(2,1)S(1)}, bf16[4,128,512]{2,1,0:T(8,128)(2,1)}, u32[]{:S(2)}, u32[]{:S(2)}) collective-permute-start(bf16[4,128,512]{2,1,0:T(8,128)(2,1)S(1)} %collective-permute-done.9.refs_2_), channel_id=1, source_target_pairs={{0,16},{1,17},{2,18},{3,19},{4,20},{5,21},{6,22},{7,23},{8,24},{9,... | collective-permute-start | bytes 1572872 | tf_op jit(solution)/shard_map/ppermute | solution.py:34
  75.6 8.1 %collective-permute-start.12 = (bf16[4,128,512]{2,1,0:T(8,128)(2,1)S(1)}, bf16[4,128,512]{2,1,0:T(8,128)(2,1)}, u32[]{:S(2)}, u32[]{:S(2)}) collective-permute-start(bf16[4,128,512]{2,1,0:T(8,128)(2,1)S(1)} %collective-permute-done.8.refs_1_), channel_id=1, source_target_pairs={{0,16},{1,17},{2,18},{3,19},{4,20},{5,21},{6,22},{7,23},{8,24},{9,... | collective-permute-start | bytes 1572872 | tf_op jit(solution)/shard_map/ppermute | solution.py:34

commit v4 on v3

--- a/solution.py
+++ b/solution.py
@@ -10,7 +10,7 @@
 NX, NL, NC, NY, NH = 4, 4, 2, 4, 4
 VMEM = pl.BlockSpec(memory_space=pltpu.VMEM)
 SMEM = pl.BlockSpec(memory_space=pltpu.SMEM)
-HBM = pl.BlockSpec(memory_space=pl.ANY)
+HBM = pl.BlockSpec(memory_space=pltpu.HBM)
 
 
 def moves(rule):
@@ -41,49 +41,73 @@
     return out
 
 
-def cut_kernel(role, field, came, *refs):
-    units, sem = refs[:-1], refs[-1]
-    rows = units[0].shape[1]
-    cols = units[0].shape[2]
-
-    def run(copies):
-        for copy in copies:
-            copy.start()
-        for copy in copies:
-            copy.wait()
+def run(copies):
+    for copy in copies:
+        copy.start()
+    for copy in copies:
+        copy.wait()
+
+
+def first_kernel(role, field, *refs):
+    panel, bits, sem = refs[0], refs[1:-1], refs[-1]
+    rows = bits[0].shape[1]
+    cols = bits[0].shape[2]
 
     @pl.when(role[0] == 1)
     def _():
         run([
             pltpu.make_async_copy(
-                field.at[:, pl.ds(rows * d, rows), pl.ds(cols * t, cols)], unit.at[pl.ds(2 * t, 2)], sem.at[2 * d + t]
+                field.at[:, pl.ds(rows * i, rows), pl.ds(cols * t, cols)], bit.at[pl.ds(2 * t, 2)], sem.at[2 * i + t]
             )
-            for d, unit in enumerate(units)
+            for i, bit in enumerate(bits)
             for t in range(2)
         ])
 
-    @pl.when(role[0] == 2)
+    @pl.when(role[1] == 1)
+    def _():
+        run([pltpu.make_async_copy(field.at[:, :, pl.ds(0, cols)], panel, sem.at[16])])
+
+
+def first(role, field, shape):
+    return pl.pallas_call(
+        first_kernel,
+        out_shape=[jax.ShapeDtypeStruct((2, field.shape[1], WIDTH), jnp.bfloat16)]
+        + [jax.ShapeDtypeStruct(shape, jnp.bfloat16)] * 8,
+        in_specs=[SMEM, HBM],
+        out_specs=[VMEM] * 9,
+        scratch_shapes=[pltpu.SemaphoreType.DMA((17,))],
+        compiler_params=pltpu.CompilerParams(vmem_limit_bytes=16 * 1024 * 1024),
+    )(role, field)
+
+
+def second_kernel(role, field, came, *refs):
+    bits, sem = refs[8:-1], refs[-1]
+    rows = bits[0].shape[1]
+    cols = bits[0].shape[2]
+
+    @pl.when(role[2] == 1)
     def _():
         run([
             pltpu.make_async_copy(
-                came.at[:, pl.ds(rows * d, rows)] if t == 0 else field.at[:, pl.ds(rows * d, rows), pl.ds(0, cols)],
-                unit.at[pl.ds(2 * t, 2)],
-                sem.at[2 * d + t],
+                came.at[:, pl.ds(rows * i, rows)] if t == 0 else field.at[:, pl.ds(rows * i, rows), pl.ds(0, cols)],
+                bit.at[pl.ds(2 * t, 2)],
+                sem.at[2 * i + t],
             )
-            for d, unit in enumerate(units)
+            for i, bit in enumerate(bits)
             for t in range(2)
         ])
 
 
-def cut(role, field, came, unit_shape):
+def second(role, field, came, bits):
     return pl.pallas_call(
-        cut_kernel,
-        out_shape=[jax.ShapeDtypeStruct(unit_shape, jnp.bfloat16)] * 4,
-        in_specs=[SMEM, HBM, HBM],
-        out_specs=[VMEM] * 4,
-        scratch_shapes=[pltpu.SemaphoreType.DMA((8,))],
+        second_kernel,
+        out_shape=[jax.ShapeDtypeStruct(bit.shape, bit.dtype) for bit in bits],
+        in_specs=[SMEM, HBM] + [VMEM] * 9,
+        out_specs=[VMEM] * 8,
+        input_output_aliases={3 + i: i for i in range(8)},
+        scratch_shapes=[pltpu.SemaphoreType.DMA((16,))],
         compiler_params=pltpu.CompilerParams(vmem_limit_bytes=16 * 1024 * 1024),
-    )(role, field, came)
+    )(role, field, came, *bits)
 
 
 def product_kernel(at, *refs):
@@ -151,13 +175,12 @@
     s, r = lax.axis_index("shot"), lax.axis_index("rcv")
     x, l, c, y, h = s // (NL * NC), s // NC % NL, s % NC, r // NH, r % NH
     part = WIDTH // 4
-    unit_shape = (4, part, WIDTH)
-
-    came = send(field[:, :, :WIDTH], lambda x, l, c, y, h: (x, l, 1, y, h) if c == 0 and y == 0 and h == 0 else None)
-    right_root = (c == 0) & (x == 0) & (l == 0)
-    left_root = (c == 1) & (y == 0) & (h == 0)
-    role = jnp.where(right_root, 1, jnp.where(left_root, 2, 0)).astype(jnp.int32).reshape(1)
-    units = cut(role, field, came, unit_shape)
+
+    left_root = (y == 0) & (h == 0)
+    role = jnp.stack([(c == 0) & (x == 0) & (l == 0), left_root & (c == 0), left_root & (c == 1)]).astype(jnp.int32)
+    panel, *bits = first(role, field, (4, part // 2, WIDTH))
+    came = send(panel, lambda x, l, c, y, h: (x, l, 1, y, h) if c == 0 and y == 0 and h == 0 else None)
+    bits = second(role, field, came, bits)
 
     def scatter(d):
         def rule(x, l, c, y, h):
@@ -166,10 +189,12 @@
             return (x, l, c, d, h) if y == 0 and h == 0 else None
         return rule
 
-    got = {d: send(units[d], scatter(d)) for d in (2, 1, 3)}
-    unit = jnp.where(jnp.where(c == 0, x, y) == 0, units[0], got[1] + got[2] + got[3])
-
-    a, e = unit[:, : part // 2], unit[:, part // 2 :]
+    at_root = jnp.where(c == 0, x, y) == 0
+    a, e = (
+        jnp.where(at_root, bits[t], sum(send(bits[2 * d + t], scatter(d)) for d in (1, 3, 2)))
+        for t in range(2)
+    )
+
 
     def hop(to):
         def rule(x, l, c, y, h):
@@ -199,7 +224,7 @@
     def gather(d):
         return lambda x, l, c, y, h: (x + d, l, c, y, h) if c == 0 else (x, l, c, y + d, h)
 
-    order = (0, 2, 1, 3)
+    order = (0, 1, 3, 2)
     mine = [unit] + [send(unit, gather(d)) for d in order[1:]]
     theirs = [send(value, lambda x, l, c, y, h: (x, l, 1 - c, y, h)) for value in mine]
     at = jnp.stack([c] + [(y - d) % NY * part for d in order] + [(x - d) % NX * part for d in order]).astype(jnp.int32)

time: 88.7 us -> 80.5 us (0.908)
  the two profiles are of different devices: /device:TPU:249 before, /device:TPU:1 now
where the time goes in v4:
time: 80.5 us; the launch traced here: 80 us
  starting transfers between devices  39 us (48%)
  waiting for transfers between devices  31.6 us (39%)
  Pallas kernels  6.87 us (9%)
  local copies, waits for them, and re-layouts  1.68 us (2%)
    ppermute x18, starting transfers between devices, send(): return lax.ppermute(value, AXES, moves(rule))  39 us
    ppermute x18, waiting for transfers between devices, send(): return lax.ppermute(value, AXES, moves(rule))  31.6 us
    pallas_call x1, Pallas kernels, product(): pl.pallas_call(product_kernel, out_shape=jax.ShapeDtypeStruct(shape, jnp....  4.45 us
    pallas_call x1, Pallas kernels, second(): pl.pallas_call(second_kernel, out_shape=[jax.ShapeDtypeStruct(bit.shape,...  1.71 us
  transfers between devices with their start and end apart: 18, of which 9 were waited for; matrix products, arithmetic and copies ran while one was open for 0% of the time, Pallas kernels for 0%

profile of v4, /device:TPU:1, one launch (start us, length us, event | category | flops | bytes accessed | tf_op | source)
XLA Modules:
  0.0 80.0 jit_solution(13179632697337038647)
XLA Ops:
  0.1 1.6 %copy-done = bf16[2,512,1024]{2,1,0:T(8,128)(2,1)S(1)} copy-done((bf16[2,512,1024]{2,1,0:T(8,128)(2,1)S(1)}, bf16[2,512,1024]{2,1,0:T(8,128)(2,1)}, u32[]{:S(2)}) %copy-start) | copy-done | bytes 2097176
  3.7 9.5 %collective-permute-done.came = bf16[2,512,512]{2,1,0:T(8,128)(2,1)S(1)} collective-permute-done((bf16[2,512,512]{2,1,0:T(8,128)(2,1)S(1)}, bf16[2,512,512]{2,1,0:T(8,128)(2,1)S(1)}, u32[]{:S(2)}, u32[]{:S(2)}) %collective-permute-start) | collective-permute-done | bytes 1048608 | tf_op jit(solution)/shard_map/ppermute | solution.py:34
  13.2 1.7 %shard_map.18 = (bf16[4,64,512]{2,1,0:T(8,128)(2,1)S(1)}, bf16[4,64,512]{2,1,0:T(8,128)(2,1)S(1)}, bf16[4,64,512]{2,1,0:T(8,128)(2,1)S(1)}, bf16[4,64,512]{2,1,0...) custom-call(s32[3]{0:T(128)S(1)} %add_convert_fusion.role, ...), custom_call_target="tpu_custom_call", output_to_operand_aliasing={{0}: (3, {}), {1}: (4, {}), {2}: (5, {}), {3}: (6, {}), {4}... | custom-call | tf_op jit(solution)/shard_map/pallas_call | solution.py:102
  14.9 1.3 %collective-permute-start.1 = (bf16[4,64,512]{2,1,0:T(8,128)(2,1)S(1)}, bf16[4,64,512]{2,1,0:T(8,128)(2,1)S(1)}, u32[]{:S(2)}, u32[]{:S(2)}) collective-permute-start(bf16[4,64,512]{2,1,0:T(8,128)(2,1)S(1)} %get-tuple-element.36), channel_id=1, source_target_pairs={{0,128},{1,129},{2,130},{3,131},{4,132},{5,133},{6,134},{7,135},{8... | collective-permute-start | bytes 786440 | tf_op jit(solution)/shard_map/ppermute | solution.py:34
  16.2 1.3 %collective-permute-start.2 = (bf16[4,64,512]{2,1,0:T(8,128)(2,1)S(1)}, bf16[4,64,512]{2,1,0:T(8,128)(2,1)S(1)}, u32[]{:S(2)}, u32[]{:S(2)}) collective-permute-start(bf16[4,64,512]{2,1,0:T(8,128)(2,1)S(1)} %get-tuple-element.37), channel_id=1, source_target_pairs={{0,384},{1,385},{2,386},{3,387},{4,388},{5,389},{6,390},{7,391},{8... | collective-permute-start | bytes 786440 | tf_op jit(solution)/shard_map/ppermute | solution.py:34
  17.5 1.3 %collective-permute-start.3 = (bf16[4,64,512]{2,1,0:T(8,128)(2,1)S(1)}, bf16[4,64,512]{2,1,0:T(8,128)(2,1)S(1)}, u32[]{:S(2)}, u32[]{:S(2)}) collective-permute-start(bf16[4,64,512]{2,1,0:T(8,128)(2,1)S(1)} %get-tuple-element.38), channel_id=1, source_target_pairs={{0,256},{1,257},{2,258},{3,259},{4,260},{5,261},{6,262},{7,263},{8... | collective-permute-start | bytes 786440 | tf_op jit(solution)/shard_map/ppermute | solution.py:34
  18.8 1.3 %collective-permute-start.4 = (bf16[4,64,512]{2,1,0:T(8,128)(2,1)S(1)}, bf16[4,64,512]{2,1,0:T(8,128)(2,1)S(1)}, u32[]{:S(2)}, u32[]{:S(2)}) collective-permute-start(bf16[4,64,512]{2,1,0:T(8,128)(2,1)S(1)} %get-tuple-element.40), channel_id=1, source_target_pairs={{0,128},{1,129},{2,130},{3,131},{4,132},{5,133},{6,134},{7,135},{8... | collective-permute-start | bytes 786440 | tf_op jit(solution)/shard_map/ppermute | solution.py:34
  20.1 1.3 %collective-permute-start.5 = (bf16[4,64,512]{2,1,0:T(8,128)(2,1)S(1)}, bf16[4,64,512]{2,1,0:T(8,128)(2,1)S(1)}, u32[]{:S(2)}, u32[]{:S(2)}) collective-permute-start(bf16[4,64,512]{2,1,0:T(8,128)(2,1)S(1)} %get-tuple-element.41), channel_id=1, source_target_pairs={{0,384},{1,385},{2,386},{3,387},{4,388},{5,389},{6,390},{7,391},{8... | collective-permute-start | bytes 786440 | tf_op jit(solution)/shard_map/ppermute | solution.py:34
  21.4 1.3 %collective-permute-start.6 = (bf16[4,64,512]{2,1,0:T(8,128)(2,1)S(1)}, bf16[4,64,512]{2,1,0:T(8,128)(2,1)S(1)}, u32[]{:S(2)}, u32[]{:S(2)}) collective-permute-start(bf16[4,64,512]{2,1,0:T(8,128)(2,1)S(1)} %get-tuple-element.42), channel_id=1, source_target_pairs={{0,256},{1,257},{2,258},{3,259},{4,260},{5,261},{6,262},{7,263},{8... | collective-permute-start | bytes 786440 | tf_op jit(solution)/shard_map/ppermute | solution.py:34
  22.9 1.3 %collective-permute-start.7 = (bf16[4,64,512]{2,1,0:T(8,128)(2,1)S(1)}, bf16[4,64,512]{2,1,0:T(8,128)(2,1)S(1)}, u32[]{:S(2)}, u32[]{:S(2)}) collective-permute-start(bf16[4,64,512]{2,1,0:T(8,128)(2,1)S(1)} %add_select_fusion.1), channel_id=1, source_target_pairs={{0,64},{1,65},{2,66},{3,67},{4,68},{5,69},{6,70},{7,71},{8,72},{9,... | collective-permute-start | bytes 786440 | tf_op jit(solution)/shard_map/ppermute | solution.py:34
  25.1 2.8 %collective-permute-done.6 = bf16[4,64,512]{2,1,0:T(8,128)(2,1)S(1)} collective-permute-done((bf16[4,64,512]{2,1,0:T(8,128)(2,1)S(1)}, bf16[4,64,512]{2,1,0:T(8,128)(2,1)S(1)}, u32[]{:S(2)}, u32[]{:S(2)}) %collective-permute-start.6) | collective-permute-done | bytes 262176 | tf_op jit(solution)/shard_map/ppermute | solution.py:34
  27.9 1.3 %collective-permute-start.8 = (bf16[4,64,512]{2,1,0:T(8,128)(2,1)S(1)}, bf16[4,64,512]{2,1,0:T(8,128)(2,1)S(1)}, u32[]{:S(2)}, u32[]{:S(2)}) collective-permute-start(bf16[4,64,512]{2,1,0:T(8,128)(2,1)S(1)} %add_select_fusion), channel_id=1, source_target_pairs={{0,64},{1,65},{2,66},{3,67},{4,68},{5,69},{6,70},{7,71},{8,72},{9,... | collective-permute-start | bytes 786440 | tf_op jit(solution)/shard_map/ppermute | solution.py:34
  29.6 7.3 %collective-permute-done.8 = bf16[4,64,512]{2,1,0:T(8,128)(2,1)S(1)} collective-permute-done((bf16[4,64,512]{2,1,0:T(8,128)(2,1)S(1)}, bf16[4,64,512]{2,1,0:T(8,128)(2,1)S(1)}, u32[]{:S(2)}, u32[]{:S(2)}) %collective-permute-start.8) | collective-permute-done | bytes 262176 | tf_op jit(solution)/shard_map/ppermute | solution.py:34
  38.3 7.2 %collective-permute-start.10 = (bf16[4,64,512]{2,1,0:T(8,128)(2,1)S(1)}, bf16[4,64,512]{2,1,0:T(8,128)(2,1)S(1)}, u32[]{:S(2)}, u32[]{:S(2)}) collective-permute-start(bf16[4,64,512]{2,1,0:T(8,128)(2,1)S(1)} %get-tuple-element.46), channel_id=1, source_target_pairs={{0,32},{1,33},{2,34},{3,35},{4,36},{5,37},{6,38},{7,39},{8,40},{9,... | collective-permute-start | bytes 786440 | tf_op jit(solution)/shard_map/ppermute | solution.py:34
  45.6 7.4 %collective-permute-done.10 = bf16[4,64,512]{2,1,0:T(8,128)(2,1)S(1)} collective-permute-done((bf16[4,64,512]{2,1,0:T(8,128)(2,1)S(1)}, bf16[4,64,512]{2,1,0:T(8,128)(2,1)S(1)}, u32[]{:S(2)}, u32[]{:S(2)}) %collective-permute-start.10) | collective-permute-done | bytes 262176 | tf_op jit(solution)/shard_map/ppermute | solution.py:34
  53.2 5.3 %collective-permute-start.13 = (bf16[4,128,512]{2,1,0:T(8,128)(2,1)S(1)}, bf16[4,128,512]{2,1,0:T(8,128)(2,1)S(1)}, u32[]{:S(2)}, u32[]{:S(2)}) collective-permute-start(bf16[4,128,512]{2,1,0:T(8,128)(2,1)S(1)} %pad_maximum_fusion.refs_0_), channel_id=1, source_target_pairs={{0,256},{1,257},{2,258},{3,259},{4,260},{5,261},{6,262},{7,263},{8... | collective-permute-start | bytes 1572872 | tf_op jit(solution)/shard_map/ppermute | solution.py:34
  58.5 1.9 %collective-permute-start.12 = (bf16[4,128,512]{2,1,0:T(8,128)(2,1)S(1)}, bf16[4,128,512]{2,1,0:T(8,128)(2,1)S(1)}, u32[]{:S(2)}, u32[]{:S(2)}) collective-permute-start(bf16[4,128,512]{2,1,0:T(8,128)(2,1)S(1)} %pad_maximum_fusion.refs_0_), channel_id=1, source_target_pairs={{0,384},{1,385},{2,386},{3,387},{4,388},{5,389},{6,390},{7,391},{8... | collective-permute-start | bytes 1572872 | tf_op jit(solution)/shard_map/ppermute | solution.py:34
  60.5 3.4 %collective-permute-start.11 = (bf16[4,128,512]{2,1,0:T(8,128)(2,1)S(1)}, bf16[4,128,512]{2,1,0:T(8,128)(2,1)S(1)}, u32[]{:S(2)}, u32[]{:S(2)}) collective-permute-start(bf16[4,128,512]{2,1,0:T(8,128)(2,1)S(1)} %pad_maximum_fusion.refs_0_), channel_id=1, source_target_pairs={{0,128},{1,129},{2,130},{3,131},{4,132},{5,133},{6,134},{7,135},{8... | collective-permute-start | bytes 1572872 | tf_op jit(solution)/shard_map/ppermute | solution.py:34
  63.8 1.9 %collective-permute-start.14 = (bf16[4,128,512]{2,1,0:T(8,128)(2,1)S(1)}, bf16[4,128,512]{2,1,0:T(8,128)(2,1)S(1)}, u32[]{:S(2)}, u32[]{:S(2)}) collective-permute-start(bf16[4,128,512]{2,1,0:T(8,128)(2,1)S(1)} %pad_maximum_fusion.refs_0_), channel_id=1, source_target_pairs={{0,16},{1,17},{2,18},{3,19},{4,20},{5,21},{6,22},{7,23},{8,24},{9,... | collective-permute-start | bytes 1572872 | tf_op jit(solution)/shard_map/ppermute | solution.py:34
  65.8 2.4 %collective-permute-start.17 = (bf16[4,128,512]{2,1,0:T(8,128)(2,1)S(1)}, bf16[4,128,512]{2,1,0:T(8,128)(2,1)S(1)}, u32[]{:S(2)}, u32[]{:S(2)}) collective-permute-start(bf16[4,128,512]{2,1,0:T(8,128)(2,1)S(1)} %collective-permute-done.13.refs_3_), channel_id=1, source_target_pairs={{0,16},{1,17},{2,18},{3,19},{4,20},{5,21},{6,22},{7,23},{8,24},{9,... | collective-permute-start | bytes 1572872 | tf_op jit(solution)/shard_map/ppermute | solution.py:34
  68.4 1.9 %collective-permute-start.16 = (bf16[4,128,512]{2,1,0:T(8,128)(2,1)S(1)}, bf16[4,128,512]{2,1,0:T(8,128)(2,1)}, u32[]{:S(2)}, u32[]{:S(2)}) collective-permute-start(bf16[4,128,512]{2,1,0:T(8,128)(2,1)S(1)} %collective-permute-done.12.refs_2_), channel_id=1, source_target_pairs={{0,16},{1,17},{2,18},{3,19},{4,20},{5,21},{6,22},{7,23},{8,24},{9,... | collective-permute-start | bytes 1572872 | tf_op jit(solution)/shard_map/ppermute | solution.py:34
  71.6 1.9 %collective-permute-start.15 = (bf16[4,128,512]{2,1,0:T(8,128)(2,1)S(1)}, bf16[4,128,512]{2,1,0:T(8,128)(2,1)}, u32[]{:S(2)}, u32[]{:S(2)}) collective-permute-start(bf16[4,128,512]{2,1,0:T(8,128)(2,1)S(1)} %collective-permute-done.11.refs_1_), channel_id=1, source_target_pairs={{0,16},{1,17},{2,18},{3,19},{4,20},{5,21},{6,22},{7,23},{8,24},{9,... | collective-permute-start | bytes 1572872 | tf_op jit(solution)/shard_map/ppermute | solution.py:34
  73.7 1.8 %collective-permute-done.15.refs_5_ = bf16[4,128,512]{2,1,0:T(8,128)(2,1)} collective-permute-done((bf16[4,128,512]{2,1,0:T(8,128)(2,1)S(1)}, bf16[4,128,512]{2,1,0:T(8,128)(2,1)}, u32[]{:S(2)}, u32[]{:S(2)}) %collective-permute-start.15) | collective-permute-done | bytes 524320 | tf_op jit(solution)/shard_map/ppermute | solution.py:34
  75.5 4.5 %shard_map.19 = bf16[2,512,1024]{2,1,0:T(8,128)(2,1)} custom-call(s32[9]{0:T(128)S(1)} %stack.51.at, bf16[4,128,512]{2,1,0:T(8,128)(2,1)S(1)} %pad_maximum_fusion.refs_0_, bf16[4,128,512]{2,1,0:T(8,128)(2,1)S(1)} %collective-permute-done.11.refs_1_, bf16[4,128,512]{2,1,0:T(8,128)(2,1)S(1)} %collective-permute-done.12.refs_2_, ...), custom_call_target="tpu_custom_call" | custom-call | flops 2147483648 | bytes 4194304 | tf_op jit(solution)/shard_map/pallas_call | solution.py:158
  (24 shorter events, 6.5 us)
Async XLA Ops:
  0.1 1.6 %copy-start = (bf16[2,512,1024]{2,1,0:T(8,128)(2,1)S(1)}, bf16[2,512,1024]{2,1,0:T(8,128)(2,1)}, u32[]{:S(2)}) copy-start(bf16[2,512,1024]{2,1,0:T(8,128)(2,1)} %field.3) | copy-start | bytes 6291460
  2.4 10.8 %collective-permute-start = (bf16[2,512,512]{2,1,0:T(8,128)(2,1)S(1)}, bf16[2,512,512]{2,1,0:T(8,128)(2,1)S(1)}, u32[]{:S(2)}, u32[]{:S(2)}) collective-permute-start(bf16[2,512,512]{2,1,0:T(8,128)(2,1)S(1)} %get-tuple-element.26), channel_id=1, source_target_pairs={{0,16},{32,48},{64,80},{96,112},{128,144},{160,176},{192,208},{224... | collective-permute-start | bytes 3145736 | tf_op jit(solution)/shard_map/ppermute | solution.py:34
  14.9 6.6 %collective-permute-start.1 = (bf16[4,64,512]{2,1,0:T(8,128)(2,1)S(1)}, bf16[4,64,512]{2,1,0:T(8,128)(2,1)S(1)}, u32[]{:S(2)}, u32[]{:S(2)}) collective-permute-start(bf16[4,64,512]{2,1,0:T(8,128)(2,1)S(1)} %get-tuple-element.36), channel_id=1, source_target_pairs={{0,128},{1,129},{2,130},{3,131},{4,132},{5,133},{6,134},{7,135},{8... | collective-permute-start | bytes 786440 | tf_op jit(solution)/shard_map/ppermute | solution.py:34
  16.2 6.6 %collective-permute-start.2 = (bf16[4,64,512]{2,1,0:T(8,128)(2,1)S(1)}, bf16[4,64,512]{2,1,0:T(8,128)(2,1)S(1)}, u32[]{:S(2)}, u32[]{:S(2)}) collective-permute-start(bf16[4,64,512]{2,1,0:T(8,128)(2,1)S(1)} %get-tuple-element.37), channel_id=1, source_target_pairs={{0,384},{1,385},{2,386},{3,387},{4,388},{5,389},{6,390},{7,391},{8... | collective-permute-start | bytes 786440 | tf_op jit(solution)/shard_map/ppermute | solution.py:34
  17.5 5.3 %collective-permute-start.3 = (bf16[4,64,512]{2,1,0:T(8,128)(2,1)S(1)}, bf16[4,64,512]{2,1,0:T(8,128)(2,1)S(1)}, u32[]{:S(2)}, u32[]{:S(2)}) collective-permute-start(bf16[4,64,512]{2,1,0:T(8,128)(2,1)S(1)} %get-tuple-element.38), channel_id=1, source_target_pairs={{0,256},{1,257},{2,258},{3,259},{4,260},{5,261},{6,262},{7,263},{8... | collective-permute-start | bytes 786440 | tf_op jit(solution)/shard_map/ppermute | solution.py:34
  18.8 6.3 %collective-permute-start.4 = (bf16[4,64,512]{2,1,0:T(8,128)(2,1)S(1)}, bf16[4,64,512]{2,1,0:T(8,128)(2,1)S(1)}, u32[]{:S(2)}, u32[]{:S(2)}) collective-permute-start(bf16[4,64,512]{2,1,0:T(8,128)(2,1)S(1)} %get-tuple-element.40), channel_id=1, source_target_pairs={{0,128},{1,129},{2,130},{3,131},{4,132},{5,133},{6,134},{7,135},{8... | collective-permute-start | bytes 786440 | tf_op jit(solution)/shard_map/ppermute | solution.py:34
  20.1 5.0 %collective-permute-start.5 = (bf16[4,64,512]{2,1,0:T(8,128)(2,1)S(1)}, bf16[4,64,512]{2,1,0:T(8,128)(2,1)S(1)}, u32[]{:S(2)}, u32[]{:S(2)}) collective-permute-start(bf16[4,64,512]{2,1,0:T(8,128)(2,1)S(1)} %get-tuple-element.41), channel_id=1, source_target_pairs={{0,384},{1,385},{2,386},{3,387},{4,388},{5,389},{6,390},{7,391},{8... | collective-permute-start | bytes 786440 | tf_op jit(solution)/shard_map/ppermute | solution.py:34
  21.4 6.4 %collective-permute-start.6 = (bf16[4,64,512]{2,1,0:T(8,128)(2,1)S(1)}, bf16[4,64,512]{2,1,0:T(8,128)(2,1)S(1)}, u32[]{:S(2)}, u32[]{:S(2)}) collective-permute-start(bf16[4,64,512]{2,1,0:T(8,128)(2,1)S(1)} %get-tuple-element.42), channel_id=1, source_target_pairs={{0,256},{1,257},{2,258},{3,259},{4,260},{5,261},{6,262},{7,263},{8... | collective-permute-start | bytes 786440 | tf_op jit(solution)/shard_map/ppermute | solution.py:34
  22.9 6.8 %collective-permute-start.7 = (bf16[4,64,512]{2,1,0:T(8,128)(2,1)S(1)}, bf16[4,64,512]{2,1,0:T(8,128)(2,1)S(1)}, u32[]{:S(2)}, u32[]{:S(2)}) collective-permute-start(bf16[4,64,512]{2,1,0:T(8,128)(2,1)S(1)} %add_select_fusion.1), channel_id=1, source_target_pairs={{0,64},{1,65},{2,66},{3,67},{4,68},{5,69},{6,70},{7,71},{8,72},{9,... | collective-permute-start | bytes 786440 | tf_op jit(solution)/shard_map/ppermute | solution.py:34
  27.9 9.0 %collective-permute-start.8 = (bf16[4,64,512]{2,1,0:T(8,128)(2,1)S(1)}, bf16[4,64,512]{2,1,0:T(8,128)(2,1)S(1)}, u32[]{:S(2)}, u32[]{:S(2)}) collective-permute-start(bf16[4,64,512]{2,1,0:T(8,128)(2,1)S(1)} %add_select_fusion), channel_id=1, source_target_pairs={{0,64},{1,65},{2,66},{3,67},{4,68},{5,69},{6,70},{7,71},{8,72},{9,... | collective-permute-start | bytes 786440 | tf_op jit(solution)/shard_map/ppermute | solution.py:34
  37.0 8.6 %collective-permute-start.9 = (bf16[4,64,512]{2,1,0:T(8,128)(2,1)S(1)}, bf16[4,64,512]{2,1,0:T(8,128)(2,1)S(1)}, u32[]{:S(2)}, u32[]{:S(2)}) collective-permute-start(bf16[4,64,512]{2,1,0:T(8,128)(2,1)S(1)} %get-tuple-element.45), channel_id=1, source_target_pairs={{0,32},{1,33},{2,34},{3,35},{4,36},{5,37},{6,38},{7,39},{8,40},{9,... | collective-permute-start | bytes 786440 | tf_op jit(solution)/shard_map/ppermute | solution.py:34
  38.3 14.8 %collective-permute-start.10 = (bf16[4,64,512]{2,1,0:T(8,128)(2,1)S(1)}, bf16[4,64,512]{2,1,0:T(8,128)(2,1)S(1)}, u32[]{:S(2)}, u32[]{:S(2)}) collective-permute-start(bf16[4,64,512]{2,1,0:T(8,128)(2,1)S(1)} %get-tuple-element.46), channel_id=1, source_target_pairs={{0,32},{1,33},{2,34},{3,35},{4,36},{5,37},{6,38},{7,39},{8,40},{9,... | collective-permute-start | bytes 786440 | tf_op jit(solution)/shard_map/ppermute | solution.py:34
  53.2 12.6 %collective-permute-start.13 = (bf16[4,128,512]{2,1,0:T(8,128)(2,1)S(1)}, bf16[4,128,512]{2,1,0:T(8,128)(2,1)S(1)}, u32[]{:S(2)}, u32[]{:S(2)}) collective-permute-start(bf16[4,128,512]{2,1,0:T(8,128)(2,1)S(1)} %pad_maximum_fusion.refs_0_), channel_id=1, source_target_pairs={{0,256},{1,257},{2,258},{3,259},{4,260},{5,261},{6,262},{7,263},{8... | collective-permute-start | bytes 1572872 | tf_op jit(solution)/shard_map/ppermute | solution.py:34
  58.5 9.9 %collective-permute-start.12 = (bf16[4,128,512]{2,1,0:T(8,128)(2,1)S(1)}, bf16[4,128,512]{2,1,0:T(8,128)(2,1)S(1)}, u32[]{:S(2)}, u32[]{:S(2)}) collective-permute-start(bf16[4,128,512]{2,1,0:T(8,128)(2,1)S(1)} %pad_maximum_fusion.refs_0_), channel_id=1, source_target_pairs={{0,384},{1,385},{2,386},{3,387},{4,388},{5,389},{6,390},{7,391},{8... | collective-permute-start | bytes 1572872 | tf_op jit(solution)/shard_map/ppermute | solution.py:34
  60.5 11.1 %collective-permute-start.11 = (bf16[4,128,512]{2,1,0:T(8,128)(2,1)S(1)}, bf16[4,128,512]{2,1,0:T(8,128)(2,1)S(1)}, u32[]{:S(2)}, u32[]{:S(2)}) collective-permute-start(bf16[4,128,512]{2,1,0:T(8,128)(2,1)S(1)} %pad_maximum_fusion.refs_0_), channel_id=1, source_target_pairs={{0,128},{1,129},{2,130},{3,131},{4,132},{5,133},{6,134},{7,135},{8... | collective-permute-start | bytes 1572872 | tf_op jit(solution)/shard_map/ppermute | solution.py:34
  63.8 9.9 %collective-permute-start.14 = (bf16[4,128,512]{2,1,0:T(8,128)(2,1)S(1)}, bf16[4,128,512]{2,1,0:T(8,128)(2,1)S(1)}, u32[]{:S(2)}, u32[]{:S(2)}) collective-permute-start(bf16[4,128,512]{2,1,0:T(8,128)(2,1)S(1)} %pad_maximum_fusion.refs_0_), channel_id=1, source_target_pairs={{0,16},{1,17},{2,18},{3,19},{4,20},{5,21},{6,22},{7,23},{8,24},{9,... | collective-permute-start | bytes 1572872 | tf_op jit(solution)/shard_map/ppermute | solution.py:34
  65.8 8.0 %collective-permute-start.17 = (bf16[4,128,512]{2,1,0:T(8,128)(2,1)S(1)}, bf16[4,128,512]{2,1,0:T(8,128)(2,1)S(1)}, u32[]{:S(2)}, u32[]{:S(2)}) collective-permute-start(bf16[4,128,512]{2,1,0:T(8,128)(2,1)S(1)} %collective-permute-done.13.refs_3_), channel_id=1, source_target_pairs={{0,16},{1,17},{2,18},{3,19},{4,20},{5,21},{6,22},{7,23},{8,24},{9,... | collective-permute-start | bytes 1572872 | tf_op jit(solution)/shard_map/ppermute | solution.py:34
  68.4 5.3 %collective-permute-start.16 = (bf16[4,128,512]{2,1,0:T(8,128)(2,1)S(1)}, bf16[4,128,512]{2,1,0:T(8,128)(2,1)}, u32[]{:S(2)}, u32[]{:S(2)}) collective-permute-start(bf16[4,128,512]{2,1,0:T(8,128)(2,1)S(1)} %collective-permute-done.12.refs_2_), channel_id=1, source_target_pairs={{0,16},{1,17},{2,18},{3,19},{4,20},{5,21},{6,22},{7,23},{8,24},{9,... | collective-permute-start | bytes 1572872 | tf_op jit(solution)/shard_map/ppermute | solution.py:34
  71.6 3.9 %collective-permute-start.15 = (bf16[4,128,512]{2,1,0:T(8,128)(2,1)S(1)}, bf16[4,128,512]{2,1,0:T(8,128)(2,1)}, u32[]{:S(2)}, u32[]{:S(2)}) collective-permute-start(bf16[4,128,512]{2,1,0:T(8,128)(2,1)S(1)} %collective-permute-done.11.refs_1_), channel_id=1, source_target_pairs={{0,16},{1,17},{2,18},{3,19},{4,20},{5,21},{6,22},{7,23},{8,24},{9,... | collective-permute-start | bytes 1572872 | tf_op jit(solution)/shard_map/ppermute | solution.py:34

commit v5 on v4

--- a/solution.py
+++ b/solution.py
@@ -49,23 +49,27 @@
 
 
 def first_kernel(role, field, *refs):
-    panel, bits, sem = refs[0], refs[1:-1], refs[-1]
-    rows = bits[0].shape[1]
-    cols = bits[0].shape[2]
+    panel, upper, lower, sem = refs[0], refs[1:5], refs[5:9], refs[9]
+    rows, cols = upper[0].shape[1:]
+
+    def part(d, t):
+        return field.at[:, pl.ds(rows * d, rows), pl.ds(cols * t, cols)]
 
     @pl.when(role[0] == 1)
     def _():
         run([
-            pltpu.make_async_copy(
-                field.at[:, pl.ds(rows * i, rows), pl.ds(cols * t, cols)], bit.at[pl.ds(2 * t, 2)], sem.at[2 * i + t]
-            )
-            for i, bit in enumerate(bits)
-            for t in range(2)
+            pltpu.make_async_copy(part(d, t), bits[d], sem.at[2 * d + t])
+            for d in range(4)
+            for t, bits in ((1, upper), (0, lower))
         ])
 
     @pl.when(role[1] == 1)
     def _():
-        run([pltpu.make_async_copy(field.at[:, :, pl.ds(0, cols)], panel, sem.at[16])])
+        run([pltpu.make_async_copy(field.at[:, :, pl.ds(0, cols)], panel, sem.at[8])])
+
+    @pl.when(role[2] == 1)
+    def _():
+        run([pltpu.make_async_copy(part(d, 0), bit, sem.at[d]) for d, bit in enumerate(upper)])
 
 
 def first(role, field, shape):
@@ -75,39 +79,32 @@
         + [jax.ShapeDtypeStruct(shape, jnp.bfloat16)] * 8,
         in_specs=[SMEM, HBM],
         out_specs=[VMEM] * 9,
-        scratch_shapes=[pltpu.SemaphoreType.DMA((17,))],
+        scratch_shapes=[pltpu.SemaphoreType.DMA((9,))],
         compiler_params=pltpu.CompilerParams(vmem_limit_bytes=16 * 1024 * 1024),
     )(role, field)
 
 
-def second_kernel(role, field, came, *refs):
-    bits, sem = refs[8:-1], refs[-1]
-    rows = bits[0].shape[1]
-    cols = bits[0].shape[2]
+def second_kernel(role, came, *refs):
+    lower, sem = refs[4:8], refs[8]
+    rows = lower[0].shape[1]
 
     @pl.when(role[2] == 1)
     def _():
         run([
-            pltpu.make_async_copy(
-                came.at[:, pl.ds(rows * i, rows)] if t == 0 else field.at[:, pl.ds(rows * i, rows), pl.ds(0, cols)],
-                bit.at[pl.ds(2 * t, 2)],
-                sem.at[2 * i + t],
-            )
-            for i, bit in enumerate(bits)
-            for t in range(2)
+            pltpu.make_async_copy(came.at[:, pl.ds(rows * d, rows)], bit, sem.at[d]) for d, bit in enumerate(lower)
         ])
 
 
-def second(role, field, came, bits):
+def second(role, came, bits):
     return pl.pallas_call(
         second_kernel,
         out_shape=[jax.ShapeDtypeStruct(bit.shape, bit.dtype) for bit in bits],
-        in_specs=[SMEM, HBM] + [VMEM] * 9,
-        out_specs=[VMEM] * 8,
-        input_output_aliases={3 + i: i for i in range(8)},
-        scratch_shapes=[pltpu.SemaphoreType.DMA((16,))],
+        in_specs=[SMEM] + [VMEM] * 5,
+        out_specs=[VMEM] * 4,
+        input_output_aliases={2 + i: i for i in range(4)},
+        scratch_shapes=[pltpu.SemaphoreType.DMA((4,))],
         compiler_params=pltpu.CompilerParams(vmem_limit_bytes=16 * 1024 * 1024),
-    )(role, field, came, *bits)
+    )(role, came, *bits)
 
 
 def product_kernel(at, *refs):
@@ -178,9 +175,10 @@
 
     left_root = (y == 0) & (h == 0)
     role = jnp.stack([(c == 0) & (x == 0) & (l == 0), left_root & (c == 0), left_root & (c == 1)]).astype(jnp.int32)
-    panel, *bits = first(role, field, (4, part // 2, WIDTH))
+    panel, *bits = first(role, field, (2, part, WIDTH))
+    upper, lower = bits[:4], bits[4:]
     came = send(panel, lambda x, l, c, y, h: (x, l, 1, y, h) if c == 0 and y == 0 and h == 0 else None)
-    bits = second(role, field, came, bits)
+    lower = second(role, came, lower)
 
     def scatter(d):
         def rule(x, l, c, y, h):
@@ -191,8 +189,8 @@
 
     at_root = jnp.where(c == 0, x, y) == 0
     a, e = (
-        jnp.where(at_root, bits[t], sum(send(bits[2 * d + t], scatter(d)) for d in (1, 3, 2)))
-        for t in range(2)
+        jnp.where(at_root, bits[0], sum(send(bits[d], scatter(d)) for d in (1, 3, 2)))
+        for bits in (upper, lower)
     )
 
 
@@ -219,7 +217,7 @@
     gup, gdown = send(up, onwards(1, (0, 1))), send(down, onwards(-1, (0, 3)))
     a_from = jnp.where(c == 0, pick(l, (0, 2, 1, 2)), pick(h, (0, 1, 2, 3)))
     e_from = jnp.where(c == 0, pick(l, (0, 3, 1, 3)), pick(h, (0, 2, 3, 1)))
-    unit = jnp.concatenate([pick(a_from, (a, za, gup, gdown)), pick(e_from, (e, ze, gup, gdown))], 1)
+    unit = jnp.concatenate([pick(e_from, (e, ze, gup, gdown)), pick(a_from, (a, za, gup, gdown))], 0)
 
     def gather(d):
         return lambda x, l, c, y, h: (x + d, l, c, y, h) if c == 0 else (x, l, c, y + d, h)

time: 80.5 us -> 78.6 us (0.976)
  waiting for transfers between devices: 31.6 us -> 26.2 us
  starting transfers between devices: 39 us -> 42.8 us
  Pallas kernels: 6.87 us -> 5.84 us
    ppermute x18, waiting for transfers between devices: 31.6 us -> 26.2 us  [send(): return lax.ppermute(value, AXES, moves(rule))]
    ppermute x18, starting transfers between devices: 39 us -> 42.8 us  [send(): return lax.ppermute(value, AXES, moves(rule))]
    pallas_call x1, Pallas kernels: 1.71 us -> 0.66 us  [second(): pl.pallas_call(second_kernel, out_shape=[jax.ShapeDtypeStruct(bit.shape,...]
  transfers between devices with their start and end apart: 18 -> 18, of which waited for: 9 -> 8; matrix products, arithmetic and copies ran while one was open for 0% -> 0% of each run, Pallas kernels for 0% -> 1%
where the time goes in v5:
time: 78.6 us; the launch traced here: 77.4 us
  starting transfers between devices  42.8 us (54%)
  waiting for transfers between devices  26.2 us (33%)
  Pallas kernels  5.84 us (7%)
  local copies, waits for them, and re-layouts  1.68 us (2%)
    ppermute x18, starting transfers between devices, send(): return lax.ppermute(value, AXES, moves(rule))  42.8 us
    ppermute x18, waiting for transfers between devices, send(): return lax.ppermute(value, AXES, moves(rule))  26.2 us
    pallas_call x1, Pallas kernels, product(): pl.pallas_call(product_kernel, out_shape=jax.ShapeDtypeStruct(shape, jnp....  4.45 us
    unnamed x2, local copies, waits for them, and re-layouts  1.59 us
  transfers between devices with their start and end apart: 18, of which 8 were waited for; matrix products, arithmetic and copies ran while one was open for 0% of the time, Pallas kernels for 1%

profile of v5, /device:TPU:1, one launch (start us, length us, event | category | flops | bytes accessed | tf_op | source)
XLA Modules:
  0.0 77.4 jit_solution(12139386170434137622)
XLA Ops:
  0.1 1.6 %copy-done = bf16[2,512,1024]{2,1,0:T(8,128)(2,1)S(1)} copy-done((bf16[2,512,1024]{2,1,0:T(8,128)(2,1)S(1)}, bf16[2,512,1024]{2,1,0:T(8,128)(2,1)}, u32[]{:S(2)}) %copy-start) | copy-done | bytes 2097176
  3.7 3.4 %collective-permute-start = (bf16[2,128,512]{2,1,0:T(8,128)(2,1)S(1)}, bf16[2,128,512]{2,1,0:T(8,128)(2,1)S(1)}, u32[]{:S(2)}, u32[]{:S(2)}) collective-permute-start(bf16[2,128,512]{2,1,0:T(8,128)(2,1)S(1)} %get-tuple-element.23), channel_id=1, source_target_pairs={{0,128},{1,129},{2,130},{3,131},{4,132},{5,133},{6,134},{7,135},{8... | collective-permute-start | bytes 786440 | tf_op jit(solution)/shard_map/ppermute | solution.py:34
  7.1 2.1 %collective-permute-start.1 = (bf16[2,128,512]{2,1,0:T(8,128)(2,1)S(1)}, bf16[2,128,512]{2,1,0:T(8,128)(2,1)S(1)}, u32[]{:S(2)}, u32[]{:S(2)}) collective-permute-start(bf16[2,128,512]{2,1,0:T(8,128)(2,1)S(1)} %get-tuple-element.24), channel_id=1, source_target_pairs={{0,384},{1,385},{2,386},{3,387},{4,388},{5,389},{6,390},{7,391},{8... | collective-permute-start | bytes 786440 | tf_op jit(solution)/shard_map/ppermute | solution.py:34
  9.2 1.3 %collective-permute-start.2 = (bf16[2,128,512]{2,1,0:T(8,128)(2,1)S(1)}, bf16[2,128,512]{2,1,0:T(8,128)(2,1)S(1)}, u32[]{:S(2)}, u32[]{:S(2)}) collective-permute-start(bf16[2,128,512]{2,1,0:T(8,128)(2,1)S(1)} %get-tuple-element.25), channel_id=1, source_target_pairs={{0,256},{1,257},{2,258},{3,259},{4,260},{5,261},{6,262},{7,263},{8... | collective-permute-start | bytes 786440 | tf_op jit(solution)/shard_map/ppermute | solution.py:34
  10.5 2.4 %collective-permute-done.3.came = bf16[2,512,512]{2,1,0:T(8,128)(2,1)S(1)} collective-permute-done((bf16[2,512,512]{2,1,0:T(8,128)(2,1)S(1)}, bf16[2,512,512]{2,1,0:T(8,128)(2,1)S(1)}, u32[]{:S(2)}, u32[]{:S(2)}) %collective-permute-start.3) | collective-permute-done | bytes 1048608 | tf_op jit(solution)/shard_map/ppermute | solution.py:34
  13.6 1.3 %collective-permute-start.4 = (bf16[2,128,512]{2,1,0:T(8,128)(2,1)S(1)}, bf16[2,128,512]{2,1,0:T(8,128)(2,1)S(1)}, u32[]{:S(2)}, u32[]{:S(2)}) collective-permute-start(bf16[2,128,512]{2,1,0:T(8,128)(2,1)S(1)} %get-tuple-element.32), channel_id=1, source_target_pairs={{0,128},{1,129},{2,130},{3,131},{4,132},{5,133},{6,134},{7,135},{8... | collective-permute-start | bytes 786440 | tf_op jit(solution)/shard_map/ppermute | solution.py:34
  14.9 1.3 %collective-permute-start.5 = (bf16[2,128,512]{2,1,0:T(8,128)(2,1)S(1)}, bf16[2,128,512]{2,1,0:T(8,128)(2,1)S(1)}, u32[]{:S(2)}, u32[]{:S(2)}) collective-permute-start(bf16[2,128,512]{2,1,0:T(8,128)(2,1)S(1)} %get-tuple-element.33), channel_id=1, source_target_pairs={{0,384},{1,385},{2,386},{3,387},{4,388},{5,389},{6,390},{7,391},{8... | collective-permute-start | bytes 786440 | tf_op jit(solution)/shard_map/ppermute | solution.py:34
  16.2 1.3 %collective-permute-start.6 = (bf16[2,128,512]{2,1,0:T(8,128)(2,1)S(1)}, bf16[2,128,512]{2,1,0:T(8,128)(2,1)S(1)}, u32[]{:S(2)}, u32[]{:S(2)}) collective-permute-start(bf16[2,128,512]{2,1,0:T(8,128)(2,1)S(1)} %get-tuple-element.34), channel_id=1, source_target_pairs={{0,256},{1,257},{2,258},{3,259},{4,260},{5,261},{6,262},{7,263},{8... | collective-permute-start | bytes 786440 | tf_op jit(solution)/shard_map/ppermute | solution.py:34
  17.6 1.3 %collective-permute-start.7 = (bf16[2,128,512]{2,1,0:T(8,128)(2,1)S(1)}, bf16[2,128,512]{2,1,0:T(8,128)(2,1)S(1)}, u32[]{:S(2)}, u32[]{:S(2)}) collective-permute-start(bf16[2,128,512]{2,1,0:T(8,128)(2,1)S(1)} %add_select_fusion.1), channel_id=1, source_target_pairs={{0,64},{1,65},{2,66},{3,67},{4,68},{5,69},{6,70},{7,71},{8,72},{9,... | collective-permute-start | bytes 786440 | tf_op jit(solution)/shard_map/ppermute | solution.py:34
  19.5 1.5 %collective-permute-done.6 = bf16[2,128,512]{2,1,0:T(8,128)(2,1)S(1)} collective-permute-done((bf16[2,128,512]{2,1,0:T(8,128)(2,1)S(1)}, bf16[2,128,512]{2,1,0:T(8,128)(2,1)S(1)}, u32[]{:S(2)}, u32[]{:S(2)}) %collective-permute-start.6) | collective-permute-done | bytes 262176 | tf_op jit(solution)/shard_map/ppermute | solution.py:34
  23.1 11.0 %collective-permute-done.8 = bf16[2,128,512]{2,1,0:T(8,128)(2,1)S(1)} collective-permute-done((bf16[2,128,512]{2,1,0:T(8,128)(2,1)S(1)}, bf16[2,128,512]{2,1,0:T(8,128)(2,1)S(1)}, u32[]{:S(2)}, u32[]{:S(2)}) %collective-permute-start.8) | collective-permute-done | bytes 262176 | tf_op jit(solution)/shard_map/ppermute | solution.py:34
  34.1 1.3 %collective-permute-start.9 = (bf16[2,128,512]{2,1,0:T(8,128)(2,1)S(1)}, bf16[2,128,512]{2,1,0:T(8,128)(2,1)S(1)}, u32[]{:S(2)}, u32[]{:S(2)}) collective-permute-start(bf16[2,128,512]{2,1,0:T(8,128)(2,1)S(1)} %get-tuple-element.37), channel_id=1, source_target_pairs={{0,32},{1,33},{2,34},{3,35},{4,36},{5,37},{6,38},{7,39},{8,40},{9,... | collective-permute-start | bytes 786440 | tf_op jit(solution)/shard_map/ppermute | solution.py:34
  35.4 7.3 %collective-permute-start.10 = (bf16[2,128,512]{2,1,0:T(8,128)(2,1)S(1)}, bf16[2,128,512]{2,1,0:T(8,128)(2,1)S(1)}, u32[]{:S(2)}, u32[]{:S(2)}) collective-permute-start(bf16[2,128,512]{2,1,0:T(8,128)(2,1)S(1)} %get-tuple-element.38), channel_id=1, source_target_pairs={{0,32},{1,33},{2,34},{3,35},{4,36},{5,37},{6,38},{7,39},{8,40},{9,... | collective-permute-start | bytes 786440 | tf_op jit(solution)/shard_map/ppermute | solution.py:34
  42.8 7.2 %collective-permute-done.10 = bf16[2,128,512]{2,1,0:T(8,128)(2,1)S(1)} collective-permute-done((bf16[2,128,512]{2,1,0:T(8,128)(2,1)S(1)}, bf16[2,128,512]{2,1,0:T(8,128)(2,1)S(1)}, u32[]{:S(2)}, u32[]{:S(2)}) %collective-permute-start.10) | collective-permute-done | bytes 262176 | tf_op jit(solution)/shard_map/ppermute | solution.py:34
  50.1 5.7 %collective-permute-start.13 = (bf16[4,128,512]{2,1,0:T(8,128)(2,1)S(1)}, bf16[4,128,512]{2,1,0:T(8,128)(2,1)S(1)}, u32[]{:S(2)}, u32[]{:S(2)}) collective-permute-start(bf16[4,128,512]{2,1,0:T(8,128)(2,1)S(1)} %pad_maximum_fusion.refs_0_), channel_id=1, source_target_pairs={{0,256},{1,257},{2,258},{3,259},{4,260},{5,261},{6,262},{7,263},{8... | collective-permute-start | bytes 1572872 | tf_op jit(solution)/shard_map/ppermute | solution.py:34
  55.8 1.9 %collective-permute-start.12 = (bf16[4,128,512]{2,1,0:T(8,128)(2,1)S(1)}, bf16[4,128,512]{2,1,0:T(8,128)(2,1)S(1)}, u32[]{:S(2)}, u32[]{:S(2)}) collective-permute-start(bf16[4,128,512]{2,1,0:T(8,128)(2,1)S(1)} %pad_maximum_fusion.refs_0_), channel_id=1, source_target_pairs={{0,384},{1,385},{2,386},{3,387},{4,388},{5,389},{6,390},{7,391},{8... | collective-permute-start | bytes 1572872 | tf_op jit(solution)/shard_map/ppermute | solution.py:34
  57.7 3.4 %collective-permute-start.11 = (bf16[4,128,512]{2,1,0:T(8,128)(2,1)S(1)}, bf16[4,128,512]{2,1,0:T(8,128)(2,1)S(1)}, u32[]{:S(2)}, u32[]{:S(2)}) collective-permute-start(bf16[4,128,512]{2,1,0:T(8,128)(2,1)S(1)} %pad_maximum_fusion.refs_0_), channel_id=1, source_target_pairs={{0,128},{1,129},{2,130},{3,131},{4,132},{5,133},{6,134},{7,135},{8... | collective-permute-start | bytes 1572872 | tf_op jit(solution)/shard_map/ppermute | solution.py:34
  61.1 1.9 %collective-permute-start.14 = (bf16[4,128,512]{2,1,0:T(8,128)(2,1)S(1)}, bf16[4,128,512]{2,1,0:T(8,128)(2,1)S(1)}, u32[]{:S(2)}, u32[]{:S(2)}) collective-permute-start(bf16[4,128,512]{2,1,0:T(8,128)(2,1)S(1)} %pad_maximum_fusion.refs_0_), channel_id=1, source_target_pairs={{0,16},{1,17},{2,18},{3,19},{4,20},{5,21},{6,22},{7,23},{8,24},{9,... | collective-permute-start | bytes 1572872 | tf_op jit(solution)/shard_map/ppermute | solution.py:34
  63.0 2.4 %collective-permute-start.17 = (bf16[4,128,512]{2,1,0:T(8,128)(2,1)S(1)}, bf16[4,128,512]{2,1,0:T(8,128)(2,1)S(1)}, u32[]{:S(2)}, u32[]{:S(2)}) collective-permute-start(bf16[4,128,512]{2,1,0:T(8,128)(2,1)S(1)} %collective-permute-done.13.refs_3_), channel_id=1, source_target_pairs={{0,16},{1,17},{2,18},{3,19},{4,20},{5,21},{6,22},{7,23},{8,24},{9,... | collective-permute-start | bytes 1572872 | tf_op jit(solution)/shard_map/ppermute | solution.py:34
  65.4 1.5 %collective-permute-done.12.refs_2_ = bf16[4,128,512]{2,1,0:T(8,128)(2,1)S(1)} collective-permute-done((bf16[4,128,512]{2,1,0:T(8,128)(2,1)S(1)}, bf16[4,128,512]{2,1,0:T(8,128)(2,1)S(1)}, u32[]{:S(2)}, u32[]{:S(2)}) %collective-permute-start.12) | collective-permute-done | bytes 524320 | tf_op jit(solution)/shard_map/ppermute | solution.py:34
  66.9 1.9 %collective-permute-start.16 = (bf16[4,128,512]{2,1,0:T(8,128)(2,1)S(1)}, bf16[4,128,512]{2,1,0:T(8,128)(2,1)}, u32[]{:S(2)}, u32[]{:S(2)}) collective-permute-start(bf16[4,128,512]{2,1,0:T(8,128)(2,1)S(1)} %collective-permute-done.12.refs_2_), channel_id=1, source_target_pairs={{0,16},{1,17},{2,18},{3,19},{4,20},{5,21},{6,22},{7,23},{8,24},{9,... | collective-permute-start | bytes 1572872 | tf_op jit(solution)/shard_map/ppermute | solution.py:34
  68.8 2.4 %collective-permute-start.15 = (bf16[4,128,512]{2,1,0:T(8,128)(2,1)S(1)}, bf16[4,128,512]{2,1,0:T(8,128)(2,1)}, u32[]{:S(2)}, u32[]{:S(2)}) collective-permute-start(bf16[4,128,512]{2,1,0:T(8,128)(2,1)S(1)} %collective-permute-done.11.refs_1_), channel_id=1, source_target_pairs={{0,16},{1,17},{2,18},{3,19},{4,20},{5,21},{6,22},{7,23},{8,24},{9,... | collective-permute-start | bytes 1572872 | tf_op jit(solution)/shard_map/ppermute | solution.py:34
  71.5 1.4 %collective-permute-done.15.refs_5_ = bf16[4,128,512]{2,1,0:T(8,128)(2,1)} collective-permute-done((bf16[4,128,512]{2,1,0:T(8,128)(2,1)S(1)}, bf16[4,128,512]{2,1,0:T(8,128)(2,1)}, u32[]{:S(2)}, u32[]{:S(2)}) %collective-permute-start.15) | collective-permute-done | bytes 524320 | tf_op jit(solution)/shard_map/ppermute | solution.py:34
  72.9 4.5 %shard_map.19 = bf16[2,512,1024]{2,1,0:T(8,128)(2,1)} custom-call(s32[9]{0:T(128)S(1)} %stack.51.at, bf16[4,128,512]{2,1,0:T(8,128)(2,1)S(1)} %pad_maximum_fusion.refs_0_, bf16[4,128,512]{2,1,0:T(8,128)(2,1)S(1)} %collective-permute-done.11.refs_1_, bf16[4,128,512]{2,1,0:T(8,128)(2,1)S(1)} %collective-permute-done.12.refs_2_, ...), custom_call_target="tpu_custom_call" | custom-call | flops 2147483648 | bytes 4194304 | tf_op jit(solution)/shard_map/pallas_call | solution.py:155
  (24 shorter events, 5.7 us)
Async XLA Ops:
  0.1 1.6 %copy-start = (bf16[2,512,1024]{2,1,0:T(8,128)(2,1)S(1)}, bf16[2,512,1024]{2,1,0:T(8,128)(2,1)}, u32[]{:S(2)}) copy-start(bf16[2,512,1024]{2,1,0:T(8,128)(2,1)} %field.1) | copy-start | bytes 6291460
  2.4 10.5 %collective-permute-start.3 = (bf16[2,512,512]{2,1,0:T(8,128)(2,1)S(1)}, bf16[2,512,512]{2,1,0:T(8,128)(2,1)S(1)}, u32[]{:S(2)}, u32[]{:S(2)}) collective-permute-start(bf16[2,512,512]{2,1,0:T(8,128)(2,1)S(1)} %get-tuple-element.26), channel_id=1, source_target_pairs={{0,16},{32,48},{64,80},{96,112},{128,144},{160,176},{192,208},{224... | collective-permute-start | bytes 3145736 | tf_op jit(solution)/shard_map/ppermute | solution.py:34
  3.7 12.5 %collective-permute-start = (bf16[2,128,512]{2,1,0:T(8,128)(2,1)S(1)}, bf16[2,128,512]{2,1,0:T(8,128)(2,1)S(1)}, u32[]{:S(2)}, u32[]{:S(2)}) collective-permute-start(bf16[2,128,512]{2,1,0:T(8,128)(2,1)S(1)} %get-tuple-element.23), channel_id=1, source_target_pairs={{0,128},{1,129},{2,130},{3,131},{4,132},{5,133},{6,134},{7,135},{8... | collective-permute-start | bytes 786440 | tf_op jit(solution)/shard_map/ppermute | solution.py:34
  7.1 10.4 %collective-permute-start.1 = (bf16[2,128,512]{2,1,0:T(8,128)(2,1)S(1)}, bf16[2,128,512]{2,1,0:T(8,128)(2,1)S(1)}, u32[]{:S(2)}, u32[]{:S(2)}) collective-permute-start(bf16[2,128,512]{2,1,0:T(8,128)(2,1)S(1)} %get-tuple-element.24), channel_id=1, source_target_pairs={{0,384},{1,385},{2,386},{3,387},{4,388},{5,389},{6,390},{7,391},{8... | collective-permute-start | bytes 786440 | tf_op jit(solution)/shard_map/ppermute | solution.py:34
  9.2 8.3 %collective-permute-start.2 = (bf16[2,128,512]{2,1,0:T(8,128)(2,1)S(1)}, bf16[2,128,512]{2,1,0:T(8,128)(2,1)S(1)}, u32[]{:S(2)}, u32[]{:S(2)}) collective-permute-start(bf16[2,128,512]{2,1,0:T(8,128)(2,1)S(1)} %get-tuple-element.25), channel_id=1, source_target_pairs={{0,256},{1,257},{2,258},{3,259},{4,260},{5,261},{6,262},{7,263},{8... | collective-permute-start | bytes 786440 | tf_op jit(solution)/shard_map/ppermute | solution.py:34
  13.6 5.4 %collective-permute-start.4 = (bf16[2,128,512]{2,1,0:T(8,128)(2,1)S(1)}, bf16[2,128,512]{2,1,0:T(8,128)(2,1)S(1)}, u32[]{:S(2)}, u32[]{:S(2)}) collective-permute-start(bf16[2,128,512]{2,1,0:T(8,128)(2,1)S(1)} %get-tuple-element.32), channel_id=1, source_target_pairs={{0,128},{1,129},{2,130},{3,131},{4,132},{5,133},{6,134},{7,135},{8... | collective-permute-start | bytes 786440 | tf_op jit(solution)/shard_map/ppermute | solution.py:34
  14.9 4.6 %collective-permute-start.5 = (bf16[2,128,512]{2,1,0:T(8,128)(2,1)S(1)}, bf16[2,128,512]{2,1,0:T(8,128)(2,1)S(1)}, u32[]{:S(2)}, u32[]{:S(2)}) collective-permute-start(bf16[2,128,512]{2,1,0:T(8,128)(2,1)S(1)} %get-tuple-element.33), channel_id=1, source_target_pairs={{0,384},{1,385},{2,386},{3,387},{4,388},{5,389},{6,390},{7,391},{8... | collective-permute-start | bytes 786440 | tf_op jit(solution)/shard_map/ppermute | solution.py:34
  16.2 4.8 %collective-permute-start.6 = (bf16[2,128,512]{2,1,0:T(8,128)(2,1)S(1)}, bf16[2,128,512]{2,1,0:T(8,128)(2,1)S(1)}, u32[]{:S(2)}, u32[]{:S(2)}) collective-permute-start(bf16[2,128,512]{2,1,0:T(8,128)(2,1)S(1)} %get-tuple-element.34), channel_id=1, source_target_pairs={{0,256},{1,257},{2,258},{3,259},{4,260},{5,261},{6,262},{7,263},{8... | collective-permute-start | bytes 786440 | tf_op jit(solution)/shard_map/ppermute | solution.py:34
  17.6 5.5 %collective-permute-start.7 = (bf16[2,128,512]{2,1,0:T(8,128)(2,1)S(1)}, bf16[2,128,512]{2,1,0:T(8,128)(2,1)S(1)}, u32[]{:S(2)}, u32[]{:S(2)}) collective-permute-start(bf16[2,128,512]{2,1,0:T(8,128)(2,1)S(1)} %add_select_fusion.1), channel_id=1, source_target_pairs={{0,64},{1,65},{2,66},{3,67},{4,68},{5,69},{6,70},{7,71},{8,72},{9,... | collective-permute-start | bytes 786440 | tf_op jit(solution)/shard_map/ppermute | solution.py:34
  21.1 13.0 %collective-permute-start.8 = (bf16[2,128,512]{2,1,0:T(8,128)(2,1)S(1)}, bf16[2,128,512]{2,1,0:T(8,128)(2,1)S(1)}, u32[]{:S(2)}, u32[]{:S(2)}) collective-permute-start(bf16[2,128,512]{2,1,0:T(8,128)(2,1)S(1)} %add_select_fusion), channel_id=1, source_target_pairs={{0,64},{1,65},{2,66},{3,67},{4,68},{5,69},{6,70},{7,71},{8,72},{9,... | collective-permute-start | bytes 786440 | tf_op jit(solution)/shard_map/ppermute | solution.py:34
  34.1 8.6 %collective-permute-start.9 = (bf16[2,128,512]{2,1,0:T(8,128)(2,1)S(1)}, bf16[2,128,512]{2,1,0:T(8,128)(2,1)S(1)}, u32[]{:S(2)}, u32[]{:S(2)}) collective-permute-start(bf16[2,128,512]{2,1,0:T(8,128)(2,1)S(1)} %get-tuple-element.37), channel_id=1, source_target_pairs={{0,32},{1,33},{2,34},{3,35},{4,36},{5,37},{6,38},{7,39},{8,40},{9,... | collective-permute-start | bytes 786440 | tf_op jit(solution)/shard_map/ppermute | solution.py:34
  35.4 14.5 %collective-permute-start.10 = (bf16[2,128,512]{2,1,0:T(8,128)(2,1)S(1)}, bf16[2,128,512]{2,1,0:T(8,128)(2,1)S(1)}, u32[]{:S(2)}, u32[]{:S(2)}) collective-permute-start(bf16[2,128,512]{2,1,0:T(8,128)(2,1)S(1)} %get-tuple-element.38), channel_id=1, source_target_pairs={{0,32},{1,33},{2,34},{3,35},{4,36},{5,37},{6,38},{7,39},{8,40},{9,... | collective-permute-start | bytes 786440 | tf_op jit(solution)/shard_map/ppermute | solution.py:34
  50.1 12.9 %collective-permute-start.13 = (bf16[4,128,512]{2,1,0:T(8,128)(2,1)S(1)}, bf16[4,128,512]{2,1,0:T(8,128)(2,1)S(1)}, u32[]{:S(2)}, u32[]{:S(2)}) collective-permute-start(bf16[4,128,512]{2,1,0:T(8,128)(2,1)S(1)} %pad_maximum_fusion.refs_0_), channel_id=1, source_target_pairs={{0,256},{1,257},{2,258},{3,259},{4,260},{5,261},{6,262},{7,263},{8... | collective-permute-start | bytes 1572872 | tf_op jit(solution)/shard_map/ppermute | solution.py:34
  55.8 11.2 %collective-permute-start.12 = (bf16[4,128,512]{2,1,0:T(8,128)(2,1)S(1)}, bf16[4,128,512]{2,1,0:T(8,128)(2,1)S(1)}, u32[]{:S(2)}, u32[]{:S(2)}) collective-permute-start(bf16[4,128,512]{2,1,0:T(8,128)(2,1)S(1)} %pad_maximum_fusion.refs_0_), channel_id=1, source_target_pairs={{0,384},{1,385},{2,386},{3,387},{4,388},{5,389},{6,390},{7,391},{8... | collective-permute-start | bytes 1572872 | tf_op jit(solution)/shard_map/ppermute | solution.py:34
  57.7 11.1 %collective-permute-start.11 = (bf16[4,128,512]{2,1,0:T(8,128)(2,1)S(1)}, bf16[4,128,512]{2,1,0:T(8,128)(2,1)S(1)}, u32[]{:S(2)}, u32[]{:S(2)}) collective-permute-start(bf16[4,128,512]{2,1,0:T(8,128)(2,1)S(1)} %pad_maximum_fusion.refs_0_), channel_id=1, source_target_pairs={{0,128},{1,129},{2,130},{3,131},{4,132},{5,133},{6,134},{7,135},{8... | collective-permute-start | bytes 1572872 | tf_op jit(solution)/shard_map/ppermute | solution.py:34
  61.1 10.4 %collective-permute-start.14 = (bf16[4,128,512]{2,1,0:T(8,128)(2,1)S(1)}, bf16[4,128,512]{2,1,0:T(8,128)(2,1)S(1)}, u32[]{:S(2)}, u32[]{:S(2)}) collective-permute-start(bf16[4,128,512]{2,1,0:T(8,128)(2,1)S(1)} %pad_maximum_fusion.refs_0_), channel_id=1, source_target_pairs={{0,16},{1,17},{2,18},{3,19},{4,20},{5,21},{6,22},{7,23},{8,24},{9,... | collective-permute-start | bytes 1572872 | tf_op jit(solution)/shard_map/ppermute | solution.py:34
  63.0 8.5 %collective-permute-start.17 = (bf16[4,128,512]{2,1,0:T(8,128)(2,1)S(1)}, bf16[4,128,512]{2,1,0:T(8,128)(2,1)S(1)}, u32[]{:S(2)}, u32[]{:S(2)}) collective-permute-start(bf16[4,128,512]{2,1,0:T(8,128)(2,1)S(1)} %collective-permute-done.13.refs_3_), channel_id=1, source_target_pairs={{0,16},{1,17},{2,18},{3,19},{4,20},{5,21},{6,22},{7,23},{8,24},{9,... | collective-permute-start | bytes 1572872 | tf_op jit(solution)/shard_map/ppermute | solution.py:34
  66.9 4.6 %collective-permute-start.16 = (bf16[4,128,512]{2,1,0:T(8,128)(2,1)S(1)}, bf16[4,128,512]{2,1,0:T(8,128)(2,1)}, u32[]{:S(2)}, u32[]{:S(2)}) collective-permute-start(bf16[4,128,512]{2,1,0:T(8,128)(2,1)S(1)} %collective-permute-done.12.refs_2_), channel_id=1, source_target_pairs={{0,16},{1,17},{2,18},{3,19},{4,20},{5,21},{6,22},{7,23},{8,24},{9,... | collective-permute-start | bytes 1572872 | tf_op jit(solution)/shard_map/ppermute | solution.py:34
  68.8 4.1 %collective-permute-start.15 = (bf16[4,128,512]{2,1,0:T(8,128)(2,1)S(1)}, bf16[4,128,512]{2,1,0:T(8,128)(2,1)}, u32[]{:S(2)}, u32[]{:S(2)}) collective-permute-start(bf16[4,128,512]{2,1,0:T(8,128)(2,1)S(1)} %collective-permute-done.11.refs_1_), channel_id=1, source_target_pairs={{0,16},{1,17},{2,18},{3,19},{4,20},{5,21},{6,22},{7,23},{8,24},{9,... | collective-permute-start | bytes 1572872 | tf_op jit(solution)/shard_map/ppermute | solution.py:34

commit v6 on v5

--- a/solution.py
+++ b/solution.py
@@ -114,18 +114,16 @@
     dot = lambda a, b: jnp.dot(a, b, preferred_element_type=jnp.float32)
 
     def work(lefts, rights, first):
+        copies = []
         for i, left in enumerate(lefts):
+            here = pl.ds(rows * i, rows)
             for j in range(4):
                 k = pl.ds(pl.multiple_of(at[5 + j], rows), rows)
                 re, im = left[first, :, k], left[first + 1, :, k]
-                here = pl.ds(rows * i, rows)
                 lre[j, here, :rows] = -re
                 lre[j, here, rows:] = im
                 lim[j, here, :rows] = -im
                 lim[j, here, rows:] = -re
-        copies = []
-        for i in range(4):
-            here = pl.ds(rows * i, rows)
             for t in range(2):
                 cols = pl.ds(WIDTH * t, WIDTH)
                 for q, lhs in ((0, lre), (1, lim)):

time: 78.6 us -> 78.6 us (level)
  no operation moved by 1% of the time
where the time goes in v6:
time: 78.6 us; the launch traced here: 77.4 us
  starting transfers between devices  42.8 us (54%)
  waiting for transfers between devices  26.2 us (33%)
  Pallas kernels  5.84 us (7%)
  local copies, waits for them, and re-layouts  1.68 us (2%)
    ppermute x18, starting transfers between devices, send(): return lax.ppermute(value, AXES, moves(rule))  42.8 us
    ppermute x18, waiting for transfers between devices, send(): return lax.ppermute(value, AXES, moves(rule))  26.2 us
    pallas_call x1, Pallas kernels, product(): pl.pallas_call(product_kernel, out_shape=jax.ShapeDtypeStruct(shape, jnp....  4.45 us
    unnamed x2, local copies, waits for them, and re-layouts  1.59 us
  transfers between devices with their start and end apart: 18, of which 8 were waited for; matrix products, arithmetic and copies ran while one was open for 0% of the time, Pallas kernels for 1%

profile of v6, /device:TPU:1, one launch (start us, length us, event | category | flops | bytes accessed | tf_op | source)
XLA Modules:
  0.0 77.4 jit_solution(12139386170434137622)
XLA Ops:
  0.1 1.6 %copy-done = bf16[2,512,1024]{2,1,0:T(8,128)(2,1)S(1)} copy-done((bf16[2,512,1024]{2,1,0:T(8,128)(2,1)S(1)}, bf16[2,512,1024]{2,1,0:T(8,128)(2,1)}, u32[]{:S(2)}) %copy-start) | copy-done | bytes 2097176
  3.7 3.4 %collective-permute-start = (bf16[2,128,512]{2,1,0:T(8,128)(2,1)S(1)}, bf16[2,128,512]{2,1,0:T(8,128)(2,1)S(1)}, u32[]{:S(2)}, u32[]{:S(2)}) collective-permute-start(bf16[2,128,512]{2,1,0:T(8,128)(2,1)S(1)} %get-tuple-element.23), channel_id=1, source_target_pairs={{0,128},{1,129},{2,130},{3,131},{4,132},{5,133},{6,134},{7,135},{8... | collective-permute-start | bytes 786440 | tf_op jit(solution)/shard_map/ppermute | solution.py:34
  7.1 2.1 %collective-permute-start.1 = (bf16[2,128,512]{2,1,0:T(8,128)(2,1)S(1)}, bf16[2,128,512]{2,1,0:T(8,128)(2,1)S(1)}, u32[]{:S(2)}, u32[]{:S(2)}) collective-permute-start(bf16[2,128,512]{2,1,0:T(8,128)(2,1)S(1)} %get-tuple-element.24), channel_id=1, source_target_pairs={{0,384},{1,385},{2,386},{3,387},{4,388},{5,389},{6,390},{7,391},{8... | collective-permute-start | bytes 786440 | tf_op jit(solution)/shard_map/ppermute | solution.py:34
  9.2 1.3 %collective-permute-start.2 = (bf16[2,128,512]{2,1,0:T(8,128)(2,1)S(1)}, bf16[2,128,512]{2,1,0:T(8,128)(2,1)S(1)}, u32[]{:S(2)}, u32[]{:S(2)}) collective-permute-start(bf16[2,128,512]{2,1,0:T(8,128)(2,1)S(1)} %get-tuple-element.25), channel_id=1, source_target_pairs={{0,256},{1,257},{2,258},{3,259},{4,260},{5,261},{6,262},{7,263},{8... | collective-permute-start | bytes 786440 | tf_op jit(solution)/shard_map/ppermute | solution.py:34
  10.5 2.4 %collective-permute-done.3.came = bf16[2,512,512]{2,1,0:T(8,128)(2,1)S(1)} collective-permute-done((bf16[2,512,512]{2,1,0:T(8,128)(2,1)S(1)}, bf16[2,512,512]{2,1,0:T(8,128)(2,1)S(1)}, u32[]{:S(2)}, u32[]{:S(2)}) %collective-permute-start.3) | collective-permute-done | bytes 1048608 | tf_op jit(solution)/shard_map/ppermute | solution.py:34
  13.6 1.3 %collective-permute-start.4 = (bf16[2,128,512]{2,1,0:T(8,128)(2,1)S(1)}, bf16[2,128,512]{2,1,0:T(8,128)(2,1)S(1)}, u32[]{:S(2)}, u32[]{:S(2)}) collective-permute-start(bf16[2,128,512]{2,1,0:T(8,128)(2,1)S(1)} %get-tuple-element.32), channel_id=1, source_target_pairs={{0,128},{1,129},{2,130},{3,131},{4,132},{5,133},{6,134},{7,135},{8... | collective-permute-start | bytes 786440 | tf_op jit(solution)/shard_map/ppermute | solution.py:34
  14.9 1.3 %collective-permute-start.5 = (bf16[2,128,512]{2,1,0:T(8,128)(2,1)S(1)}, bf16[2,128,512]{2,1,0:T(8,128)(2,1)S(1)}, u32[]{:S(2)}, u32[]{:S(2)}) collective-permute-start(bf16[2,128,512]{2,1,0:T(8,128)(2,1)S(1)} %get-tuple-element.33), channel_id=1, source_target_pairs={{0,384},{1,385},{2,386},{3,387},{4,388},{5,389},{6,390},{7,391},{8... | collective-permute-start | bytes 786440 | tf_op jit(solution)/shard_map/ppermute | solution.py:34
  16.2 1.3 %collective-permute-start.6 = (bf16[2,128,512]{2,1,0:T(8,128)(2,1)S(1)}, bf16[2,128,512]{2,1,0:T(8,128)(2,1)S(1)}, u32[]{:S(2)}, u32[]{:S(2)}) collective-permute-start(bf16[2,128,512]{2,1,0:T(8,128)(2,1)S(1)} %get-tuple-element.34), channel_id=1, source_target_pairs={{0,256},{1,257},{2,258},{3,259},{4,260},{5,261},{6,262},{7,263},{8... | collective-permute-start | bytes 786440 | tf_op jit(solution)/shard_map/ppermute | solution.py:34
  17.6 1.3 %collective-permute-start.7 = (bf16[2,128,512]{2,1,0:T(8,128)(2,1)S(1)}, bf16[2,128,512]{2,1,0:T(8,128)(2,1)S(1)}, u32[]{:S(2)}, u32[]{:S(2)}) collective-permute-start(bf16[2,128,512]{2,1,0:T(8,128)(2,1)S(1)} %add_select_fusion.1), channel_id=1, source_target_pairs={{0,64},{1,65},{2,66},{3,67},{4,68},{5,69},{6,70},{7,71},{8,72},{9,... | collective-permute-start | bytes 786440 | tf_op jit(solution)/shard_map/ppermute | solution.py:34
  19.5 1.5 %collective-permute-done.6 = bf16[2,128,512]{2,1,0:T(8,128)(2,1)S(1)} collective-permute-done((bf16[2,128,512]{2,1,0:T(8,128)(2,1)S(1)}, bf16[2,128,512]{2,1,0:T(8,128)(2,1)S(1)}, u32[]{:S(2)}, u32[]{:S(2)}) %collective-permute-start.6) | collective-permute-done | bytes 262176 | tf_op jit(solution)/shard_map/ppermute | solution.py:34
  23.1 11.0 %collective-permute-done.8 = bf16[2,128,512]{2,1,0:T(8,128)(2,1)S(1)} collective-permute-done((bf16[2,128,512]{2,1,0:T(8,128)(2,1)S(1)}, bf16[2,128,512]{2,1,0:T(8,128)(2,1)S(1)}, u32[]{:S(2)}, u32[]{:S(2)}) %collective-permute-start.8) | collective-permute-done | bytes 262176 | tf_op jit(solution)/shard_map/ppermute | solution.py:34
  34.1 1.3 %collective-permute-start.9 = (bf16[2,128,512]{2,1,0:T(8,128)(2,1)S(1)}, bf16[2,128,512]{2,1,0:T(8,128)(2,1)S(1)}, u32[]{:S(2)}, u32[]{:S(2)}) collective-permute-start(bf16[2,128,512]{2,1,0:T(8,128)(2,1)S(1)} %get-tuple-element.37), channel_id=1, source_target_pairs={{0,32},{1,33},{2,34},{3,35},{4,36},{5,37},{6,38},{7,39},{8,40},{9,... | collective-permute-start | bytes 786440 | tf_op jit(solution)/shard_map/ppermute | solution.py:34
  35.4 7.3 %collective-permute-start.10 = (bf16[2,128,512]{2,1,0:T(8,128)(2,1)S(1)}, bf16[2,128,512]{2,1,0:T(8,128)(2,1)S(1)}, u32[]{:S(2)}, u32[]{:S(2)}) collective-permute-start(bf16[2,128,512]{2,1,0:T(8,128)(2,1)S(1)} %get-tuple-element.38), channel_id=1, source_target_pairs={{0,32},{1,33},{2,34},{3,35},{4,36},{5,37},{6,38},{7,39},{8,40},{9,... | collective-permute-start | bytes 786440 | tf_op jit(solution)/shard_map/ppermute | solution.py:34
  42.8 7.2 %collective-permute-done.10 = bf16[2,128,512]{2,1,0:T(8,128)(2,1)S(1)} collective-permute-done((bf16[2,128,512]{2,1,0:T(8,128)(2,1)S(1)}, bf16[2,128,512]{2,1,0:T(8,128)(2,1)S(1)}, u32[]{:S(2)}, u32[]{:S(2)}) %collective-permute-start.10) | collective-permute-done | bytes 262176 | tf_op jit(solution)/shard_map/ppermute | solution.py:34
  50.1 5.7 %collective-permute-start.13 = (bf16[4,128,512]{2,1,0:T(8,128)(2,1)S(1)}, bf16[4,128,512]{2,1,0:T(8,128)(2,1)S(1)}, u32[]{:S(2)}, u32[]{:S(2)}) collective-permute-start(bf16[4,128,512]{2,1,0:T(8,128)(2,1)S(1)} %pad_maximum_fusion.refs_0_), channel_id=1, source_target_pairs={{0,256},{1,257},{2,258},{3,259},{4,260},{5,261},{6,262},{7,263},{8... | collective-permute-start | bytes 1572872 | tf_op jit(solution)/shard_map/ppermute | solution.py:34
  55.8 1.9 %collective-permute-start.12 = (bf16[4,128,512]{2,1,0:T(8,128)(2,1)S(1)}, bf16[4,128,512]{2,1,0:T(8,128)(2,1)S(1)}, u32[]{:S(2)}, u32[]{:S(2)}) collective-permute-start(bf16[4,128,512]{2,1,0:T(8,128)(2,1)S(1)} %pad_maximum_fusion.refs_0_), channel_id=1, source_target_pairs={{0,384},{1,385},{2,386},{3,387},{4,388},{5,389},{6,390},{7,391},{8... | collective-permute-start | bytes 1572872 | tf_op jit(solution)/shard_map/ppermute | solution.py:34
  57.7 3.4 %collective-permute-start.11 = (bf16[4,128,512]{2,1,0:T(8,128)(2,1)S(1)}, bf16[4,128,512]{2,1,0:T(8,128)(2,1)S(1)}, u32[]{:S(2)}, u32[]{:S(2)}) collective-permute-start(bf16[4,128,512]{2,1,0:T(8,128)(2,1)S(1)} %pad_maximum_fusion.refs_0_), channel_id=1, source_target_pairs={{0,128},{1,129},{2,130},{3,131},{4,132},{5,133},{6,134},{7,135},{8... | collective-permute-start | bytes 1572872 | tf_op jit(solution)/shard_map/ppermute | solution.py:34
  61.1 1.9 %collective-permute-start.14 = (bf16[4,128,512]{2,1,0:T(8,128)(2,1)S(1)}, bf16[4,128,512]{2,1,0:T(8,128)(2,1)S(1)}, u32[]{:S(2)}, u32[]{:S(2)}) collective-permute-start(bf16[4,128,512]{2,1,0:T(8,128)(2,1)S(1)} %pad_maximum_fusion.refs_0_), channel_id=1, source_target_pairs={{0,16},{1,17},{2,18},{3,19},{4,20},{5,21},{6,22},{7,23},{8,24},{9,... | collective-permute-start | bytes 1572872 | tf_op jit(solution)/shard_map/ppermute | solution.py:34
  63.0 2.4 %collective-permute-start.17 = (bf16[4,128,512]{2,1,0:T(8,128)(2,1)S(1)}, bf16[4,128,512]{2,1,0:T(8,128)(2,1)S(1)}, u32[]{:S(2)}, u32[]{:S(2)}) collective-permute-start(bf16[4,128,512]{2,1,0:T(8,128)(2,1)S(1)} %collective-permute-done.13.refs_3_), channel_id=1, source_target_pairs={{0,16},{1,17},{2,18},{3,19},{4,20},{5,21},{6,22},{7,23},{8,24},{9,... | collective-permute-start | bytes 1572872 | tf_op jit(solution)/shard_map/ppermute | solution.py:34
  65.4 1.5 %collective-permute-done.12.refs_2_ = bf16[4,128,512]{2,1,0:T(8,128)(2,1)S(1)} collective-permute-done((bf16[4,128,512]{2,1,0:T(8,128)(2,1)S(1)}, bf16[4,128,512]{2,1,0:T(8,128)(2,1)S(1)}, u32[]{:S(2)}, u32[]{:S(2)}) %collective-permute-start.12) | collective-permute-done | bytes 524320 | tf_op jit(solution)/shard_map/ppermute | solution.py:34
  66.9 1.9 %collective-permute-start.16 = (bf16[4,128,512]{2,1,0:T(8,128)(2,1)S(1)}, bf16[4,128,512]{2,1,0:T(8,128)(2,1)}, u32[]{:S(2)}, u32[]{:S(2)}) collective-permute-start(bf16[4,128,512]{2,1,0:T(8,128)(2,1)S(1)} %collective-permute-done.12.refs_2_), channel_id=1, source_target_pairs={{0,16},{1,17},{2,18},{3,19},{4,20},{5,21},{6,22},{7,23},{8,24},{9,... | collective-permute-start | bytes 1572872 | tf_op jit(solution)/shard_map/ppermute | solution.py:34
  68.8 2.4 %collective-permute-start.15 = (bf16[4,128,512]{2,1,0:T(8,128)(2,1)S(1)}, bf16[4,128,512]{2,1,0:T(8,128)(2,1)}, u32[]{:S(2)}, u32[]{:S(2)}) collective-permute-start(bf16[4,128,512]{2,1,0:T(8,128)(2,1)S(1)} %collective-permute-done.11.refs_1_), channel_id=1, source_target_pairs={{0,16},{1,17},{2,18},{3,19},{4,20},{5,21},{6,22},{7,23},{8,24},{9,... | collective-permute-start | bytes 1572872 | tf_op jit(solution)/shard_map/ppermute | solution.py:34
  71.5 1.4 %collective-permute-done.15.refs_5_ = bf16[4,128,512]{2,1,0:T(8,128)(2,1)} collective-permute-done((bf16[4,128,512]{2,1,0:T(8,128)(2,1)S(1)}, bf16[4,128,512]{2,1,0:T(8,128)(2,1)}, u32[]{:S(2)}, u32[]{:S(2)}) %collective-permute-start.15) | collective-permute-done | bytes 524320 | tf_op jit(solution)/shard_map/ppermute | solution.py:34
  72.9 4.5 %shard_map.19 = bf16[2,512,1024]{2,1,0:T(8,128)(2,1)} custom-call(s32[9]{0:T(128)S(1)} %stack.51.at, bf16[4,128,512]{2,1,0:T(8,128)(2,1)S(1)} %pad_maximum_fusion.refs_0_, bf16[4,128,512]{2,1,0:T(8,128)(2,1)S(1)} %collective-permute-done.11.refs_1_, bf16[4,128,512]{2,1,0:T(8,128)(2,1)S(1)} %collective-permute-done.12.refs_2_, ...), custom_call_target="tpu_custom_call" | custom-call | flops 2147483648 | bytes 4194304 | tf_op jit(solution)/shard_map/pallas_call | solution.py:153
  (24 shorter events, 5.7 us)
Async XLA Ops:
  0.1 1.6 %copy-start = (bf16[2,512,1024]{2,1,0:T(8,128)(2,1)S(1)}, bf16[2,512,1024]{2,1,0:T(8,128)(2,1)}, u32[]{:S(2)}) copy-start(bf16[2,512,1024]{2,1,0:T(8,128)(2,1)} %field.1) | copy-start | bytes 6291460
  2.4 10.5 %collective-permute-start.3 = (bf16[2,512,512]{2,1,0:T(8,128)(2,1)S(1)}, bf16[2,512,512]{2,1,0:T(8,128)(2,1)S(1)}, u32[]{:S(2)}, u32[]{:S(2)}) collective-permute-start(bf16[2,512,512]{2,1,0:T(8,128)(2,1)S(1)} %get-tuple-element.26), channel_id=1, source_target_pairs={{0,16},{32,48},{64,80},{96,112},{128,144},{160,176},{192,208},{224... | collective-permute-start | bytes 3145736 | tf_op jit(solution)/shard_map/ppermute | solution.py:34
  3.7 12.5 %collective-permute-start = (bf16[2,128,512]{2,1,0:T(8,128)(2,1)S(1)}, bf16[2,128,512]{2,1,0:T(8,128)(2,1)S(1)}, u32[]{:S(2)}, u32[]{:S(2)}) collective-permute-start(bf16[2,128,512]{2,1,0:T(8,128)(2,1)S(1)} %get-tuple-element.23), channel_id=1, source_target_pairs={{0,128},{1,129},{2,130},{3,131},{4,132},{5,133},{6,134},{7,135},{8... | collective-permute-start | bytes 786440 | tf_op jit(solution)/shard_map/ppermute | solution.py:34
  7.1 10.4 %collective-permute-start.1 = (bf16[2,128,512]{2,1,0:T(8,128)(2,1)S(1)}, bf16[2,128,512]{2,1,0:T(8,128)(2,1)S(1)}, u32[]{:S(2)}, u32[]{:S(2)}) collective-permute-start(bf16[2,128,512]{2,1,0:T(8,128)(2,1)S(1)} %get-tuple-element.24), channel_id=1, source_target_pairs={{0,384},{1,385},{2,386},{3,387},{4,388},{5,389},{6,390},{7,391},{8... | collective-permute-start | bytes 786440 | tf_op jit(solution)/shard_map/ppermute | solution.py:34
  9.2 8.3 %collective-permute-start.2 = (bf16[2,128,512]{2,1,0:T(8,128)(2,1)S(1)}, bf16[2,128,512]{2,1,0:T(8,128)(2,1)S(1)}, u32[]{:S(2)}, u32[]{:S(2)}) collective-permute-start(bf16[2,128,512]{2,1,0:T(8,128)(2,1)S(1)} %get-tuple-element.25), channel_id=1, source_target_pairs={{0,256},{1,257},{2,258},{3,259},{4,260},{5,261},{6,262},{7,263},{8... | collective-permute-start | bytes 786440 | tf_op jit(solution)/shard_map/ppermute | solution.py:34
  13.6 5.4 %collective-permute-start.4 = (bf16[2,128,512]{2,1,0:T(8,128)(2,1)S(1)}, bf16[2,128,512]{2,1,0:T(8,128)(2,1)S(1)}, u32[]{:S(2)}, u32[]{:S(2)}) collective-permute-start(bf16[2,128,512]{2,1,0:T(8,128)(2,1)S(1)} %get-tuple-element.32), channel_id=1, source_target_pairs={{0,128},{1,129},{2,130},{3,131},{4,132},{5,133},{6,134},{7,135},{8... | collective-permute-start | bytes 786440 | tf_op jit(solution)/shard_map/ppermute | solution.py:34
  14.9 4.6 %collective-permute-start.5 = (bf16[2,128,512]{2,1,0:T(8,128)(2,1)S(1)}, bf16[2,128,512]{2,1,0:T(8,128)(2,1)S(1)}, u32[]{:S(2)}, u32[]{:S(2)}) collective-permute-start(bf16[2,128,512]{2,1,0:T(8,128)(2,1)S(1)} %get-tuple-element.33), channel_id=1, source_target_pairs={{0,384},{1,385},{2,386},{3,387},{4,388},{5,389},{6,390},{7,391},{8... | collective-permute-start | bytes 786440 | tf_op jit(solution)/shard_map/ppermute | solution.py:34
  16.2 4.8 %collective-permute-start.6 = (bf16[2,128,512]{2,1,0:T(8,128)(2,1)S(1)}, bf16[2,128,512]{2,1,0:T(8,128)(2,1)S(1)}, u32[]{:S(2)}, u32[]{:S(2)}) collective-permute-start(bf16[2,128,512]{2,1,0:T(8,128)(2,1)S(1)} %get-tuple-element.34), channel_id=1, source_target_pairs={{0,256},{1,257},{2,258},{3,259},{4,260},{5,261},{6,262},{7,263},{8... | collective-permute-start | bytes 786440 | tf_op jit(solution)/shard_map/ppermute | solution.py:34
  17.6 5.5 %collective-permute-start.7 = (bf16[2,128,512]{2,1,0:T(8,128)(2,1)S(1)}, bf16[2,128,512]{2,1,0:T(8,128)(2,1)S(1)}, u32[]{:S(2)}, u32[]{:S(2)}) collective-permute-start(bf16[2,128,512]{2,1,0:T(8,128)(2,1)S(1)} %add_select_fusion.1), channel_id=1, source_target_pairs={{0,64},{1,65},{2,66},{3,67},{4,68},{5,69},{6,70},{7,71},{8,72},{9,... | collective-permute-start | bytes 786440 | tf_op jit(solution)/shard_map/ppermute | solution.py:34
  21.1 13.0 %collective-permute-start.8 = (bf16[2,128,512]{2,1,0:T(8,128)(2,1)S(1)}, bf16[2,128,512]{2,1,0:T(8,128)(2,1)S(1)}, u32[]{:S(2)}, u32[]{:S(2)}) collective-permute-start(bf16[2,128,512]{2,1,0:T(8,128)(2,1)S(1)} %add_select_fusion), channel_id=1, source_target_pairs={{0,64},{1,65},{2,66},{3,67},{4,68},{5,69},{6,70},{7,71},{8,72},{9,... | collective-permute-start | bytes 786440 | tf_op jit(solution)/shard_map/ppermute | solution.py:34
  34.1 8.6 %collective-permute-start.9 = (bf16[2,128,512]{2,1,0:T(8,128)(2,1)S(1)}, bf16[2,128,512]{2,1,0:T(8,128)(2,1)S(1)}, u32[]{:S(2)}, u32[]{:S(2)}) collective-permute-start(bf16[2,128,512]{2,1,0:T(8,128)(2,1)S(1)} %get-tuple-element.37), channel_id=1, source_target_pairs={{0,32},{1,33},{2,34},{3,35},{4,36},{5,37},{6,38},{7,39},{8,40},{9,... | collective-permute-start | bytes 786440 | tf_op jit(solution)/shard_map/ppermute | solution.py:34
  35.4 14.5 %collective-permute-start.10 = (bf16[2,128,512]{2,1,0:T(8,128)(2,1)S(1)}, bf16[2,128,512]{2,1,0:T(8,128)(2,1)S(1)}, u32[]{:S(2)}, u32[]{:S(2)}) collective-permute-start(bf16[2,128,512]{2,1,0:T(8,128)(2,1)S(1)} %get-tuple-element.38), channel_id=1, source_target_pairs={{0,32},{1,33},{2,34},{3,35},{4,36},{5,37},{6,38},{7,39},{8,40},{9,... | collective-permute-start | bytes 786440 | tf_op jit(solution)/shard_map/ppermute | solution.py:34
  50.1 12.9 %collective-permute-start.13 = (bf16[4,128,512]{2,1,0:T(8,128)(2,1)S(1)}, bf16[4,128,512]{2,1,0:T(8,128)(2,1)S(1)}, u32[]{:S(2)}, u32[]{:S(2)}) collective-permute-start(bf16[4,128,512]{2,1,0:T(8,128)(2,1)S(1)} %pad_maximum_fusion.refs_0_), channel_id=1, source_target_pairs={{0,256},{1,257},{2,258},{3,259},{4,260},{5,261},{6,262},{7,263},{8... | collective-permute-start | bytes 1572872 | tf_op jit(solution)/shard_map/ppermute | solution.py:34
  55.8 11.2 %collective-permute-start.12 = (bf16[4,128,512]{2,1,0:T(8,128)(2,1)S(1)}, bf16[4,128,512]{2,1,0:T(8,128)(2,1)S(1)}, u32[]{:S(2)}, u32[]{:S(2)}) collective-permute-start(bf16[4,128,512]{2,1,0:T(8,128)(2,1)S(1)} %pad_maximum_fusion.refs_0_), channel_id=1, source_target_pairs={{0,384},{1,385},{2,386},{3,387},{4,388},{5,389},{6,390},{7,391},{8... | collective-permute-start | bytes 1572872 | tf_op jit(solution)/shard_map/ppermute | solution.py:34
  57.7 11.1 %collective-permute-start.11 = (bf16[4,128,512]{2,1,0:T(8,128)(2,1)S(1)}, bf16[4,128,512]{2,1,0:T(8,128)(2,1)S(1)}, u32[]{:S(2)}, u32[]{:S(2)}) collective-permute-start(bf16[4,128,512]{2,1,0:T(8,128)(2,1)S(1)} %pad_maximum_fusion.refs_0_), channel_id=1, source_target_pairs={{0,128},{1,129},{2,130},{3,131},{4,132},{5,133},{6,134},{7,135},{8... | collective-permute-start | bytes 1572872 | tf_op jit(solution)/shard_map/ppermute | solution.py:34
  61.1 10.4 %collective-permute-start.14 = (bf16[4,128,512]{2,1,0:T(8,128)(2,1)S(1)}, bf16[4,128,512]{2,1,0:T(8,128)(2,1)S(1)}, u32[]{:S(2)}, u32[]{:S(2)}) collective-permute-start(bf16[4,128,512]{2,1,0:T(8,128)(2,1)S(1)} %pad_maximum_fusion.refs_0_), channel_id=1, source_target_pairs={{0,16},{1,17},{2,18},{3,19},{4,20},{5,21},{6,22},{7,23},{8,24},{9,... | collective-permute-start | bytes 1572872 | tf_op jit(solution)/shard_map/ppermute | solution.py:34
  63.0 8.5 %collective-permute-start.17 = (bf16[4,128,512]{2,1,0:T(8,128)(2,1)S(1)}, bf16[4,128,512]{2,1,0:T(8,128)(2,1)S(1)}, u32[]{:S(2)}, u32[]{:S(2)}) collective-permute-start(bf16[4,128,512]{2,1,0:T(8,128)(2,1)S(1)} %collective-permute-done.13.refs_3_), channel_id=1, source_target_pairs={{0,16},{1,17},{2,18},{3,19},{4,20},{5,21},{6,22},{7,23},{8,24},{9,... | collective-permute-start | bytes 1572872 | tf_op jit(solution)/shard_map/ppermute | solution.py:34
  66.9 4.6 %collective-permute-start.16 = (bf16[4,128,512]{2,1,0:T(8,128)(2,1)S(1)}, bf16[4,128,512]{2,1,0:T(8,128)(2,1)}, u32[]{:S(2)}, u32[]{:S(2)}) collective-permute-start(bf16[4,128,512]{2,1,0:T(8,128)(2,1)S(1)} %collective-permute-done.12.refs_2_), channel_id=1, source_target_pairs={{0,16},{1,17},{2,18},{3,19},{4,20},{5,21},{6,22},{7,23},{8,24},{9,... | collective-permute-start | bytes 1572872 | tf_op jit(solution)/shard_map/ppermute | solution.py:34
  68.8 4.1 %collective-permute-start.15 = (bf16[4,128,512]{2,1,0:T(8,128)(2,1)S(1)}, bf16[4,128,512]{2,1,0:T(8,128)(2,1)}, u32[]{:S(2)}, u32[]{:S(2)}) collective-permute-start(bf16[4,128,512]{2,1,0:T(8,128)(2,1)S(1)} %collective-permute-done.11.refs_1_), channel_id=1, source_target_pairs={{0,16},{1,17},{2,18},{3,19},{4,20},{5,21},{6,22},{7,23},{8,24},{9,... | collective-permute-start | bytes 1572872 | tf_op jit(solution)/shard_map/ppermute | solution.py:34
